TPU v7x, 32 devices: a whole 2x2x4 slice. The times are simulated.
32 devices in a mesh: dp: 4 (over y, x), blk: 8 (over z, core).
Axes of the slice: x: 2, y: 2, z: 4, core: 2. Of those that a mesh axis runs over, the one named last changes fastest.
Arguments:
- tokens: bfloat16 [2, 8192, 768], P(None, ('dp', 'blk')), may hold values from -6 to 6
- cotangent: bfloat16 [2, 8192, 768], P(None, ('dp', 'blk')), may hold values from -6 to 6
- lengths: int32 [2, 4, 4], P(None, 'dp'), may hold values from 1 to 2045, as said below
- norm_gain: bfloat16 [768], replicated, may hold values from 0.099609375 to 1.8984375
- norm_bias: bfloat16 [768], replicated, may hold values from -3 to 3
- w_qkv: bfloat16 [768, 2304], replicated, may hold values from -0.3125 to 0.3125
- w_out: bfloat16 [768, 768], replicated, may hold values from -0.875 to 0.875
- w_up: bfloat16 [768, 3072], replicated, may hold values from -0.21875 to 0.21875
- w_down: bfloat16 [3072, 768], replicated, may hold values from -0.109375 to 0.109375
Outputs:
- output: bfloat16 [2, 8192, 768], P(None, ('dp', 'blk'))
- input_grad: float32 [2, 8192, 768], P(None, ('dp', 'blk'))
- grad_gain: float32 [768], replicated
- grad_bias: float32 [768], replicated
- grad_qkv: float32 [768, 2304], replicated
- grad_out: float32 [768, 768], replicated
- grad_up: float32 [768, 3072], replicated
- grad_down: float32 [3072, 768], replicated
Inputs may be any that keep to these rules, and one draw needn't show every extreme that they name: Each of the 2 x 4 rows holds 4 document lengths of 1 or more that sum to 2048.
All inputs are finite; a program needn't handle non-finite values.
Results may differ from a plain program's by a relative error of at most 0.012.
The roundings to bfloat16 on the way count: a program that leaves them out, or rounds other values in their place, can miss the bound.
Values may be sent and summed in bfloat16 or wider, within the bound.
No kernel may reach another device: no remote copies, remote signals or barrier semaphores. Data moves between devices by JAX's collectives and lax.ppermute only.
A program may use at most 320 MiB of HBM per device.

v0:
```python
from functools import partial

import jax
import jax.numpy as jnp
from jax import lax
from jax.sharding import PartitionSpec as P

HEAD = 64
ROT = 16


norm_eps = 1e-05
masked_score = -1e30


def contract_rows(operand, factor):
    return lax.dot_general(
        operand, factor, (((0,), (0,)), ((), ())), preferred_element_type=jnp.float32
    )


def contract_cols(operand, factor):
    return lax.dot_general(
        operand, factor, (((1,), (1,)), ((), ())), preferred_element_type=jnp.float32
    )


def doc_of(index_rows, doc_ends):
    return jnp.sum((index_rows[:, None] >= doc_ends[None, :]).astype(jnp.int32), axis=1)


def angles(positions, rot_dims):
    half_dims = rot_dims // 2
    frequency = 10000.0 ** (-2.0 * jnp.arange(half_dims, dtype=jnp.float32) / rot_dims)
    phases = positions.astype(jnp.float32)[:, None] * frequency[None, :]
    return (jnp.cos(phases)[:, None, :], jnp.sin(phases)[:, None, :])


def turn_field(rows_in, cos_rows, sin_rows, rot_dims):
    half_dims = rot_dims // 2
    first_half = rows_in[..., :half_dims]
    second = rows_in[..., half_dims:rot_dims]
    return jnp.concatenate(
        [
            first_half * cos_rows - second * sin_rows,
            second * cos_rows + first_half * sin_rows,
            rows_in[..., rot_dims:],
        ],
        axis=-1,
    )


def block_split(length):
    block_rows = min(512, length)
    return block_rows


def key_mask(key_first, key_count, query_index, query_docs, doc_ends):
    key_index = key_first + jnp.arange(key_count, dtype=jnp.int32)
    key_docs = doc_of(key_index, doc_ends)
    return (query_docs[:, None] == key_docs[None, :]) & (query_index[:, None] >= key_index[None, :])


def attend_step(fold_state, key_rows, value_rows, key_first, query_side):
    queries, query_index, query_docs, doc_ends = query_side
    allowed = key_mask(key_first, key_rows.shape[0], query_index, query_docs, doc_ends)
    score_scale = queries.shape[-1] ** (-0.5)
    running, totals, gathered = fold_state
    scores = (
        jnp.einsum("qhd,khd->hqk", queries, key_rows, preferred_element_type=jnp.float32)
        * score_scale
    )
    scores = jnp.where(allowed[None], scores, masked_score)
    highest = jnp.maximum(running, jnp.max(scores, axis=-1))
    weights = jnp.where(allowed[None], jnp.exp(scores - highest[..., None]), 0.0)
    rescale = jnp.exp(running - highest)
    totals = totals * rescale + jnp.sum(weights, axis=-1)
    gathered = gathered * rescale[..., None] + jnp.einsum(
        "hqk,khd->hqd", weights.astype(jnp.bfloat16), value_rows, preferred_element_type=jnp.float32
    )
    return (highest, totals, gathered)


def attend_piece(fold_state, pieces, query_side):
    key_rows, value_rows = pieces
    length = key_rows.shape[0]
    block_rows = block_split(length)
    blocks = length // block_rows

    def attend_advance(fold_state, scanned):
        number, key_block, value_block = scanned
        return (
            attend_step(fold_state, key_block, value_block, number * block_rows, query_side),
            None,
        )

    fold_state, ignored = lax.scan(
        attend_advance,
        fold_state,
        (
            jnp.arange(blocks, dtype=jnp.int32),
            key_rows.reshape((blocks, block_rows) + key_rows.shape[1:]),
            value_rows.reshape((blocks, block_rows) + value_rows.shape[1:]),
        ),
    )
    return fold_state


def grad_step(dq_acc, key_rows, value_rows, key_first, back_side):
    queries, query_index, query_docs, doc_ends, out_grad, log_totals, deltas = back_side
    allowed = key_mask(key_first, key_rows.shape[0], query_index, query_docs, doc_ends)
    score_scale = queries.shape[-1] ** (-0.5)
    compute_dq_acc = dq_acc
    scores = (
        jnp.einsum("qhd,khd->hqk", queries, key_rows, preferred_element_type=jnp.float32)
        * score_scale
    )
    attention = jnp.where(allowed[None], jnp.exp(scores - log_totals[..., None]), 0.0)
    prob_grad = jnp.einsum("qhd,khd->hqk", out_grad, value_rows, preferred_element_type=jnp.float32)
    score_grad = (attention * (prob_grad - deltas[..., None])).astype(jnp.bfloat16)
    compute_dq_acc = (
        compute_dq_acc
        + jnp.einsum("hqk,khd->qhd", score_grad, key_rows, preferred_element_type=jnp.float32)
        * score_scale
    )
    value_grad = jnp.einsum(
        "hqk,qhd->khd", attention.astype(jnp.bfloat16), out_grad, preferred_element_type=jnp.float32
    )
    key_grad = (
        jnp.einsum("hqk,qhd->khd", score_grad, queries, preferred_element_type=jnp.float32)
        * score_scale
    )
    return (compute_dq_acc, (key_grad, value_grad))


def grad_over(kv_pair, back_side, dq_init):
    key_all, value_all = kv_pair
    length = key_all.shape[0]
    block_rows = block_split(length)
    blocks = length // block_rows

    def grad_advance(dq_acc, scanned):
        number, key_block, value_block = scanned
        return grad_step(dq_acc, key_block, value_block, number * block_rows, back_side)

    dq_total, kv_grads = lax.scan(
        grad_advance,
        dq_init,
        (
            jnp.arange(blocks, dtype=jnp.int32),
            key_all.reshape((blocks, block_rows) + key_all.shape[1:]),
            value_all.reshape((blocks, block_rows) + value_all.shape[1:]),
        ),
    )
    return (dq_total, kv_grads[0].reshape(key_all.shape), kv_grads[1].reshape(value_all.shape))


def local(tokens, cotangent, lengths, norm_gain, norm_bias, w_qkv, w_out, w_up, w_down):
    micro_count, tok_rows, model_width = tokens.shape
    head_count = model_width // HEAD
    own_first = lax.axis_index("blk") * tok_rows
    query_index = own_first + jnp.arange(tok_rows, dtype=jnp.int32)
    norm_scale = norm_gain.astype(jnp.float32)
    norm_shift = norm_bias.astype(jnp.float32)
    grad_gain = jnp.zeros((model_width,), jnp.float32)
    grad_bias = jnp.zeros((model_width,), jnp.float32)
    grad_qkv = jnp.zeros(w_qkv.shape, jnp.float32)
    grad_out = jnp.zeros(w_out.shape, jnp.float32)
    grad_up = jnp.zeros(w_up.shape, jnp.float32)
    grad_down = jnp.zeros(w_down.shape, jnp.float32)
    outputs = []
    input_grads = []
    for micro_step in range(micro_count):
        x_rows = tokens[micro_step].astype(jnp.float32)
        doc_lengths = lengths[micro_step, 0]
        doc_ends = jnp.cumsum(doc_lengths, dtype=jnp.int32)
        doc_starts = doc_ends - doc_lengths
        query_docs = doc_of(query_index, doc_ends)
        picked = query_docs[:, None] == jnp.arange(doc_lengths.shape[0], dtype=jnp.int32)[None, :]
        positions = query_index - jnp.sum(jnp.where(picked, doc_starts[None, :], 0), axis=1)
        row_mean = jnp.mean(x_rows, axis=1, keepdims=True)
        centred = x_rows - row_mean
        inverse = lax.rsqrt(jnp.mean(centred * centred, axis=1, keepdims=True) + norm_eps)
        scaled = centred * inverse
        normed = (scaled * norm_scale + norm_shift).astype(jnp.bfloat16)
        projected = jnp.dot(normed, w_qkv, preferred_element_type=jnp.float32).reshape(
            tok_rows, 3, head_count, HEAD
        )
        cos_rows, sin_rows = angles(positions, ROT)
        queries = turn_field(projected[:, 0], cos_rows, sin_rows, ROT).astype(jnp.bfloat16)
        key_own = turn_field(projected[:, 1], cos_rows, sin_rows, ROT).astype(jnp.bfloat16)
        value_own = projected[:, 2].astype(jnp.bfloat16)
        query_side = (queries, query_index, query_docs, doc_ends)
        init_state = (
            jnp.full((head_count, tok_rows), masked_score, jnp.float32),
            jnp.zeros((head_count, tok_rows), jnp.float32),
            jnp.zeros((head_count, tok_rows, HEAD), jnp.float32),
        )
        running, totals, gathered = attend_piece(
            init_state,
            (
                lax.all_gather(key_own, "blk", axis=0, tiled=True),
                lax.all_gather(value_own, "blk", axis=0, tiled=True),
            ),
            query_side,
        )
        attended = gathered / totals[..., None]
        log_totals = running + jnp.log(totals)
        attended_rows = (
            attended.transpose(1, 0, 2).reshape(tok_rows, model_width).astype(jnp.bfloat16)
        )
        hidden = jnp.dot(normed, w_up, preferred_element_type=jnp.float32)
        active, gelu_back = jax.vjp(partial(jax.nn.gelu, approximate=False), hidden)
        active_low = active.astype(jnp.bfloat16)
        summed_out = (
            x_rows
            + jnp.dot(attended_rows, w_out, preferred_element_type=jnp.float32)
            + jnp.dot(active_low, w_down, preferred_element_type=jnp.float32)
        )
        outputs.append(summed_out.astype(jnp.bfloat16))
        out_cot = cotangent[micro_step]
        grad_down = grad_down + contract_rows(active_low, out_cot)
        grad_out = grad_out + contract_rows(attended_rows, out_cot)
        hidden_grad = gelu_back(contract_cols(out_cot, w_down))[0].astype(jnp.bfloat16)
        grad_up = grad_up + contract_rows(normed, hidden_grad)
        normed_grad = contract_cols(hidden_grad, w_up)
        attn_grad = (
            contract_cols(out_cot, w_out).astype(jnp.bfloat16).reshape(tok_rows, head_count, HEAD)
        )
        deltas = jnp.einsum("qhd,hqd->hq", attn_grad.astype(jnp.float32), attended)
        back_side = (queries, query_index, query_docs, doc_ends, attn_grad, log_totals, deltas)
        kv_whole = (
            lax.all_gather(key_own, "blk", axis=0, tiled=True),
            lax.all_gather(value_own, "blk", axis=0, tiled=True),
        )
        dq_init = jnp.zeros((tok_rows, head_count, HEAD), jnp.float32)
        query_grad, key_grads, value_grads = grad_over(kv_whole, back_side, dq_init)
        key_grad, value_grad = (
            lax.psum_scatter(
                key_grads.astype(jnp.bfloat16), "blk", scatter_dimension=0, tiled=True
            ).astype(jnp.float32),
            lax.psum_scatter(
                value_grads.astype(jnp.bfloat16), "blk", scatter_dimension=0, tiled=True
            ).astype(jnp.float32),
        )
        query_back = turn_field(query_grad, cos_rows, -sin_rows, ROT)
        key_back = turn_field(key_grad, cos_rows, -sin_rows, ROT)
        joined_grad = (
            jnp.stack([query_back, key_back, value_grad], axis=1)
            .reshape(tok_rows, 3 * model_width)
            .astype(jnp.bfloat16)
        )
        grad_qkv = grad_qkv + contract_rows(normed, joined_grad)
        normed_grad = normed_grad + contract_cols(joined_grad, w_qkv)
        scaled_grad = normed_grad * norm_scale
        grad_gain = grad_gain + jnp.sum(normed_grad * scaled, axis=0)
        grad_bias = grad_bias + jnp.sum(normed_grad, axis=0)
        input_grad = out_cot.astype(jnp.float32) + inverse * (
            scaled_grad
            - jnp.mean(scaled_grad, axis=1, keepdims=True)
            - scaled * jnp.mean(scaled_grad * scaled, axis=1, keepdims=True)
        )
        input_grads.append(input_grad)
    norm_flat = jnp.stack([grad_gain, grad_bias]).reshape(-1)
    shares = (
        lax.psum_scatter(norm_flat, ("dp", "blk"), scatter_dimension=0, tiled=True),
        lax.psum_scatter(grad_qkv.reshape(-1), ("dp", "blk"), scatter_dimension=0, tiled=True),
        lax.psum_scatter(grad_out.reshape(-1), ("dp", "blk"), scatter_dimension=0, tiled=True),
        lax.psum_scatter(grad_up.reshape(-1), ("dp", "blk"), scatter_dimension=0, tiled=True),
        lax.psum_scatter(grad_down.reshape(-1), ("dp", "blk"), scatter_dimension=0, tiled=True),
    )
    gathered_grads = (
        lax.all_gather(shares[0].astype(jnp.bfloat16), ("dp", "blk"), axis=0, tiled=True).astype(
            jnp.float32
        ),
        lax.all_gather(shares[1].astype(jnp.bfloat16), ("dp", "blk"), axis=0, tiled=True).astype(
            jnp.float32
        ),
        lax.all_gather(shares[2].astype(jnp.bfloat16), ("dp", "blk"), axis=0, tiled=True).astype(
            jnp.float32
        ),
        lax.all_gather(shares[3].astype(jnp.bfloat16), ("dp", "blk"), axis=0, tiled=True).astype(
            jnp.float32
        ),
        lax.all_gather(shares[4].astype(jnp.bfloat16), ("dp", "blk"), axis=0, tiled=True).astype(
            jnp.float32
        ),
    )
    norm_pair = gathered_grads[0].reshape(2, model_width)
    return (
        jnp.stack(outputs),
        jnp.stack(input_grads),
        norm_pair[0],
        norm_pair[1],
        gathered_grads[1].reshape(w_qkv.shape),
        gathered_grads[2].reshape(w_out.shape),
        gathered_grads[3].reshape(w_up.shape),
        gathered_grads[4].reshape(w_down.shape),
    )


def solution(mesh):
    placed = (
        P(None, ("dp", "blk"), None),
        P(None, ("dp", "blk"), None),
        P(None, "dp", None),
        P(),
        P(),
        P(),
        P(),
        P(),
        P(),
    )
    return jax.shard_map(
        local,
        mesh=mesh,
        in_specs=placed,
        out_specs=(
            P(None, ("dp", "blk"), None),
            P(None, ("dp", "blk"), None),
            P(),
            P(),
            P(),
            P(),
            P(),
            P(),
        ),
        check_vma=False,
    )
```

profile of v0, /device:TPU:0, one launch (start us, length us, event | category | flops | bytes accessed | tf_op | source)
XLA Modules:
  0.0 1313.6 jit_solution(1264949167406635137)
XLA Ops:
  12.6 5.8 copy.95
  46.6 21.7 %all-gather.13.cloned.1.call-done = bf16[2048,12,64]{0,2,1:T(8,128)(2,1)} async-done(((bf16[256,12,64]{0,2,1:T(8,128)(2,1)}), bf16[2048,12,64]{0,2,1:T(8,128)(2,1)}) %all-gather.13.cloned.1.call-update) | async-done | bytes 3145744 | tf_op jit(solution)/shard_map/all_gather | solution.py:202
  72.4 35.6 %all-gather.25.cloned.1.call-done = bf16[2048,1,12,64]{0,3,2,1:T(8,128)(2,1)} async-done(((bf16[256,1,12,64]{0,3,2,1:T(8,128)(2,1)}), bf16[2048,1,12,64]{0,3,2,1:T(8,128)(2,1)}) %all-gather.25.cloned.1.call-update) | async-done | bytes 3145744 | tf_op jit(solution)/shard_map/all_gather | solution.py:203
  108.0 6.3 reshape.788
  118.7 28.3 %all-gather.11.cloned.1.call-done = bf16[2048,12,64]{0,2,1:T(8,128)(2,1)} async-done(((bf16[256,12,64]{0,2,1:T(8,128)(2,1)}), bf16[2048,12,64]{0,2,1:T(8,128)(2,1)}) %all-gather.11.cloned.1.call-update) | async-done | bytes 3145744 | tf_op jit(solution)/shard_map/all_gather | solution.py:202
  151.1 60.5 %while.61 = (s32[]{:T(128)}, f32[12,256]{1,0:T(8,128)S(1)}, f32[12,256]{1,0:T(8,128)S(1)}, f32[12,256,64]{1,2,0:T(8,128)}, s32[256]{0:T(256)S(1)}, /*index=5*/s3...) while((s32[]{:T(128)}, f32[12,256]{1,0:T(8,128)S(1)}, ...), condition=%wide.region_19.20_spmd.clone, body=%wide.region_15.19_spmd.clone.sunk | while | flops 424105216 | bytes 48313580 | solution.py:97
  211.6 6.1 reshape.784
  222.1 60.5 %while.60 = (s32[]{:T(128)}, f32[12,256]{1,0:T(8,128)S(1)}, f32[12,256]{1,0:T(8,128)S(1)}, f32[12,256,64]{1,2,0:T(8,128)}, s32[256]{0:T(256)S(1)}, /*index=5*/s3...) while((s32[]{:T(128)}, f32[12,256]{1,0:T(8,128)S(1)}, ...), condition=%wide.region_9.10_spmd.clone, body=%wide.region_5.9_spmd.clone.sunk | while | flops 424105216 | bytes 48313580 | solution.py:97
  288.8 66.9 %while.63 = (s32[]{:T(128)}, f32[256,12,64]{0,2,1:T(8,128)S(1)}, bf16[4,512,12,64]{1,3,2,0:T(8,128)(2,1)}, bf16[4,512,12,64]{1,3,2,0:T(8,128)(2,1)}, bf16[4,512,...) while((s32[]{:T(128)}, f32[256,12,64]{0,2,1:T(8,128)S(1)}, ...), condition=%wide.region_29.30_spmd.clone, body=%wide.region_27.29_spmd.clone.sunk | while | flops 1023744256 | bytes 103466368 | solution.py:146
  292.8 5.4 fusion.333
  309.5 5.4 fusion.333
  326.2 5.4 fusion.333
  342.9 5.4 fusion.333
  366.2 66.4 %while.62 = (s32[]{:T(128)}, f32[256,12,64]{0,2,1:T(8,128)S(1)}, bf16[4,512,12,64]{1,3,2,0:T(8,128)(2,1)}, bf16[4,512,12,64]{1,3,2,0:T(8,128)(2,1)}, bf16[4,512,...) while((s32[]{:T(128)}, f32[256,12,64]{0,2,1:T(8,128)S(1)}, ...), condition=%wide.region_22.23_spmd.clone, body=%wide.region_20.22_spmd.clone.sunk | while | flops 1023744256 | bytes 100320576 | solution.py:146
  370.1 5.4 fusion.320
  386.7 5.4 fusion.320
  441.9 10.9 multiply_convert_fusion.1
  452.9 5.6 add_convert_fusion.1
  458.5 11.6 multiply_convert_fusion
  483.1 5.9 copy.142
  495.7 11.0 reshape.801
  539.6 19.2 %reduce-scatter.11.cloned.1.call-done = bf16[256,12,64]{0,2,1:T(8,128)(2,1)} async-done(((bf16[2048,12,64]{0,2,1:T(8,128)(2,1)}), bf16[256,12,64]{0,2,1:T(8,128)(2,1)}) %reduce-scatter.11.cloned.1.call-update) | async-done | bytes 393232 | tf_op jit(solution)/shard_map/reduce_scatter | solution.py:242
  568.4 7.7 convolution_add_fusion
  576.1 7.9 reshape.792
  584.0 463.5 %all-reduce.8 = (bf16[1536]{0:T(1024)(128)(2,1)}, bf16[1769472]{0:T(1024)(128)(2,1)}, bf16[589824]{0:T(1024)(128)(2,1)}, bf16[2359296]{0:T(1024)(128)(2,1)}, bf16[2359296]{0:T(1024)(128)(2,1)}) all-reduce(f32[1536]{0:T(1024)} %reshape.791, f32[1769472]{0:T(1024)} %reshape.792, ...), channel_id=8, replica_groups=mesh['dp'=4,'blk'=8] {'dp','blk'}, use_global_device_ids=true, to_apply=%region_38.39.clone | all-reduce | flops 7079424 | bytes 42476544
  1065.0 38.1 %all-reduce = bf16[1536]{0:T(1024)(128)(2,1)S(1)} all-reduce(bf16[1536]{0:T(1024)(128)(2,1)S(1)} %dynamic-update-slice), channel_id=1, replica_groups=mesh['dp'=4,'blk'=8] {'dp','blk'}, use_global_device_ids=true, to_apply=%add | all-reduce | flops 1536 | bytes 6144
  1112.9 51.9 %all-gather.15.cloned.1.call-done = bf16[1769472]{0:T(1024)(128)(2,1)} async-done(((bf16[55296]{0:T(1024)(128)(2,1)}), bf16[1769472]{0:T(1024)(128)(2,1)}) %all-gather.15.cloned.1.call-update) | async-done | bytes 3538960 | tf_op jit(solution)/shard_map/all_gather | solution.py:276
  1164.8 7.9 reshape.807
  1172.7 58.2 %all-gather.19.cloned.1.call-done = bf16[2359296]{0:T(1024)(128)(2,1)} async-done(((bf16[73728]{0:T(1024)(128)(2,1)}), bf16[2359296]{0:T(1024)(128)(2,1)}) %all-gather.19.cloned.1.call-update) | async-done | bytes 4718608 | tf_op jit(solution)/shard_map/all_gather | solution.py:282
  1230.9 8.7 reshape.811
  1239.7 56.6 %all-gather.21.cloned.1.call-done = bf16[2359296]{0:T(1024)(128)(2,1)} async-done(((bf16[73728]{0:T(1024)(128)(2,1)}), bf16[2359296]{0:T(1024)(128)(2,1)}) %all-gather.21.cloned.1.call-update) | async-done | bytes 4718608 | tf_op jit(solution)/shard_map/all_gather | solution.py:285
  1296.3 10.0 reshape.813
  (529 shorter events, 375.3 us)
Async XLA Ops:
  7.2 31.0 %copy-start = (bf16[768,768]{1,0:T(8,128)(2,1)S(1)}, bf16[768,768]{1,0:T(8,128)(2,1)}, u32[]{:S(2)}) copy-start(bf16[768,768]{1,0:T(8,128)(2,1)} %param.23) | copy-start | bytes 3538948
  7.2 61.2 %all-gather.13.cloned.1.call-start = ((), (), s32[]{:S(2)}) async-start(), calls=%async_computation.5 | async-start | bytes 3538944 | tf_op jit(solution)/shard_map/all_gather | solution.py:202
  8.6 9.8 copy-start.65
  8.6 19.7 %copy-start.59 = (f32[256]{0:T(256)}, f32[256]{0:T(256)S(1)}, u32[]{:S(2)}) copy-start(f32[256]{0:T(256)S(1)} %get-tuple-element.846) | copy-start | bytes 3076
  10.2 8.3 copy-start.70
  10.8 17.5 %copy-start.40 = (f32[768]{0:T(1024)}, f32[768]{0:T(1024)S(1)}, u32[]{:S(2)}) copy-start(f32[768]{0:T(1024)S(1)} %convert_element_type.240) | copy-start | bytes 9220
  11.5 16.9 %copy-start.36 = (f32[768]{0:T(1024)}, f32[768]{0:T(1024)S(1)}, u32[]{:S(2)}) copy-start(f32[768]{0:T(1024)S(1)} %convert_element_type.239) | copy-start | bytes 9220
  12.4 11.4 copy-start.55
  12.6 11.2 copy-start.57
  24.8 9.0 copy-start.52
  26.3 81.7 %all-gather.25.cloned.1.call-start = ((), (), s32[]{:S(2)}) async-start(), calls=%async_computation.15 | async-start | bytes 3538944 | tf_op jit(solution)/shard_map/all_gather | solution.py:203
  28.3 118.7 %all-gather.11.cloned.1.call-start = ((), (), s32[]{:S(2)}) async-start(), calls=%async_computation.4 | async-start | bytes 3538944 | tf_op jit(solution)/shard_map/all_gather | solution.py:202
  35.3 176.2 %all-gather.23.cloned.1.call-start = ((), (), s32[]{:S(2)}) async-start(), calls=%async_computation.14 | async-start | bytes 3538944 | tf_op jit(solution)/shard_map/all_gather | solution.py:203
  37.4 486.6 %reduce-scatter.9.cloned.1.call-start = ((), (), s32[]{:S(2)}) async-start(), calls=%async_computation.8 | async-start | bytes 3538944 | tf_op jit(solution)/shard_map/reduce_scatter | solution.py:239
  291.0 7.1 copy-start.5
  324.5 7.1 copy-start.5
  341.2 7.1 copy-start.5
  360.1 167.5 %reduce-scatter.5.cloned.1.call-start = ((), (), s32[]{:S(2)}) async-start(), calls=%async_computation.6 | async-start | bytes 3538944 | tf_op jit(solution)/shard_map/reduce_scatter | solution.py:239
  368.3 7.1 copy-start.7
  385.0 7.1 copy-start.7
  436.7 96.6 %reduce-scatter.7.cloned.1.call-start = ((), (), s32[]{:S(2)}) async-start(), calls=%async_computation.7 | async-start | bytes 3538944 | tf_op jit(solution)/shard_map/reduce_scatter | solution.py:242
  440.8 118.1 %reduce-scatter.11.cloned.1.call-start = ((), (), s32[]{:S(2)}) async-start(), calls=%async_computation.9 | async-start | bytes 3538944 | tf_op jit(solution)/shard_map/reduce_scatter | solution.py:242
  441.9 10.9 copy-start.18
  458.5 11.6 copy-start.14
  472.3 637.3 %all-gather.17.cloned.1.call-start = ((), (), s32[]{:S(2)}) async-start(), calls=%async_computation.11 | async-start | bytes 1216512 | tf_op jit(solution)/shard_map/all_gather | solution.py:279
  523.9 7.7 copy-start.53
  584.0 469.9 %copy-start.22 = (bf16[256,3072]{1,0:T(8,128)(2,1)S(1)}, bf16[256,3072]{1,0:T(8,128)(2,1)}, u32[]{:S(2)}) copy-start(bf16[256,3072]{1,0:T(8,128)(2,1)} %get-tuple-element.787) | copy-start | bytes 4718596
  1049.0 115.9 %all-gather.15.cloned.1.call-start = ((), (), s32[]{:S(2)}) async-start(), calls=%async_computation.10 | async-start | bytes 3649536 | tf_op jit(solution)/shard_map/all_gather | solution.py:276
  1050.6 180.3 %all-gather.19.cloned.1.call-start = ((), (), s32[]{:S(2)}) async-start(), calls=%async_computation.12 | async-start | bytes 4866048 | tf_op jit(solution)/shard_map/all_gather | solution.py:282
  1052.2 244.0 %all-gather.21.cloned.1.call-start = ((), (), s32[]{:S(2)}) async-start(), calls=%async_computation.13 | async-start | bytes 4866048 | tf_op jit(solution)/shard_map/all_gather | solution.py:285
  1062.6 43.1 %copy-start.20 = (bf16[2,256,768]{2,1,0:T(8,128)(2,1)S(1)}, bf16[2,256,768]{2,1,0:T(8,128)(2,1)}, u32[]{:S(2)}) copy-start(bf16[2,256,768]{2,1,0:T(8,128)(2,1)} %param.18) | copy-start | bytes 2359300
  1062.6 43.1 %copy-start.69 = (f32[256]{0:T(256)S(1)}, f32[256]{0:T(256)}, u32[]{:S(2)}) copy-start(f32[256]{0:T(256)} %copy-done.65) | copy-start | bytes 3076
  (90 other events, 338.9 us)
Sparse Core Ops, SparseCore 0:
  26.4 41.8 all-gather.12
  70.5 37.4 all-gather.24
  109.6 37.4 all-gather.10
  148.5 37.4 all-gather.22
  360.2 38.5 reduce-scatter.8
  436.8 38.5 reduce-scatter.4
  477.7 39.3 reduce-scatter.6
  519.4 39.4 reduce-scatter.10
  1049.1 53.0 all-gather.16
  1105.6 59.1 all-gather.14
  1168.4 62.4 all-gather.18
  1233.8 62.4 all-gather.20
where the time goes:
time: 1320 us; the launch traced here: 1310 us
  blocking collectives  502 us (38%)
  matrix products  283 us (21%)
  waiting for transfers between devices  272 us (21%)
  local copies, waits for them, and re-layouts  158 us (12%)
  other arithmetic  71 us (5%)
  between operations  15.4 us (1%)
    unnamed x2, blocking collectives  502 us
    all_gather x1, waiting for transfers between devices, local(): lax.all_gather(shares[3].astype(jnp.bfloat16), ('dp', 'blk'), axis=0, til...  58.2 us
    all_gather x1, waiting for transfers between devices, local(): lax.all_gather(shares[4].astype(jnp.bfloat16), ('dp', 'blk'), axis=0, til...  56.6 us
    all_gather x1, waiting for transfers between devices, local(): lax.all_gather(shares[1].astype(jnp.bfloat16), ('dp', 'blk'), axis=0, til...  51.9 us
    all_gather x2, waiting for transfers between devices, local(): lax.all_gather(key_own, 'blk', axis=0, tiled=True)  50.1 us
    dot_general x8, matrix products, grad_step(): jnp.einsum('qhd,khd->hqk', out_grad, value_rows, preferred_element_type=j...  43.1 us
    dot_general x8, matrix products, attend_step(): jnp.einsum('qhd,khd->hqk', queries, key_rows, preferred_element_type=jnp....  40 us
    unnamed x149, local copies, waits for them, and re-layouts  36.6 us
  transfers between devices with their start and end apart: 12, of which 7 were waited for; matrix products, arithmetic and copies ran while one was open for 23% of the time, Pallas kernels for 0%

commit v1 on v0

v1 whole, which is shorter than its diff:
```python
from functools import partial

import jax
import jax.numpy as jnp
from jax import lax
from jax.experimental import pallas as pl
from jax.experimental.pallas import tpu as pltpu
from jax.sharding import PartitionSpec as P

HEAD = 64
ROT = 16
TENSOR = 4
LANES = 128
norm_eps = 1e-05
masked_score = -1e30
F32 = jnp.float32
BF16 = jnp.bfloat16
VMEM_LIMIT = 56 * 1024 * 1024

NN = (((1,), (0,)), ((), ()))
NT = (((1,), (1,)), ((), ()))
TN = (((0,), (0,)), ((), ()))


def mul(a, b, dims=NN):
    return lax.dot_general(a, b, dims, preferred_element_type=F32)


def params(semantics=1):
    return pltpu.CompilerParams(
        dimension_semantics=("arbitrary",) * semantics, vmem_limit_bytes=VMEM_LIMIT
    )


def cost(flops, moved, special=0):
    return pl.CostEstimate(flops=int(flops), bytes_accessed=int(moved), transcendentals=int(special))


def sds(shape, dtype):
    return jax.ShapeDtypeStruct(shape, dtype)


def whole(shape):
    return pl.BlockSpec(shape, lambda *_: (0,) * len(shape))


def lane_low(rows):
    return lax.broadcasted_iota(jnp.int32, (rows, LANES), 1) < HEAD


def project_kernel(n_heads, scalars, x_ref, gain_ref, bias_ref, w_ref, cc_ref, ss_ref, *refs):
    normed_ref, q_ref, k_ref, kt_ref, v_ref, vt_ref = refs[-6:]
    x = x_ref[0].astype(F32)
    mean = jnp.mean(x, axis=1, keepdims=True)
    centred = x - mean
    inverse = lax.rsqrt(jnp.mean(centred * centred, axis=1, keepdims=True) + norm_eps)
    normed = (centred * inverse * gain_ref[...] + bias_ref[...]).astype(BF16)
    normed_ref[0] = normed
    wide = mul(normed, w_ref[...])
    cc, ss = cc_ref[0], ss_ref[0]

    def turned(index):
        part = wide[:, index * LANES : (index + 1) * LANES]
        return part * cc + pltpu.roll(part, HEAD, 1) * ss

    for h in range(n_heads):
        q_ref[0, h] = (turned(h) * (0.5 * HEAD**-0.5)).astype(BF16)
        key = turned(n_heads + h)
        k_ref[0, h] = key.astype(BF16)
        kt_ref[0, h] = key.T.astype(BF16)
    values = wide[:, 2 * n_heads * LANES :]
    v_ref[0] = values.astype(BF16)
    vt_ref[0] = values.T.astype(BF16)


def project(x_blocks, base, total, shared, earlier, sizes):
    n, rows, width = x_blocks.shape
    n_heads, v_wide = sizes
    gain, bias, w_wide, cc, ss = shared
    out_shapes = [
        sds((total, rows, width), BF16),
        sds((total, n_heads, rows, LANES), BF16),
        sds((total, n_heads, rows, LANES), BF16),
        sds((total, n_heads, LANES, rows), BF16),
        sds((total, rows, v_wide), BF16),
        sds((total, v_wide, rows), BF16),
    ]

    def at(shape):
        zeros = (0,) * (len(shape) - 1)
        return pl.BlockSpec((1,) + tuple(shape[1:]), lambda i, s: (i + base,) + zeros)

    in_specs = [
        pl.BlockSpec((1, rows, width), lambda i, s: (i, 0, 0)),
        whole((1, width)),
        whole((1, width)),
        whole(w_wide.shape),
        at(cc.shape),
        at(ss.shape),
    ]
    operands = [x_blocks, gain, bias, w_wide, cc, ss]
    aliases = {}
    if earlier is not None:
        for k, array in enumerate(earlier):
            aliases[1 + len(operands)] = k
            operands.append(array)
            in_specs.append(pl.BlockSpec(memory_space=pl.ANY))
    return pl.pallas_call(
        partial(project_kernel, n_heads),
        out_shape=out_shapes,
        grid_spec=pltpu.PrefetchScalarGridSpec(
            num_scalar_prefetch=1,
            grid=(n,),
            in_specs=in_specs,
            out_specs=[at(o.shape) for o in out_shapes],
        ),
        input_output_aliases=aliases,
        compiler_params=params(),
        cost_estimate=cost(2 * n * rows * width * w_wide.shape[1], 4 * n * rows * width * 3),
        name="project",
    )(jnp.zeros((1,), jnp.int32), *operands)


def attend_kernel(n_heads, tabs, q_ref, k_ref, vt_ref, start_ref, att_ref, attf_ref, lse_ref):
    q_log, d_first, d_last, k_arr = tabs
    j = pl.program_id(0)
    rows = q_ref.shape[2]
    block = q_log[j]
    starts = start_ref[0]
    q_index = block * rows + lax.broadcasted_iota(jnp.int32, (1, rows), 1)

    def step(kb, carry, masked):
        ka = k_arr[kb]
        if masked:
            k_index = kb * rows + lax.broadcasted_iota(jnp.int32, (rows, rows), 0)
            allowed = (k_index >= starts) & (k_index <= q_index)
        new = []
        for h in range(n_heads):
            m, l, acc = carry[h]
            s = mul(k_ref[ka, h], q_ref[0, h], NT)
            if masked:
                s = jnp.where(allowed, s, masked_score)
            top = jnp.maximum(m, jnp.max(s, axis=0, keepdims=True))
            p = jnp.exp(s - top)
            fade = jnp.exp(m - top)
            l = l * fade + jnp.sum(p, axis=0, keepdims=True)
            acc = acc * fade + mul(vt_ref[ka, h * HEAD : (h + 1) * HEAD], p.astype(BF16))
            new.append((top, l, acc))
        return tuple(new)

    carry = tuple(
        (
            jnp.full((1, rows), masked_score, F32),
            jnp.zeros((1, rows), F32),
            jnp.zeros((HEAD, rows), F32),
        )
        for _ in range(n_heads)
    )
    carry = step(block, carry, True)
    low = d_first[j] // rows
    full = jnp.minimum(block, (d_last[j] + rows - 1) // rows)
    carry = lax.fori_loop(low, full, lambda kb, c: step(kb, c, True), carry)
    carry = lax.fori_loop(full, block, lambda kb, c: step(kb, c, False), carry)
    lse_ref[0] = jnp.zeros_like(lse_ref[0])
    for h in range(n_heads):
        m, l, acc = carry[h]
        out = acc / l
        attf_ref[0, h * HEAD : (h + 1) * HEAD] = out
        att_ref[0, h * HEAD : (h + 1) * HEAD] = out.astype(BF16)
        lse_ref[0, h : h + 1] = m + jnp.log(l)


def attend(tabs, q, k, vt, starts):
    n, n_heads, rows, _ = q.shape
    wide = n_heads * HEAD
    pairs = 0.56 * n * k.shape[0]

    def at(shape):
        zeros = (0,) * (len(shape) - 1)
        return pl.BlockSpec((1,) + tuple(shape[1:]), lambda i, *s: (i,) + zeros)

    out_shapes = [
        sds((n, wide, rows), BF16),
        sds((n, wide, rows), F32),
        sds((n, 8, rows), F32),
    ]

    def body(a, b, c, d, *refs):
        attend_kernel(n_heads, (a, b, c, d), *refs)

    return pl.pallas_call(
        body,
        out_shape=out_shapes,
        grid_spec=pltpu.PrefetchScalarGridSpec(
            num_scalar_prefetch=4,
            grid=(n,),
            in_specs=[at(q.shape), whole(k.shape), whole(vt.shape), at(starts.shape)],
            out_specs=[at(o.shape) for o in out_shapes],
        ),
        compiler_params=params(),
        cost_estimate=cost(
            pairs * n_heads * rows * rows * 256 * 2, 8 * n * rows * LANES * 12, pairs * rows * rows * 3
        ),
        name="attend",
    )(*tabs, q, k, vt, starts)


def gelu_pair(hidden):
    cdf = 0.5 + 0.5 * lax.erf(hidden * (0.5**0.5))
    density = jnp.exp(hidden * hidden * -0.5) * 0.3989422804014327
    return hidden * cdf, cdf + hidden * density


def put_pieces(scratch, where, piece, outs, slot):
    x, y = where
    send_a, keep_a, send_b, keep_b = outs

    def rows_of(ab, cx, cy):
        return scratch[pl.ds(pl.multiple_of(((ab * 2 + cx) * 2 + cy) * piece, 16), piece), :].astype(BF16)

    for other in range(2):
        cy = jnp.bitwise_xor(y, other)
        send_a[other, slot, 0:piece] = rows_of(0, 1 - x, cy)
        keep_a[other, slot, 0:piece] = rows_of(0, x, cy)
        cx = jnp.bitwise_xor(x, other)
        send_b[other, slot, 0:piece] = rows_of(1, cx, 1 - y)
        keep_b[other, slot, 0:piece] = rows_of(1, cx, y)


def feed_kernel(n, first, last, where, normed_ref, cot_ref, up_ref, down_ref, *refs):
    n_in = 0 if first else 4
    ins, outs = refs[:n_in], refs[n_in:]
    mo_ref, ng_ref = outs[0], outs[1]
    gup_ref, gdn_ref = (outs[2], outs[3]) if not last else outs[-2:]
    i = pl.program_id(0)
    normed, cot = normed_ref[0], cot_ref[0]
    up, down = up_ref[...], down_ref[...]
    hidden = mul(normed, up)
    active, slope = gelu_pair(hidden)
    active = active.astype(BF16)
    mo_ref[0] = mul(active, down)
    hidden_grad = (mul(cot, down, NT) * slope).astype(BF16)
    ng_ref[0] = mul(hidden_grad, up, NT)
    gup = mul(normed, hidden_grad, TN)
    gdn = mul(active, cot, TN)

    @pl.when(i == 0)
    def _():
        if first:
            gup_ref[...] = gup
            gdn_ref[...] = gdn
        else:
            gup_ref[...] = ins[2][...] + gup
            gdn_ref[...] = ins[3][...] + gdn

    @pl.when(i > 0)
    def _():
        gup_ref[...] += gup
        gdn_ref[...] += gdn

    if last:

        @pl.when(i == n - 1)
        def _():
            piece = gup_ref.shape[0] // 8
            spot = (where[1], where[2])
            put_pieces(gup_ref, spot, piece, outs[2:6], 0)
            put_pieces(gdn_ref, spot, piece, outs[2:6], 1)


def feed(where, normed, cot_blocks, base, w_up, w_down, earlier, last):
    n, rows, width = cot_blocks.shape
    total = normed.shape[0]
    inner = w_up.shape[1] // TENSOR
    first = earlier is None
    at = pl.BlockSpec((1, rows, width), lambda i, s: (i + base, 0, 0))
    in_specs = [
        at,
        pl.BlockSpec((1, rows, width), lambda i, s: (i, 0, 0)),
        pl.BlockSpec((width, inner), lambda i, s: (0, s[0])),
        pl.BlockSpec((inner, width), lambda i, s: (s[0], 0)),
    ]
    operands = [normed, cot_blocks, w_up, w_down]
    out_shapes = [sds((total, rows, width), F32)] * 2
    out_specs = [at, at]
    scratch = []
    aliases = {}
    if not first:
        in_specs += [pl.BlockSpec(memory_space=pl.ANY)] * 2 + [whole((width, inner)), whole((inner, width))]
        operands += list(earlier)
        aliases = {5: 0, 6: 1}
    if last:
        piece = sds((2, 2, inner // 8, width), BF16)
        out_shapes += [piece] * 4
        out_specs += [whole(piece.shape)] * 4
        scratch = [pltpu.VMEM((width, inner), F32), pltpu.VMEM((inner, width), F32)]
    else:
        out_shapes += [sds((width, inner), F32), sds((inner, width), F32)]
        out_specs += [whole((width, inner)), whole((inner, width))]
    return pl.pallas_call(
        partial(feed_kernel, n, first, last),
        out_shape=out_shapes,
        grid_spec=pltpu.PrefetchScalarGridSpec(
            num_scalar_prefetch=1,
            grid=(n,),
            in_specs=in_specs,
            out_specs=out_specs,
            scratch_shapes=scratch,
        ),
        input_output_aliases=aliases,
        compiler_params=params(),
        cost_estimate=cost(12 * n * rows * width * inner, 12 * n * rows * width + 4 * width * inner),
        name="feed",
    )(where, *operands)


def mix_kernel(n_heads, where, att_ref, attf_ref, cot_ref, mo_ref, w_ref, out_ref, do_ref, delta_ref, go_ref):
    i = pl.program_id(0)
    wide = n_heads * HEAD
    att, cot, w = att_ref[0], cot_ref[0], w_ref[...]
    out_ref[0] = (mo_ref[0] + mul(att, w, TN)).astype(BF16)
    grad = mul(cot, w, NT).astype(BF16)
    do_ref[0] = jnp.zeros_like(do_ref[0])
    do_ref[0, :, 0:wide] = grad
    rows = cot.shape[0]
    product = mul(w, cot, NT).astype(BF16).astype(F32) * attf_ref[0]
    delta_ref[0] = jnp.zeros_like(delta_ref[0])
    for h in range(n_heads):
        delta_ref[0, h : h + 1] = jnp.sum(product[h * HEAD : (h + 1) * HEAD], axis=0, keepdims=True)
    go = mul(att, cot)

    @pl.when(i == 0)
    def _():
        go_ref[...] = go

    @pl.when(i > 0)
    def _():
        go_ref[...] += go


def mix(where, att, attf, cot, mo, w_out, v_wide):
    n, rows, width = cot.shape
    wide = att.shape[1]
    n_heads = wide // HEAD

    def at(shape):
        zeros = (0,) * (len(shape) - 1)
        return pl.BlockSpec((1,) + tuple(shape[1:]), lambda i, s: (i,) + zeros)

    out_shapes = [
        sds((n, rows, width), BF16),
        sds((n, rows, v_wide), BF16),
        sds((n, 8, rows), F32),
        sds((wide, width), F32),
    ]
    return pl.pallas_call(
        partial(mix_kernel, n_heads),
        out_shape=out_shapes,
        grid_spec=pltpu.PrefetchScalarGridSpec(
            num_scalar_prefetch=1,
            grid=(n,),
            in_specs=[
                at(att.shape),
                at(attf.shape),
                at(cot.shape),
                at(mo.shape),
                pl.BlockSpec((wide, width), lambda i, s: (s[0], 0)),
            ],
            out_specs=[at(o.shape) for o in out_shapes[:3]] + [whole((wide, width))],
        ),
        compiler_params=params(),
        cost_estimate=cost(8 * n * rows * width * wide, 10 * n * rows * width),
        name="mix",
    )(where, att, attf, cot, mo, w_out)


def back_kernel(
    n_heads, n_q, n_k, tabs, q_ref, do_ref, lse_ref, delta_ref, start_ref, ccq_ref, ssq_ref, k_ref, kt_ref, v_ref, cck_ref, ssk_ref, jq_ref, jk_ref, jv_ref, dq_ref, dk_ref, dv_ref
):
    q_log, d_first, d_last, k_log = tabs
    i = pl.program_id(0)
    rows = k_ref.shape[2]
    kb = k_log[i]
    low = lane_low(rows)

    @pl.when(i == 0)
    def _():
        dq_ref[...] = jnp.zeros_like(dq_ref)

    dk_ref[...] = jnp.zeros_like(dk_ref)
    dv_ref[...] = jnp.zeros_like(dv_ref)
    v_heads = []
    for h in range(n_heads):
        tile = v_ref[0, :, (h // 2) * LANES : (h // 2 + 1) * LANES]
        keep = low if h % 2 == 0 else ~low
        v_heads.append(jnp.where(keep, tile, jnp.zeros_like(tile)))

    def step(j, masked):
        if masked:
            k_index = kb * rows + lax.broadcasted_iota(jnp.int32, (rows, rows), 0)
            q_index = q_log[j] * rows + lax.broadcasted_iota(jnp.int32, (1, rows), 1)
            allowed = (k_index >= start_ref[j]) & (k_index <= q_index)
        for h in range(n_heads):
            q = q_ref[j, h]
            do = do_ref[j, :, (h // 2) * LANES : (h // 2 + 1) * LANES]
            s = mul(k_ref[0, h], q, NT)
            p = jnp.exp(s - lse_ref[j, h : h + 1])
            if masked:
                p = jnp.where(allowed, p, 0.0)
            dp = mul(v_heads[h], do, NT)
            ds = (p * (dp - delta_ref[j, h : h + 1])).astype(BF16)
            dv_ref[h] += mul(p.astype(BF16), do)
            dk_ref[h] += mul(ds, q)
            dq_ref[j, h] += mul(kt_ref[0, h], ds)

    def visit(j, _):
        block = q_log[j]
        active = (block >= kb) & (d_first[j] < (kb + 1) * rows)
        masked = (block == kb) | (d_last[j] > kb * rows)

        @pl.when(active & masked)
        def _():
            step(j, True)

        @pl.when(active & jnp.logical_not(masked))
        def _():
            step(j, False)

        return 0

    lax.fori_loop(0, n_q, visit, 0)

    def unturn(grad, cc, ss, scale):
        both = grad * jnp.where(low, cc, ss)
        return (both + pltpu.roll(both, HEAD, 1)) * scale

    def pack(parts):
        tiles = []
        for h in range(0, n_heads, 2):
            second = parts[h + 1] if h + 1 < n_heads else jnp.zeros_like(parts[h])
            tiles.append(jnp.where(low, parts[h], second))
        return tiles

    cck, ssk = cck_ref[0], ssk_ref[0]
    for t, tile in enumerate(pack([unturn(dk_ref[h], cck, ssk, 2.0) for h in range(n_heads)])):
        jk_ref[0, :, t * LANES : (t + 1) * LANES] = tile.astype(BF16)
    for t, tile in enumerate(pack([dv_ref[h] for h in range(n_heads)])):
        jv_ref[0, :, t * LANES : (t + 1) * LANES] = tile.astype(BF16)

    @pl.when(i == n_k - 1)
    def _():
        def finish(j, _):
            cc, ss = ccq_ref[j], ssq_ref[j]
            parts = [unturn(dq_ref[j, h].T, cc, ss, HEAD**-0.5) for h in range(n_heads)]
            for t, tile in enumerate(pack(parts)):
                jq_ref[j, :, t * LANES : (t + 1) * LANES] = tile.astype(BF16)
            return 0

        lax.fori_loop(0, n_q, finish, 0)


def attend_back(tabs, q, do, lse, delta, starts, ccq, ssq, k, kt, v, cck, ssk):
    n_q, n_heads, rows, _ = q.shape
    n_k = k.shape[0]
    v_wide = v.shape[2]
    pairs = 0.56 * n_q * n_k

    def at(shape):
        zeros = (0,) * (len(shape) - 1)
        return pl.BlockSpec((1,) + tuple(shape[1:]), lambda i, *s: (i,) + zeros)

    def body(a, b, c, d, *refs):
        back_kernel(n_heads, n_q, n_k, (a, b, c, d), *refs)

    full = [q, do, lse, delta, starts, ccq, ssq]
    cut = [k, kt, v, cck, ssk]
    out_shapes = [
        sds((n_q, rows, v_wide), BF16),
        sds((n_k, rows, v_wide), BF16),
        sds((n_k, rows, v_wide), BF16),
    ]
    return pl.pallas_call(
        body,
        out_shape=out_shapes,
        grid_spec=pltpu.PrefetchScalarGridSpec(
            num_scalar_prefetch=4,
            grid=(n_k,),
            in_specs=[whole(a.shape) for a in full] + [at(a.shape) for a in cut],
            out_specs=[whole(out_shapes[0].shape)] + [at(o.shape) for o in out_shapes[1:]],
            scratch_shapes=[
                pltpu.VMEM((n_q, n_heads, LANES, rows), F32),
                pltpu.VMEM((n_heads, rows, LANES), F32),
                pltpu.VMEM((n_heads, rows, LANES), F32),
            ],
        ),
        compiler_params=params(),
        cost_estimate=cost(
            pairs * n_heads * rows * rows * 256 * 2 * 3, 10 * n_q * rows * 768, pairs * rows * rows * 3
        ),
        name="attend_back",
    )(*tabs, *full, *cut)


def join_kernel(n, n_heads, where, jq_ref, jk_ref, jv_ref, normed_ref, x_ref, ngm_ref, w_ref, go_ref, ng_ref, *refs):
    outs, (gq_ref, gb_ref, all_ref) = refs[:4], refs[4:]
    i = pl.program_id(0)
    v_wide = jq_ref.shape[2]
    wide = n_heads * HEAD
    joined = jnp.concatenate([jq_ref[0], jk_ref[0], jv_ref[0]], axis=1)
    gq = mul(joined, normed_ref[0], TN)
    ng = ngm_ref[0] + mul(joined, w_ref[...], NT)
    ng_ref[0] = ng.astype(BF16)
    x = x_ref[0].astype(F32)
    centred = x - jnp.mean(x, axis=1, keepdims=True)
    xhat = centred * lax.rsqrt(jnp.mean(centred * centred, axis=1, keepdims=True) + norm_eps)
    sums = jnp.concatenate(
        [jnp.sum(ng * xhat, axis=0, keepdims=True), jnp.sum(ng, axis=0, keepdims=True), jnp.zeros((14, ng.shape[1]), F32)],
        axis=0,
    )

    @pl.when(i == 0)
    def _():
        gq_ref[...] = gq
        gb_ref[...] = sums

    @pl.when(i > 0)
    def _():
        gq_ref[...] += gq
        gb_ref[...] += sums

    @pl.when(i == n - 1)
    def _():
        for third in range(3):
            all_ref[third * wide : (third + 1) * wide, :] = gq_ref[third * v_wide : third * v_wide + wide, :]
        all_ref[3 * wide :, :] = go_ref[...]
        piece = all_ref.shape[0] // 8
        put_pieces(all_ref, (where[1], where[2]), piece, outs, 0)
        extra = gb_ref[...].astype(BF16)
        for out in outs:
            for other in range(2):
                out[other, 0, piece:] = extra


def join(where, jq, jk, jv, normed, x, ngm, w_pad, grad_out):
    n, rows, width = normed.shape
    wide = grad_out.shape[0]
    n_heads = wide // HEAD

    def at(shape):
        zeros = (0,) * (len(shape) - 1)
        return pl.BlockSpec((1,) + tuple(shape[1:]), lambda i, s: (i,) + zeros)

    piece = sds((2, 1, 4 * wide // 8 + 16, width), BF16)
    tiled = [jq, jk, jv, normed, x, ngm]
    return pl.pallas_call(
        partial(join_kernel, n, n_heads),
        out_shape=[sds((n, rows, width), BF16)] + [piece] * 4,
        grid_spec=pltpu.PrefetchScalarGridSpec(
            num_scalar_prefetch=1,
            grid=(n,),
            in_specs=[at(a.shape) for a in tiled] + [whole(w_pad.shape), whole(grad_out.shape)],
            out_specs=[at(normed.shape)] + [whole(piece.shape)] * 4,
            scratch_shapes=[
                pltpu.VMEM((w_pad.shape[1], width), F32),
                pltpu.VMEM((16, width), F32),
                pltpu.VMEM((4 * wide, width), F32),
            ],
        ),
        compiler_params=params(),
        cost_estimate=cost(4 * n * rows * width * w_pad.shape[1], 14 * n * rows * width),
        name="join",
    )(where, *tiled, w_pad, grad_out)


def swap(x, axis, size, mask):
    return lax.ppermute(x, axis, [(i, i ^ mask) for i in range(size)])


def add(a, b):
    return a.astype(F32) + b.astype(F32)


def fill_kernel(table, src_ref, *refs):
    up_ref, down_ref = refs[-2:]
    up_ref[...] = src_ref[0, 0, 0].astype(F32)
    down_ref[...] = src_ref[0, 0, 1].astype(F32)


def fill(arrays, tables, shapes, earlier):
    for array, table in zip(arrays, tables):
        a, b, _, rows, width = array.shape
        aliases, extra, specs = {}, [], []
        if earlier is not None:
            aliases = {2: 0, 3: 1}
            extra = list(earlier)
            specs = [pl.BlockSpec(memory_space=pl.ANY)] * 2
        earlier = pl.pallas_call(
            fill_kernel,
            out_shape=[sds(s, F32) for s in shapes],
            grid_spec=pltpu.PrefetchScalarGridSpec(
                num_scalar_prefetch=1,
                grid=(a * b,),
                in_specs=[
                    pl.BlockSpec((1, 1, 2, rows, width), lambda i, s: (i // b, lax.rem(i, b), 0, 0, 0))
                ]
                + specs,
                out_specs=[
                    pl.BlockSpec((rows, width), lambda i, s: (s[2 * i], s[2 * i + 1])),
                    pl.BlockSpec((rows, width), lambda i, s: (s[2 * i + 1] * 8 + s[2 * i], 0)),
                ],
            ),
            input_output_aliases=aliases,
            compiler_params=params(),
            cost_estimate=cost(0, array.size * 6),
            name="fill",
        )(table, array, *extra)
    return earlier


def reduce_over_dp(parts):
    send_a, keep_a, send_b, keep_b = parts
    got_a, got_b = swap(send_a, "dp", 4, 1), swap(send_b, "dp", 4, 2)
    sum_a, sum_b = add(keep_a, got_a).astype(BF16), add(keep_b, got_b).astype(BF16)
    got_a, got_b = swap(sum_a[1], "dp", 4, 2), swap(sum_b[1], "dp", 4, 1)
    return jnp.stack([add(sum_a[0], got_a), add(sum_b[0], got_b)]).astype(BF16)


def spread(own, n_blk):
    other = swap(own, "blk", n_blk, n_blk // 2)
    total = add(own, other).astype(BF16)
    near = swap(total, "blk", n_blk, 2)
    pair = jnp.stack([total, near])
    pair_a, pair_b = pair[:, 0], pair[:, 1]
    x_a, y_b = swap(pair_a, "dp", 4, 1), swap(pair_b, "dp", 4, 2)
    two_a, two_b = jnp.stack([pair_a, x_a]), jnp.stack([pair_b, y_b])
    far_a, far_b = swap(two_a, "dp", 4, 2), swap(two_b, "dp", 4, 1)
    out = [two_a, two_b, far_a, far_b]
    return out, [swap(o, "blk", n_blk, 1) for o in out]


def piece_tables(x, y, t):
    tables = []
    for core in range(2):
        for name in ("two_a", "two_b", "far_a", "far_b"):
            rows = []
            for outer in range(2):
                for rt1 in range(2):
                    if name == "two_a":
                        ab, rx, ry = 0, outer, 0
                    elif name == "two_b":
                        ab, rx, ry = 1, 0, outer
                    elif name == "far_a":
                        ab, rx, ry = 0, outer, 1
                    else:
                        ab, rx, ry = 1, 1, outer
                    piece = (ab * 2 + jnp.bitwise_xor(x, rx)) * 2 + jnp.bitwise_xor(y, ry)
                    shard = jnp.bitwise_xor(t, rt1 * 2 + core)
                    rows += [piece, shard]
            tables.append(jnp.stack(rows).astype(jnp.int32))
    return tables


def tail_kernel(n_src, wide, tabs, *refs):
    srcs, (gq_ref, go_ref, hold_ref) = refs[:n_src], refs[n_src:]
    rows = srcs[0].shape[3] - 16
    width = srcs[0].shape[4]
    for k, src in enumerate(srcs):
        for a in range(2):
            for b in range(2):
                at = (k * 4 + a * 2 + b) * 2
                piece, shard = tabs[at], tabs[at + 1]
                hold_ref[pl.ds(pl.multiple_of(shard * 4 * wide + piece * rows, 16), rows), :] = src[a, b, 0, 0:rows].astype(F32)
    for shard in range(TENSOR):
        go_ref[shard * wide : (shard + 1) * wide, :] = hold_ref[shard * 4 * wide + 3 * wide : (shard + 1) * 4 * wide, :]
    for third in range(3):
        block = jnp.concatenate(
            [hold_ref[s * 4 * wide + third * wide : s * 4 * wide + (third + 1) * wide, :] for s in range(TENSOR)], axis=0
        )
        gq_ref[:, third * width : (third + 1) * width] = block.T


def tail(arrays, tables, width, wide):
    table = jnp.concatenate(tables)
    return pl.pallas_call(
        partial(tail_kernel, len(arrays), wide),
        out_shape=[sds((width, 3 * TENSOR * wide), F32), sds((TENSOR * wide, width), F32)],
        grid_spec=pltpu.PrefetchScalarGridSpec(
            num_scalar_prefetch=1,
            grid=(1,),
            in_specs=[whole(a.shape) for a in arrays],
            out_specs=[whole((width, 3 * TENSOR * wide)), whole((TENSOR * wide, width))],
            scratch_shapes=[pltpu.VMEM((TENSOR * 4 * wide, width), F32)],
        ),
        compiler_params=params(),
        cost_estimate=cost(0, 6 * 4 * width * width),
        name="tail",
    )(table, *arrays)


def natural(parts):
    send_a, keep_a, send_b, keep_b = parts
    a = jnp.stack([keep_a, send_a])
    b = jnp.stack([keep_b, send_b]).swapaxes(0, 1)
    both = jnp.stack([a, b])
    n, rows, width = both.shape[3:]
    return both.reshape(8, n, rows, width)


def xor_gather(x, n_blk, masks):
    for mask in reversed(masks):
        x = jnp.concatenate([x, swap(x, "blk", n_blk, mask)])
    return x


def gather_half(own, n_blk):
    pair = jnp.stack([own, swap(own, "blk", n_blk, 2)])
    return jnp.concatenate([pair, swap(pair, "blk", n_blk, 1)])


def scatter_blocks(blocks, n_blk):
    send = jnp.concatenate([blocks[6:8], blocks[2:4]])
    got = swap(send, "blk", n_blk, 1)
    far = add(blocks[4:6], got[0:2]).astype(BF16)
    near = add(blocks[0:2], got[2:4]).astype(BF16)
    far_got = swap(far[1], "blk", n_blk, 2)
    far_sum = add(far[0], far_got).astype(BF16)
    other = swap(far_sum, "blk", n_blk, n_blk // 2)
    near_got = swap(near[1], "blk", n_blk, 2)
    return add(near[0], near_got), other.astype(F32)


def local(n_dp, n_blk, tokens, cotangent, lengths, norm_gain, norm_bias, w_qkv, w_out, w_up, w_down):
    micro_count, rows, width = tokens.shape
    heads = width // HEAD
    n_heads = heads // TENSOR
    v_wide = (n_heads + 1) // 2 * LANES
    wide = n_heads * HEAD
    inner = w_up.shape[1] // TENSOR
    splits = n_blk // (2 * TENSOR)
    s_masks = [TENSOR << b for b in reversed(range(splits.bit_length() - 1))]
    fast = n_dp == 4 and splits == 1
    me = lax.axis_index("blk")
    dp = lax.axis_index("dp")
    half = me // (n_blk // 2)
    quarter = lax.rem(me, TENSOR)
    x_pos, y_pos = (lax.rem(dp, 2), dp // 2) if fast else (jnp.int32(0), jnp.int32(0))
    where = jnp.stack([quarter, x_pos, y_pos]).astype(jnp.int32)

    masks = [h * (n_blk // 2) + r for h in range(2) for r in (0, 2, 1, 3)]
    n_q = len(masks)
    q_log = jnp.bitwise_xor(me, jnp.array(masks, jnp.int32))
    s_list = [0]
    for mask in reversed(s_masks):
        s_list = s_list + [v ^ mask for v in s_list]
    k_log = jnp.bitwise_xor(me, jnp.array([m ^ s for s in s_list for m in masks], jnp.int32))
    n_k = n_q * splits
    k_arr = jnp.sum(
        jnp.where(k_log[None, :] == jnp.arange(n_k)[:, None], jnp.arange(n_k)[None, :], 0), axis=1
    ).astype(jnp.int32)

    doc_lengths = lax.dynamic_index_in_dim(lengths, half, 0, False)[0]
    doc_ends = jnp.cumsum(doc_lengths, dtype=jnp.int32)
    doc_starts = doc_ends - doc_lengths

    def start_of(index):
        begun = (index[..., None] >= doc_starts).astype(jnp.int32) * doc_lengths_before
        return jnp.sum(begun, axis=-1)

    doc_lengths_before = doc_starts - jnp.concatenate([jnp.zeros((1,), jnp.int32), doc_starts[:-1]])
    q_index = q_log[:, None] * rows + jnp.arange(rows, dtype=jnp.int32)[None, :]
    starts = start_of(q_index)
    d_first, d_last = starts[:, 0], starts[:, -1]

    frequency = 10000.0 ** (-2.0 * jnp.arange(ROT // 2, dtype=F32) / ROT)

    def turn_tables(index):
        phases = (index - start_of(index)).astype(F32)[:, None, :] * frequency[None, :, None]
        cos, sin = jnp.cos(phases), jnp.sin(phases)
        ones = jnp.ones((index.shape[0], HEAD - ROT, rows), F32)
        zeros = jnp.zeros_like(ones)
        cc = jnp.concatenate([cos, cos, ones] * 2, axis=1).swapaxes(1, 2)
        ss = jnp.concatenate([-sin, sin, zeros, sin, -sin, zeros], axis=1).swapaxes(1, 2)
        return cc, ss

    cc_q, ss_q = turn_tables(q_index)
    if splits > 1:
        cc_k, ss_k = turn_tables(k_log[:, None] * rows + jnp.arange(rows, dtype=jnp.int32)[None, :])
    else:
        cc_k, ss_k = cc_q, ss_q

    cut = lax.dynamic_slice_in_dim(w_qkv.reshape(width, 3, heads * HEAD), quarter * wide, wide, 2)
    cut = cut.reshape(width, 3, n_heads, HEAD)
    swapped = jnp.concatenate([cut[..., ROT // 2 : ROT], cut[..., : ROT // 2], cut[..., ROT:]], axis=-1)
    doubled = jnp.concatenate([cut, swapped], axis=-1)[:, :2].reshape(width, 2 * n_heads * LANES)
    pad = jnp.zeros((width, 3, v_wide - wide), BF16)
    w_pad = jnp.concatenate([cut.reshape(width, 3, wide), pad], axis=2)
    w_wide = jnp.concatenate([doubled, w_pad[:, 2]], axis=1)
    w_pad = w_pad.reshape(width, 3 * v_wide)

    gain = norm_gain.astype(F32).reshape(1, width)
    bias = norm_bias.astype(F32).reshape(1, width)

    def mine(array):
        return lax.dynamic_index_in_dim(array, half, 0, False), lax.dynamic_index_in_dim(array, 1 - half, 0, False)

    x_mine, x_other = mine(tokens)
    c_mine, c_other = mine(cotangent)
    x_cross = swap(x_other, "blk", n_blk, n_blk // 2)
    x_near = gather_half(x_mine, n_blk)
    x_far = gather_half(x_cross, n_blk)
    c_cross = swap(c_other, "blk", n_blk, n_blk // 2)
    c_near = gather_half(c_mine, n_blk)
    c_far = gather_half(c_cross, n_blk)

    shared = (gain, bias, w_wide, cc_q, ss_q)
    sizes = (n_heads, v_wide)
    stage = project(x_near, 0, n_q, shared, None, sizes)
    normed, q, k, kt, v, vt = project(x_far, 4, n_q, shared, stage, sizes)
    if splits > 1:
        k, kt, v, vt = (xor_gather(a, n_blk, s_masks) for a in (k, kt, v, vt))
    starts_rows = starts[:, None, :]
    att, attf, lse = attend((q_log, d_first, d_last, k_arr), q, k, vt, starts_rows)

    feed_state = feed(where, normed, c_near, 0, w_up, w_down, None, False)
    mo, ngm, *mlp_parts = feed(where, normed, c_far, 4, w_up, w_down, feed_state, True)
    cot = jnp.concatenate([c_near, c_far])
    x_all = jnp.concatenate([x_near, x_far])
    out_part, do, delta, grad_out_part = mix(where, att, attf, cot, mo, w_out, v_wide)
    jq, jk, jv = attend_back(
        (q_log, d_first, d_last, k_log), q, do, lse, delta, starts_rows, cc_q, ss_q, k, kt, v, cc_k, ss_k
    )
    if splits > 1:
        for mask in s_masks:
            count = jk.shape[0] // 2
            jk = add(jk[:count], swap(jk[count:], "blk", n_blk, mask)).astype(BF16)
            jv = add(jv[:count], swap(jv[count:], "blk", n_blk, mask)).astype(BF16)
    ng_part, *join_parts = join(where, jq, jk, jv, normed, x_all, ngm, w_pad, grad_out_part)

    def ordered(own, other):
        return jnp.where(half == 0, jnp.stack([own, other]), jnp.stack([other, own]))

    output = (tokens.astype(F32) + ordered(*scatter_blocks(out_part, n_blk))).astype(BF16)
    normed_grad = ordered(*scatter_blocks(ng_part, n_blk))
    x_rows = tokens.astype(F32)
    centred = x_rows - jnp.mean(x_rows, axis=2, keepdims=True)
    inverse = lax.rsqrt(jnp.mean(centred * centred, axis=2, keepdims=True) + norm_eps)
    scaled = centred * inverse
    scaled_grad = normed_grad * norm_gain.astype(F32)
    input_grad = cotangent.astype(F32) + inverse * (
        scaled_grad
        - jnp.mean(scaled_grad, axis=2, keepdims=True)
        - scaled * jnp.mean(scaled_grad * scaled, axis=2, keepdims=True)
    )

    if fast:
        tables = piece_tables(x_pos, y_pos, quarter)
        first, twin = spread(reduce_over_dp(mlp_parts), n_blk)
        grad_up, grad_down = fill(first + twin, tables, [w_up.shape, w_down.shape], None)
        first, twin = spread(reduce_over_dp(join_parts), n_blk)
        grad_qkv, grad_out = tail(first + twin, tables, width, wide)
        norm_sums = sum(a[0, b, 0, -16:-14].astype(F32) for a in (first[0], twin[0]) for b in range(2))
        quads = jnp.stack([a[0, b, 0, -16:-14].astype(F32) for a in (first[0], twin[0]) for b in range(2)])
        order = jnp.bitwise_xor(quarter, jnp.array([0, 2, 1, 3], jnp.int32))
        norm_sums = sum(jnp.sum(jnp.where((order == s)[:, None, None], quads, 0.0), axis=0) for s in range(TENSOR))
    else:
        mlp = natural(mlp_parts)
        up = mlp[:, 0].reshape(width, inner)
        down = mlp[:, 1].reshape(inner, width)
        rest = natural(join_parts)[:, 0]
        norm_part = rest[0, -16:-14].astype(F32)
        rest = rest[:, :-16].reshape(4 * wide, width)
        turned = rest[: 3 * wide].T.reshape(width, 3, wide)
        zeros = partial(jnp.zeros, dtype=BF16)
        up = lax.dynamic_update_slice_in_dim(zeros(w_up.shape), up, quarter * inner, 1)
        down = lax.dynamic_update_slice_in_dim(zeros(w_down.shape), down, quarter * inner, 0)
        turned = lax.dynamic_update_slice_in_dim(zeros((width, 3, TENSOR * wide)), turned, quarter * wide, 2)
        out = lax.dynamic_update_slice_in_dim(zeros(w_out.shape), rest[3 * wide :], quarter * wide, 0)
        grads = lax.psum((up, down, turned, out), ("dp", "blk"))
        grad_up, grad_down, turned, grad_out = (g.astype(F32) for g in grads)
        grad_qkv = turned.reshape(w_qkv.shape)
        norm_sums = lax.psum(norm_part, ("dp", "blk"))
    return (output, input_grad, norm_sums[0], norm_sums[1], grad_qkv, grad_out, grad_up, grad_down)


def solution(mesh):
    tokens = P(None, ("dp", "blk"), None)
    return jax.shard_map(
        partial(local, mesh.shape["dp"], mesh.shape["blk"]),
        mesh=mesh,
        in_specs=(tokens, tokens, P(None, "dp", None)) + (P(),) * 6,
        out_specs=(tokens, tokens) + (P(),) * 6,
        check_vma=False,
    )
```

time: 1320 us -> 481 us (0.36)
  blocking collectives: 502 us -> 0 us
  matrix products: 283 us -> 0 us
  Pallas kernels: 0 us -> 202 us
  waiting for transfers between devices: 272 us -> 143 us
  local copies, waits for them, and re-layouts: 158 us -> 54.8 us
  starting transfers between devices: 0.67 us -> 41 us
  other arithmetic: 71 us -> 36.8 us
  between operations: 15.4 us -> 1.34 us
    unnamed x2 -> x0, blocking collectives: 502 us -> none
    dot_general x80 -> x0, matrix products: 283 us -> none  [the longest x8 43.1 us: grad_step(): jnp.einsum('qhd,khd->hqk', out_grad, value_rows, preferred_element_type=j...]
    all_gather x8 -> x0, waiting for transfers between devices: 252 us -> none  [the longest x1 58.2 us: local(): lax.all_gather(shares[3].astype(jnp.bfloat16), ('dp', 'blk'), axis=0, til...]
    pallas_call x0 -> x17, Pallas kernels: none -> 202 us  [the longest x1 44.6 us: attend_back(): pl.pallas_call(body, out_shape=out_shapes, grid_spec=pltpu.PrefetchScalar...]
    ppermute x0 -> x46, waiting for transfers between devices: none -> 143 us  [swap(): return lax.ppermute(x, axis, [(i, i ^ mask) for i in range(size)])]
    reshape x12 -> x5, local copies, waits for them, and re-layouts: 73.2 us -> 5.04 us  [the longest x1 2.38 us: local(): jnp.concatenate([cut, swapped], axis=-1)[:, :2]]
    ppermute x0 -> x46, starting transfers between devices: none -> 41 us  [swap(): return lax.ppermute(x, axis, [(i, i ^ mask) for i in range(size)])]
    reduce_sum x29 -> x6, other arithmetic: 39.9 us -> 2.02 us  [the longest x1 0.65 us: local(): jnp.sum(jnp.where(k_log[None, :] == jnp.arange(n_k)[:, None], jnp.arange(...]
  transfers between devices with their start and end apart: 12 -> 46, of which waited for: 7 -> 17; matrix products, arithmetic and copies ran while one was open for 23% -> 17% of each run, Pallas kernels for 0% -> 15%
where the time goes in v1:
time: 481 us; the launch traced here: 479 us
  Pallas kernels  202 us (42%)
  waiting for transfers between devices  143 us (30%)
  local copies, waits for them, and re-layouts  54.8 us (11%)
  starting transfers between devices  41 us (9%)
  other arithmetic  36.8 us (8%)
    ppermute x46, waiting for transfers between devices, swap(): return lax.ppermute(x, axis, [(i, i ^ mask) for i in range(size)])  143 us
    pallas_call x1, Pallas kernels, attend_back(): pl.pallas_call(body, out_shape=out_shapes, grid_spec=pltpu.PrefetchScalar...  44.6 us
    ppermute x46, starting transfers between devices, swap(): return lax.ppermute(x, axis, [(i, i ^ mask) for i in range(size)])  41 us
    pallas_call x1, Pallas kernels, attend(): pl.pallas_call(body, out_shape=out_shapes, grid_spec=pltpu.PrefetchScalar...  39.6 us
    pallas_call x8, Pallas kernels, fill(): pl.pallas_call(fill_kernel, out_shape=[sds(s, F32) for s in shapes], grid...  34.5 us
    pallas_call x2, Pallas kernels, feed(): pl.pallas_call(partial(feed_kernel, n, first, last), out_shape=out_shapes...  32.8 us
    unnamed x81, local copies, waits for them, and re-layouts  26.1 us
    pallas_call x1, Pallas kernels, join(): pl.pallas_call(partial(join_kernel, n, n_heads), out_shape=[sds((n, rows,...  15.6 us
  transfers between devices with their start and end apart: 46, of which 17 were waited for; matrix products, arithmetic and copies ran while one was open for 17% of the time, Pallas kernels for 15%

profile of v1, /device:TPU:0, one launch (start us, length us, event | category | flops | bytes accessed | tf_op | source)
XLA Modules:
  0.0 479.1 jit_solution(8449218463262072227)
XLA Ops:
  10.7 5.8 %copy.82 = bf16[768,2304]{0,1:T(8,128)(2,1)} copy(bf16[768,2304]{1,0:T(8,128)(2,1)} %param.17) | data formatting | bytes 7077888 | tf_op args[5]
  25.9 5.5 %multiply_sine_fusion = (f32[8,8,256]{1,2,0:T(8,128)}, f32[8,8,256]{1,2,0:T(8,128)}, f32[8,8,256]{1,2,0:T(8,128)S(1)}) fusion(f32[8]{0:T(128)S(1)} %copy-done.31, f32[8,256]{1,0:T(8,128)S(1)} %subtract_convert_fusion), kind=kLoop, calls=%fused_computation.27 | loop fusion | flops 32768 | bytes 204832 | tf_op jit(solution)/shard_map/sin | solution.py:778
  46.8 4.5 concatenate.74
  52.9 4.4 concatenate.75
  66.7 7.3 %collective-permute-done.8 = bf16[256,768]{1,0:T(8,128)(2,1)S(1)} collective-permute-done((bf16[256,768]{1,0:T(8,128)(2,1)}, bf16[256,768]{1,0:T(8,128)(2,1)S(1)}, u32[]{:S(2)}, u32[]{:S(2)}) %collective-permute-start.8) | collective-permute-done | bytes 393248 | tf_op jit(solution)/shard_map/ppermute | solution.py:576
  76.0 5.7 %collective-permute-done.1 = bf16[256,768]{1,0:T(8,128)(2,1)S(1)} collective-permute-done((bf16[256,768]{1,0:T(8,128)(2,1)}, bf16[256,768]{1,0:T(8,128)(2,1)S(1)}, u32[]{:S(2)}, u32[]{:S(2)}) %collective-permute-start.1) | collective-permute-done | bytes 393248 | tf_op jit(solution)/shard_map/ppermute | solution.py:576
  86.1 7.1 %project.2 = (bf16[8,256,768]{2,1,0:T(8,128)(2,1)}, bf16[8,3,256,128]{3,2,1,0:T(8,128)(2,1)}, bf16[8,3,256,128]{3,2,1,0:T(8,128)(2,1)}, bf16[8,3,128,256]{3,2,1,...) custom-call(s32[1]{0:T(128)} %constant.85.clone.1.scalars, ...), custom_call_target="tpu_custom_call" | custom-call | flops 1610612736 | bytes 9437184 | tf_op jit(solution)/shard_map/project/pallas_call | solution.py:108
  103.9 7.0 %project.3 = (bf16[8,256,768]{2,1,0:T(8,128)(2,1)}, bf16[8,3,256,128]{3,2,1,0:T(8,128)(2,1)}, bf16[8,3,256,128]{3,2,1,0:T(8,128)(2,1)}, bf16[8,3,128,256]{3,2,1,...) custom-call(s32[1]{0:T(128)} %constant.85.clone.1.scalars, ...), custom_call_target="tpu_custom_call", output_to_operand_aliasing={{0}: (7, {}), {1}: (8, {}), {2}: (9, {}), {3}: (10, {}), {4... | custom-call | flops 1610612736 | bytes 9437184 | tf_op jit(solution)/shard_map/project/pallas_call | solution.py:108
  110.9 15.7 %feed.2 = (f32[8,256,768]{2,1,0:T(8,128)}, f32[8,256,768]{2,1,0:T(8,128)}, f32[768,768]{1,0:T(8,128)}, f32[768,768]{1,0:T(8,128)}) custom-call(s32[3]{0:T(128)} %pad_add_fusion.where, bf16[8,256,768]{2,1,0:T(8,128)(2,1)} %get-tuple-element.74.normed_ref, bf16[4,256,768]{2,1,0:T(8,128)(2,1)} %pad_maximum_fusion.4.cot_ref, bf16[768,3072]{1,0:T(8,128)(2,1)} %up_ref.3, ...), custom_call_target="tpu_custom_call" | custom-call | flops 7247757312 | bytes 11796480 | tf_op jit(solution)/shard_map/feed/pallas_call | solution.py:300
  128.9 17.1 %feed.3 = (f32[8,256,768]{2,1,0:T(8,128)}, f32[8,256,768]{2,1,0:T(8,128)}, bf16[2,2,96,768]{3,2,1,0:T(8,128)(2,1)}, bf16[2,2,96,768]{3,2,1,0:T(8,128)(2,1)}, bf1...) custom-call(s32[3]{0:T(128)} %pad_add_fusion.where, ...), custom_call_target="tpu_custom_call", output_to_operand_aliasing={{0}: (5, {}), {1}: (6, {})} | custom-call | flops 7247757312 | bytes 11796480 | tf_op jit(solution)/shard_map/feed/pallas_call | solution.py:300
  146.0 39.6 %attend.1 = (bf16[8,192,256]{2,1,0:T(8,128)(2,1)}, f32[8,192,256]{2,1,0:T(8,128)}, f32[8,8,256]{2,1,0:T(8,128)}) custom-call(s32[8]{0:T(128)} %get-tuple-element.169.a.d, s32[8]{0:T(128)} %get-tuple-element.125.b, s32[8]{0:T(128)} %get-tuple-element.124.c, s32[8]{0:T(128)} %select_reduce_fusion.1.d, bf16[8,3,256,128]{3,2,1,0:T(8,128)(2,1)} %get-tuple-element.69.refs_0_, ...), custom_call_target="tpu_custom_call" | custom-call | flops 3607772416 | bytes 25165824 | tf_op jit(solution)/shard_map/attend/pallas_call | solution.py:191
  187.3 11.3 %mix.1 = (bf16[8,256,768]{2,1,0:T(8,128)(2,1)}, bf16[8,256,256]{2,1,0:T(8,128)(2,1)}, f32[8,8,256]{2,1,0:T(8,128)}, f32[192,768]{1,0:T(8,128)}) custom-call(s32[3]{0:T(128)} %pad_add_fusion.where, bf16[8,192,256]{2,1,0:T(8,128)(2,1)} %get-tuple-element.72.att_ref, f32[8,192,256]{2,1,0:T(8,128)} %get-tuple-element.73.attf_ref, ...), custom_call_target="tpu_custom_call" | custom-call | flops 2415919104 | bytes 15728640 | tf_op jit(solution)/shard_map/mix/pallas_call | solution.py:356
  198.7 44.6 %attend_back.1 = (bf16[8,256,256]{2,1,0:T(8,128)(2,1)}, bf16[8,256,256]{2,1,0:T(8,128)(2,1)}, bf16[8,256,256]{2,1,0:T(8,128)(2,1)}) custom-call(s32[8]{0:T(128)} %get-tuple-element.169.a.d, s32[8]{0:T(128)} %get-tuple-element.125.b, s32[8]{0:T(128)} %get-tuple-element.124.c, s32[8]{0:T(128)} %get-tuple-element.169.a.d, ...), custom_call_target="tpu_custom_call" | custom-call | flops 10823317504 | bytes 15728640 | tf_op jit(solution)/shard_map/attend_back/pallas_call | solution.py:482
  244.2 15.6 %join.1 = (bf16[8,256,768]{2,1,0:T(8,128)(2,1)}, bf16[2,1,112,768]{3,2,1,0:T(8,128)(2,1)}, bf16[2,1,112,768]{3,2,1,0:T(8,128)(2,1)}, bf16[2,1,112,768]{3,2,1,0:T(8,128)(2,1)}, bf16[2,1,112,768]{3,2,1,0:T(8,128)(2,1)}) custom-call(s32[3]{0:T(128)} %pad_add_fusion.where, bf16[8,256,256]{2,1,0:T(8,128)(2,1)} %get-tuple-element.86.jq_ref, ...), custom_call_target="tpu_custom_call" | custom-call | flops 4831838208 | bytes 22020096 | tf_op jit(solution)/shard_map/join/pallas_call | solution.py:555
  266.2 4.7 collective-permute-done.18
  274.2 14.0 %collective-permute-done.19 = bf16[1,112,768]{2,1,0:T(8,128)(2,1)S(1)} collective-permute-done((bf16[1,112,768]{2,1,0:T(8,128)(2,1)S(1)}, bf16[1,112,768]{2,1,0:T(8,128)(2,1)S(1)}, u32[]{:S(2)}, u32[]{:S(2)}) %collective-permute-start.19) | collective-permute-done | bytes 172064 | tf_op jit(solution)/shard_map/ppermute | solution.py:576
  288.7 5.3 %collective-permute-done.21 = bf16[1,112,768]{2,1,0:T(8,128)(2,1)S(1)} collective-permute-done((bf16[1,112,768]{2,1,0:T(8,128)(2,1)S(1)}, bf16[1,112,768]{2,1,0:T(8,128)(2,1)S(1)}, u32[]{:S(2)}, u32[]{:S(2)}) %collective-permute-start.21) | collective-permute-done | bytes 172064 | tf_op jit(solution)/shard_map/ppermute | solution.py:576
  299.2 11.6 %collective-permute-done.22 = bf16[2,1,112,768]{3,2,0,1:T(8,128)(2,1)S(1)} collective-permute-done((bf16[2,1,112,768]{3,2,0,1:T(8,128)(2,1)S(1)}, bf16[2,1,112,768]{3,2,0,1:T(8,128)(2,1)S(1)}, u32[]{:S(2)}, u32[]{:S(2)}) %collective-permute-start.22) | collective-permute-done | bytes 344096 | tf_op jit(solution)/shard_map/ppermute | solution.py:576
  315.4 11.3 %collective-permute-done.23 = bf16[2,1,112,768]{3,2,0,1:T(8,128)(2,1)S(1)} collective-permute-done((bf16[2,1,112,768]{3,2,0,1:T(8,128)(2,1)S(1)}, bf16[2,1,112,768]{3,2,0,1:T(8,128)(2,1)S(1)}, u32[]{:S(2)}, u32[]{:S(2)}) %collective-permute-start.23) | collective-permute-done | bytes 344096 | tf_op jit(solution)/shard_map/ppermute | solution.py:576
  329.0 12.2 %collective-permute-done.36 = bf16[2,2,96,768]{3,2,1,0:T(8,128)(2,1)S(1)} collective-permute-done((bf16[2,2,96,768]{3,2,1,0:T(8,128)(2,1)S(1)}, bf16[2,2,96,768]{3,2,1,0:T(8,128)(2,1)S(1)}, u32[]{:S(2)}, u32[]{:S(2)}) %collective-permute-start.36) | collective-permute-done | bytes 589856 | tf_op jit(solution)/shard_map/ppermute | solution.py:576
  347.3 10.4 %collective-permute-done.37 = bf16[2,2,96,768]{3,2,1,0:T(8,128)(2,1)S(1)} collective-permute-done((bf16[2,2,96,768]{3,2,1,0:T(8,128)(2,1)S(1)}, bf16[2,2,96,768]{3,2,1,0:T(8,128)(2,1)S(1)}, u32[]{:S(2)}, u32[]{:S(2)}) %collective-permute-start.37) | collective-permute-done | bytes 589856 | tf_op jit(solution)/shard_map/ppermute | solution.py:576
  358.5 7.6 %collective-permute-done.11 = bf16[256,768]{1,0:T(8,128)(2,1)S(1)} collective-permute-done((bf16[256,768]{1,0:T(8,128)(2,1)S(1)}, bf16[256,768]{1,0:T(8,128)(2,1)S(1)}, u32[]{:S(2)}, u32[]{:S(2)}) %collective-permute-start.11) | collective-permute-done | bytes 393248 | tf_op jit(solution)/shard_map/ppermute | solution.py:576
  367.7 5.0 %collective-permute-done.15 = bf16[256,768]{1,0:T(8,128)(2,1)S(1)} collective-permute-done((bf16[256,768]{1,0:T(8,128)(2,1)S(1)}, bf16[256,768]{1,0:T(8,128)(2,1)S(1)}, u32[]{:S(2)}, u32[]{:S(2)}) %collective-permute-start.15) | collective-permute-done | bytes 393248 | tf_op jit(solution)/shard_map/ppermute | solution.py:576
  375.0 4.6 collective-permute-done.38
  385.4 5.0 %collective-permute-done.16 = bf16[256,768]{1,0:T(8,128)(2,1)S(1)} collective-permute-done((bf16[256,768]{1,0:T(8,128)(2,1)S(1)}, bf16[256,768]{1,0:T(8,128)(2,1)S(1)}, u32[]{:S(2)}, u32[]{:S(2)}) %collective-permute-start.16) | collective-permute-done | bytes 393248 | tf_op jit(solution)/shard_map/ppermute | solution.py:576
  394.3 27.7 %collective-permute-done.28.refs_3_ = bf16[2,2,1,112,768]{4,3,2,1,0:T(8,128)(2,1)} collective-permute-done((bf16[2,2,1,112,768]{4,3,2,1,0:T(8,128)(2,1)S(1)}, bf16[2,2,1,112,768]{4,3,2,1,0:T(8,128)(2,1)}, u32[]{:S(2)}, u32[]{:S(2)}) %collective-permute-start.28) | collective-permute-done | bytes 688160 | tf_op jit(solution)/shard_map/ppermute | solution.py:576
  423.2 5.5 %collective-permute-done.17 = bf16[256,768]{1,0:T(8,128)(2,1)S(1)} collective-permute-done((bf16[256,768]{1,0:T(8,128)(2,1)S(1)}, bf16[256,768]{1,0:T(8,128)(2,1)S(1)}, u32[]{:S(2)}, u32[]{:S(2)}) %collective-permute-start.17) | collective-permute-done | bytes 393248 | tf_op jit(solution)/shard_map/ppermute | solution.py:576
  433.0 4.3 fill.8
  437.3 4.3 fill.9
  441.6 9.5 %tail.1 = (f32[768,2304]{1,0:T(8,128)}, f32[768,768]{1,0:T(8,128)}) custom-call(s32[64]{0:T(128)} %concatenate.83.tabs, bf16[2,2,1,112,768]{4,3,2,1,0:T(8,128)(2,1)} %get-tuple-element.155.refs_0_, bf16[2,2,1,112,768]{4,3,2,1,0:T(8,128)(2,1)} %copy-done.11, bf16[2,2,1,112,768]{4,3,2,1,0:T(8,128)(2,1)} %bitcast.201, ...), custom_call_target="tpu_custom_call" | custom-call | bytes 14155776 | tf_op jit(solution)/shard_map/tail/pallas_call | solution.py:684
  459.7 4.3 fill.12
  464.0 4.3 fill.13
  (262 shorter events, 134.9 us)
Async XLA Ops:
  2.8 59.1 %collective-permute-start.7 = (bf16[256,768]{1,0:T(8,128)(2,1)}, bf16[256,768]{1,0:T(8,128)(2,1)}, u32[]{:S(2)}, u32[]{:S(2)}) collective-permute-start(bf16[256,768]{1,0:T(8,128)(2,1)} %get-tuple-element.148), channel_id=1, source_target_pairs={{0,4},{1,5},{2,6},{3,7},{4,0},{5,1},{6,2},{7,3},{8,12},{9,13},{10,... | collective-permute-start | bytes 1179656 | tf_op jit(solution)/shard_map/ppermute | solution.py:576
  6.9 52.6 %collective-permute-start.5 = (bf16[256,768]{1,0:T(8,128)(2,1)S(1)}, bf16[256,768]{1,0:T(8,128)(2,1)}, u32[]{:S(2)}, u32[]{:S(2)}) collective-permute-start(bf16[256,768]{1,0:T(8,128)(2,1)S(1)} %bitcast.194), channel_id=1, source_target_pairs={{0,2},{1,3},{2,0},{3,1},{4,6},{5,7},{6,4},{7,5},{8,10},{9,11},{10,... | collective-permute-start | bytes 1179656 | tf_op jit(solution)/shard_map/ppermute | solution.py:576
  9.5 54.3 %collective-permute-start = (bf16[256,768]{1,0:T(8,128)(2,1)}, bf16[256,768]{1,0:T(8,128)(2,1)}, u32[]{:S(2)}, u32[]{:S(2)}) collective-permute-start(bf16[256,768]{1,0:T(8,128)(2,1)} %get-tuple-element.149), channel_id=1, source_target_pairs={{0,4},{1,5},{2,6},{3,7},{4,0},{5,1},{6,2},{7,3},{8,12},{9,13},{10,... | collective-permute-start | bytes 1179656 | tf_op jit(solution)/shard_map/ppermute | solution.py:576
  9.8 48.2 %collective-permute-start.3 = (bf16[256,768]{1,0:T(8,128)(2,1)}, bf16[256,768]{1,0:T(8,128)(2,1)}, u32[]{:S(2)}, u32[]{:S(2)}) collective-permute-start(bf16[256,768]{1,0:T(8,128)(2,1)} %bitcast.19), channel_id=1, source_target_pairs={{0,2},{1,3},{2,0},{3,1},{4,6},{5,7},{6,4},{7,5},{8,10},{9,11},{10,... | collective-permute-start | bytes 1179656 | tf_op jit(solution)/shard_map/ppermute | solution.py:576
  59.4 24.3 %collective-permute-start.4 = (bf16[2,256,768]{2,1,0:T(8,128)(2,1)S(1)}, bf16[2,256,768]{2,1,0:T(8,128)(2,1)S(1)}, u32[]{:S(2)}, u32[]{:S(2)}) collective-permute-start(bf16[2,256,768]{2,1,0:T(8,128)(2,1)S(1)} %pad_maximum_fusion.13), channel_id=1, source_target_pairs={{0,1},{1,0},{2,3},{3,2},{4,5},{5,4},{6,7},{7,6},{8,9},{9,8},{10,11... | collective-permute-start | bytes 2359304 | tf_op jit(solution)/shard_map/ppermute | solution.py:576
  61.4 31.8 %collective-permute-start.6 = (bf16[2,256,768]{2,1,0:T(8,128)(2,1)}, bf16[2,256,768]{2,1,0:T(8,128)(2,1)}, u32[]{:S(2)}, u32[]{:S(2)}) collective-permute-start(bf16[2,256,768]{2,1,0:T(8,128)(2,1)} %pad_maximum_fusion.14), channel_id=1, source_target_pairs={{0,1},{1,0},{2,3},{3,2},{4,5},{5,4},{6,7},{7,6},{8,9},{9,8},{10,11... | collective-permute-start | bytes 2359304 | tf_op jit(solution)/shard_map/ppermute | solution.py:576
  63.8 17.9 %collective-permute-start.1 = (bf16[256,768]{1,0:T(8,128)(2,1)}, bf16[256,768]{1,0:T(8,128)(2,1)S(1)}, u32[]{:S(2)}, u32[]{:S(2)}) collective-permute-start(bf16[256,768]{1,0:T(8,128)(2,1)} %collective-permute-done), channel_id=1, source_target_pairs={{0,2},{1,3},{2,0},{3,1},{4,6},{5,7},{6,4},{7,5},{8,10},{9,11},{10,... | collective-permute-start | bytes 1179656 | tf_op jit(solution)/shard_map/ppermute | solution.py:576
  76.0 50.6 %collective-permute-start.9 = (bf16[2,256,768]{2,1,0:T(8,128)(2,1)}, bf16[2,256,768]{2,1,0:T(8,128)(2,1)S(1)}, u32[]{:S(2)}, u32[]{:S(2)}) collective-permute-start(bf16[2,256,768]{2,1,0:T(8,128)(2,1)} %pad_maximum_fusion.15), channel_id=1, source_target_pairs={{0,1},{1,0},{2,3},{3,2},{4,5},{5,4},{6,7},{7,6},{8,9},{9,8},{10,11... | collective-permute-start | bytes 2359304 | tf_op jit(solution)/shard_map/ppermute | solution.py:576
  83.7 17.9 %collective-permute-start.2 = (bf16[2,256,768]{2,1,0:T(8,128)(2,1)}, bf16[2,256,768]{2,1,0:T(8,128)(2,1)S(1)}, u32[]{:S(2)}, u32[]{:S(2)}) collective-permute-start(bf16[2,256,768]{2,1,0:T(8,128)(2,1)} %pad_maximum_fusion.12), channel_id=1, source_target_pairs={{0,1},{1,0},{2,3},{3,2},{4,5},{5,4},{6,7},{7,6},{8,9},{9,8},{10,11... | collective-permute-start | bytes 2359304 | tf_op jit(solution)/shard_map/ppermute | solution.py:576
  263.0 33.7 %collective-permute-start.32 = (bf16[2,2,96,768]{3,2,1,0:T(8,128)(2,1)S(1)}, bf16[2,2,96,768]{3,2,1,0:T(8,128)(2,1)S(1)}, u32[]{:S(2)}, u32[]{:S(2)}) collective-permute-start(bf16[2,2,96,768]{3,2,1,0:T(8,128)(2,1)S(1)} %copy-done.33), channel_id=1, source_target_pairs={{0,8},{8,0},{16,24},{24,16},{1,9},{9,1},{17,25},{25,17},{2,10},{10... | collective-permute-start | bytes 1769480 | tf_op jit(solution)/shard_map/ppermute | solution.py:576
  263.6 34.9 %collective-permute-start.34 = (bf16[2,2,96,768]{3,2,1,0:T(8,128)(2,1)S(1)}, bf16[2,2,96,768]{3,2,1,0:T(8,128)(2,1)S(1)}, u32[]{:S(2)}, u32[]{:S(2)}) collective-permute-start(bf16[2,2,96,768]{3,2,1,0:T(8,128)(2,1)S(1)} %copy-done.32), channel_id=1, source_target_pairs={{0,16},{8,24},{16,0},{24,8},{1,17},{9,25},{17,1},{25,9},{2,18},{10... | collective-permute-start | bytes 1769480 | tf_op jit(solution)/shard_map/ppermute | solution.py:576
  264.2 80.0 %collective-permute-start.10 = (bf16[4,256,768]{2,1,0:T(8,128)(2,1)S(1)}, bf16[4,256,768]{2,1,0:T(8,128)(2,1)S(1)}, u32[]{:S(2)}, u32[]{:S(2)}) collective-permute-start(bf16[4,256,768]{2,1,0:T(8,128)(2,1)S(1)} %pad_maximum_fusion.5), channel_id=1, source_target_pairs={{0,1},{1,0},{2,3},{3,2},{4,5},{5,4},{6,7},{7,6},{8,9},{9,8},{10,11... | collective-permute-start | bytes 4718600 | tf_op jit(solution)/shard_map/ppermute | solution.py:576
  270.9 75.8 %collective-permute-start.14 = (bf16[4,256,768]{2,1,0:T(8,128)(2,1)S(1)}, bf16[4,256,768]{2,1,0:T(8,128)(2,1)S(1)}, u32[]{:S(2)}, u32[]{:S(2)}) collective-permute-start(bf16[4,256,768]{2,1,0:T(8,128)(2,1)S(1)} %pad_maximum_fusion.6), channel_id=1, source_target_pairs={{0,1},{1,0},{2,3},{3,2},{4,5},{5,4},{6,7},{7,6},{8,9},{9,8},{10,11... | collective-permute-start | bytes 4718600 | tf_op jit(solution)/shard_map/ppermute | solution.py:576
  294.0 16.8 %collective-permute-start.22 = (bf16[2,1,112,768]{3,2,0,1:T(8,128)(2,1)S(1)}, bf16[2,1,112,768]{3,2,0,1:T(8,128)(2,1)S(1)}, u32[]{:S(2)}, u32[]{:S(2)}) collective-permute-start(bf16[2,1,112,768]{3,2,0,1:T(8,128)(2,1)S(1)} %pad_maximum_fusion.21), channel_id=1, source_target_pairs={{0,4},{1,5},{2,6},{3,7},{4,0},{5,1},{6,2},{7,3},{8,12},{9,13},{10,... | collective-permute-start | bytes 1032200 | tf_op jit(solution)/shard_map/ppermute | solution.py:576
  310.9 15.8 %collective-permute-start.23 = (bf16[2,1,112,768]{3,2,0,1:T(8,128)(2,1)S(1)}, bf16[2,1,112,768]{3,2,0,1:T(8,128)(2,1)S(1)}, u32[]{:S(2)}, u32[]{:S(2)}) collective-permute-start(bf16[2,1,112,768]{3,2,0,1:T(8,128)(2,1)S(1)} %add_convert_fusion.7), channel_id=1, source_target_pairs={{0,2},{1,3},{2,0},{3,1},{4,6},{5,7},{6,4},{7,5},{8,10},{9,11},{10,... | collective-permute-start | bytes 1032200 | tf_op jit(solution)/shard_map/ppermute | solution.py:576
  311.9 29.4 %collective-permute-start.36 = (bf16[2,2,96,768]{3,2,1,0:T(8,128)(2,1)S(1)}, bf16[2,2,96,768]{3,2,1,0:T(8,128)(2,1)S(1)}, u32[]{:S(2)}, u32[]{:S(2)}) collective-permute-start(bf16[2,2,96,768]{3,2,1,0:T(8,128)(2,1)S(1)} %pad_maximum_fusion.19), channel_id=1, source_target_pairs={{0,4},{1,5},{2,6},{3,7},{4,0},{5,1},{6,2},{7,3},{8,12},{9,13},{10,... | collective-permute-start | bytes 1769480 | tf_op jit(solution)/shard_map/ppermute | solution.py:576
  327.4 16.7 %collective-permute-start.26 = (bf16[2,1,112,768]{3,2,0,1:T(8,128)(2,1)S(1)}, bf16[2,1,112,768]{3,2,0,1:T(8,128)(2,1)S(1)}, u32[]{:S(2)}, u32[]{:S(2)}) collective-permute-start(bf16[2,1,112,768]{3,2,0,1:T(8,128)(2,1)S(1)} %get-tuple-element.153), channel_id=1, source_target_pairs={{0,16},{8,24},{16,0},{24,8},{1,17},{9,25},{17,1},{25,9},{2,18},{10... | collective-permute-start | bytes 1032200 | tf_op jit(solution)/shard_map/ppermute | solution.py:576
  341.4 16.3 %collective-permute-start.37 = (bf16[2,2,96,768]{3,2,1,0:T(8,128)(2,1)S(1)}, bf16[2,2,96,768]{3,2,1,0:T(8,128)(2,1)S(1)}, u32[]{:S(2)}, u32[]{:S(2)}) collective-permute-start(bf16[2,2,96,768]{3,2,1,0:T(8,128)(2,1)S(1)} %add_convert_fusion.4), channel_id=1, source_target_pairs={{0,2},{1,3},{2,0},{3,1},{4,6},{5,7},{6,4},{7,5},{8,10},{9,11},{10,... | collective-permute-start | bytes 1769480 | tf_op jit(solution)/shard_map/ppermute | solution.py:576
  342.6 48.6 %collective-permute-start.27 = (bf16[2,2,1,112,768]{4,3,1,2,0:T(8,128)(2,1)S(1)}, bf16[2,2,1,112,768]{4,3,1,2,0:T(8,128)(2,1)S(1)}, u32[]{:S(2)}, u32[]{:S(2)}) collective-permute-start(bf16[2,2,1,112,768]{4,3,1,2,0:T(8,128)(2,1)S(1)} %get-tuple-element.156), channel_id=1, source_target_pairs={{0,16},{8,24},{16,0},{24,8},{1,17},{9,25},{17,1},{25,9},{2,18},{10... | collective-permute-start | bytes 2064392 | tf_op jit(solution)/shard_map/ppermute | solution.py:576
  344.1 46.3 %collective-permute-start.25 = (bf16[2,2,1,112,768]{4,3,1,2,0:T(8,128)(2,1)S(1)}, bf16[2,2,1,112,768]{4,3,1,2,0:T(8,128)(2,1)S(1)}, u32[]{:S(2)}, u32[]{:S(2)}) collective-permute-start(bf16[2,2,1,112,768]{4,3,1,2,0:T(8,128)(2,1)S(1)} %get-tuple-element.156), channel_id=1, source_target_pairs={{0,1},{1,0},{2,3},{3,2},{4,5},{5,4},{6,7},{7,6},{8,9},{9,8},{10,11... | collective-permute-start | bytes 2064392 | tf_op jit(solution)/shard_map/ppermute | solution.py:576
  344.7 21.4 %collective-permute-start.11 = (bf16[256,768]{1,0:T(8,128)(2,1)S(1)}, bf16[256,768]{1,0:T(8,128)(2,1)S(1)}, u32[]{:S(2)}, u32[]{:S(2)}) collective-permute-start(bf16[256,768]{1,0:T(8,128)(2,1)S(1)} %slice_bitcast_fusion.6), channel_id=1, source_target_pairs={{0,2},{1,3},{2,0},{3,1},{4,6},{5,7},{6,4},{7,5},{8,10},{9,11},{10,... | collective-permute-start | bytes 1179656 | tf_op jit(solution)/shard_map/ppermute | solution.py:576
  347.2 25.5 %collective-permute-start.15 = (bf16[256,768]{1,0:T(8,128)(2,1)S(1)}, bf16[256,768]{1,0:T(8,128)(2,1)S(1)}, u32[]{:S(2)}, u32[]{:S(2)}) collective-permute-start(bf16[256,768]{1,0:T(8,128)(2,1)S(1)} %slice_bitcast_fusion.2), channel_id=1, source_target_pairs={{0,2},{1,3},{2,0},{3,1},{4,6},{5,7},{6,4},{7,5},{8,10},{9,11},{10,... | collective-permute-start | bytes 1179656 | tf_op jit(solution)/shard_map/ppermute | solution.py:576
  373.1 17.3 %collective-permute-start.16 = (bf16[256,768]{1,0:T(8,128)(2,1)S(1)}, bf16[256,768]{1,0:T(8,128)(2,1)S(1)}, u32[]{:S(2)}, u32[]{:S(2)}) collective-permute-start(bf16[256,768]{1,0:T(8,128)(2,1)S(1)} %slice_bitcast_fusion), channel_id=1, source_target_pairs={{0,2},{1,3},{2,0},{3,1},{4,6},{5,7},{6,4},{7,5},{8,10},{9,11},{10,... | collective-permute-start | bytes 1179656 | tf_op jit(solution)/shard_map/ppermute | solution.py:576
  379.6 49.0 %collective-permute-start.42 = (bf16[2,2,2,96,768]{4,3,2,1,0:T(8,128)(2,1)S(1)}, bf16[2,2,2,96,768]{4,3,2,1,0:T(8,128)(2,1)S(1)}, u32[]{:S(2)}, u32[]{:S(2)}) collective-permute-start(bf16[2,2,2,96,768]{4,3,2,1,0:T(8,128)(2,1)S(1)} %pad_maximum_fusion.11.src_ref), channel_id=1, source_target_pairs={{0,16},{8,24},{16,0},{24,8},{1,17},{9,25},{17,1},{25,9},{2,18},{10... | collective-permute-start | bytes 3538952 | tf_op jit(solution)/shard_map/ppermute | solution.py:576
  384.8 44.4 %collective-permute-start.39 = (bf16[2,2,2,96,768]{4,3,2,1,0:T(8,128)(2,1)S(1)}, bf16[2,2,2,96,768]{4,3,2,1,0:T(8,128)(2,1)S(1)}, u32[]{:S(2)}, u32[]{:S(2)}) collective-permute-start(bf16[2,2,2,96,768]{4,3,2,1,0:T(8,128)(2,1)S(1)} %pad_maximum_fusion.10.src_ref), channel_id=1, source_target_pairs={{0,8},{8,0},{16,24},{24,16},{1,9},{9,1},{17,25},{25,17},{2,10},{10... | collective-permute-start | bytes 3538952 | tf_op jit(solution)/shard_map/ppermute | solution.py:576
  390.4 31.6 %collective-permute-start.28 = (bf16[2,2,1,112,768]{4,3,2,1,0:T(8,128)(2,1)S(1)}, bf16[2,2,1,112,768]{4,3,2,1,0:T(8,128)(2,1)}, u32[]{:S(2)}, u32[]{:S(2)}) collective-permute-start(bf16[2,2,1,112,768]{4,3,2,1,0:T(8,128)(2,1)S(1)} %pad_maximum_fusion.17.refs_1_), channel_id=1, source_target_pairs={{0,8},{8,0},{16,24},{24,16},{1,9},{9,1},{17,25},{25,17},{2,10},{10... | collective-permute-start | bytes 2064392 | tf_op jit(solution)/shard_map/ppermute | solution.py:576
  391.2 31.5 %collective-permute-start.13 = (bf16[256,768]{1,0:T(8,128)(2,1)S(1)}, bf16[256,768]{1,0:T(8,128)(2,1)S(1)}, u32[]{:S(2)}, u32[]{:S(2)}) collective-permute-start(bf16[256,768]{1,0:T(8,128)(2,1)S(1)} %fusion.13), channel_id=1, source_target_pairs={{0,4},{1,5},{2,6},{3,7},{4,0},{5,1},{6,2},{7,3},{8,12},{9,13},{10,... | collective-permute-start | bytes 1179656 | tf_op jit(solution)/shard_map/ppermute | solution.py:576
  392.7 35.9 %collective-permute-start.17 = (bf16[256,768]{1,0:T(8,128)(2,1)S(1)}, bf16[256,768]{1,0:T(8,128)(2,1)S(1)}, u32[]{:S(2)}, u32[]{:S(2)}) collective-permute-start(bf16[256,768]{1,0:T(8,128)(2,1)S(1)} %fusion.11), channel_id=1, source_target_pairs={{0,4},{1,5},{2,6},{3,7},{4,0},{5,1},{6,2},{7,3},{8,12},{9,13},{10,... | collective-permute-start | bytes 1179656 | tf_op jit(solution)/shard_map/ppermute | solution.py:576
  422.7 37.1 %collective-permute-start.45 = (bf16[2,2,2,96,768]{4,3,2,1,0:T(8,128)(2,1)S(1)}, bf16[2,2,2,96,768]{4,3,2,1,0:T(8,128)(2,1)}, u32[]{:S(2)}, u32[]{:S(2)}) collective-permute-start(bf16[2,2,2,96,768]{4,3,2,1,0:T(8,128)(2,1)S(1)} %pad_maximum_fusion.11.src_ref), channel_id=1, source_target_pairs={{0,1},{1,0},{2,3},{3,2},{4,5},{5,4},{6,7},{7,6},{8,9},{9,8},{10,11... | collective-permute-start | bytes 3538952 | tf_op jit(solution)/shard_map/ppermute | solution.py:576
  428.6 35.4 %collective-permute-start.44 = (bf16[2,2,2,96,768]{4,3,2,1,0:T(8,128)(2,1)S(1)}, bf16[2,2,2,96,768]{4,3,2,1,0:T(8,128)(2,1)}, u32[]{:S(2)}, u32[]{:S(2)}) collective-permute-start(bf16[2,2,2,96,768]{4,3,2,1,0:T(8,128)(2,1)S(1)} %pad_maximum_fusion.10.src_ref), channel_id=1, source_target_pairs={{0,1},{1,0},{2,3},{3,2},{4,5},{5,4},{6,7},{7,6},{8,9},{9,8},{10,11... | collective-permute-start | bytes 3538952 | tf_op jit(solution)/shard_map/ppermute | solution.py:576
  428.7 39.7 %collective-permute-start.43 = (bf16[2,2,2,96,768]{4,3,2,1,0:T(8,128)(2,1)S(1)}, bf16[2,2,2,96,768]{4,3,2,1,0:T(8,128)(2,1)S(1)}, u32[]{:S(2)}, u32[]{:S(2)}) collective-permute-start(bf16[2,2,2,96,768]{4,3,2,1,0:T(8,128)(2,1)S(1)} %collective-permute-done.42.src_ref), channel_id=1, source_target_pairs={{0,1},{1,0},{2,3},{3,2},{4,5},{5,4},{6,7},{7,6},{8,9},{9,8},{10,11... | collective-permute-start | bytes 3538952 | tf_op jit(solution)/shard_map/ppermute | solution.py:576
  429.2 44.6 %collective-permute-start.40 = (bf16[2,2,2,96,768]{4,3,2,1,0:T(8,128)(2,1)S(1)}, bf16[2,2,2,96,768]{4,3,2,1,0:T(8,128)(2,1)S(1)}, u32[]{:S(2)}, u32[]{:S(2)}) collective-permute-start(bf16[2,2,2,96,768]{4,3,2,1,0:T(8,128)(2,1)S(1)} %collective-permute-done.39.src_ref), channel_id=1, source_target_pairs={{0,1},{1,0},{2,3},{3,2},{4,5},{5,4},{6,7},{7,6},{8,9},{9,8},{10,11... | collective-permute-start | bytes 3538952 | tf_op jit(solution)/shard_map/ppermute | solution.py:576
  (48 other events, 595.9 us)

commit v2 on v0

v2 whole, which is shorter than its diff:
```python
from functools import partial

import jax
import jax.numpy as jnp
from jax import lax
from jax.experimental import pallas as pl
from jax.experimental.pallas import tpu as pltpu
from jax.sharding import PartitionSpec as P

HEAD = 64
ROT = 16
TENSOR = 4
QUADS = 8
norm_eps = 1e-05
masked_score = -1e30
F32 = jnp.float32
BF16 = jnp.bfloat16
VMEM_LIMIT = 56 * 1024 * 1024
COST = 0.02
TAIL = "QUNSSDUQDSNUSQDQOSUNuQDSOdQON"

NN = (((1,), (0,)), ((), ()))
NT = (((1,), (1,)), ((), ()))
TN = (((0,), (0,)), ((), ()))

QUARTER, X_POS, Y_POS, PLACE, HALF, DOCS = range(6)


def mul(a, b, dims=NN):
    return lax.dot_general(a, b, dims, preferred_element_type=F32)


def sds(shape, dtype):
    return jax.ShapeDtypeStruct(tuple(shape), dtype)


def whole(shape):
    return pl.BlockSpec(tuple(shape), lambda *_: (0,) * len(shape))


def once(shape):
    return pl.BlockSpec(tuple(shape), lambda *_: (0,) * len(shape), pipeline_mode=pl.Buffered(1))


def rows_at(shape, base=0, count=1):
    zeros = (0,) * (len(shape) - 1)
    return pl.BlockSpec((count,) + tuple(shape[1:]), lambda i, s: (i + base,) + zeros)


def call(body, name, meta, grid, operands, in_specs, out_shapes, out_specs, flops, moved, special=0, scratch=(), aliases=None, after=()):
    after = list(after)
    n_in = len(operands)

    def kernel(meta_ref, *refs):
        body(meta_ref, *refs[:n_in], *refs[n_in + len(after) :])

    return pl.pallas_call(
        kernel,
        out_shape=out_shapes,
        grid_spec=pltpu.PrefetchScalarGridSpec(
            num_scalar_prefetch=1,
            grid=grid,
            in_specs=list(in_specs) + [pl.BlockSpec(memory_space=pl.ANY)] * len(after),
            out_specs=out_specs,
            scratch_shapes=list(scratch),
        ),
        input_output_aliases=aliases or {},
        compiler_params=pltpu.CompilerParams(
            dimension_semantics=("arbitrary",) * len(grid), vmem_limit_bytes=VMEM_LIMIT
        ),
        cost_estimate=pl.CostEstimate(flops=int(flops * COST), bytes_accessed=int(moved * COST), transcendentals=int(special * COST)),
        name=name,
    )(meta, *operands, *after)


def place_mask(j, n_blk):
    return (j // 4) * (n_blk // 2) + lax.rem(j, 2) * 2 + lax.rem(j // 2, 2)


def q_block(meta, j, n_blk):
    return jnp.bitwise_xor(meta[PLACE], place_mask(j, n_blk))


def k_block(meta, i, n_blk):
    return jnp.bitwise_xor(q_block(meta, lax.rem(i, QUADS), n_blk), (i // QUADS) * TENSOR)


def k_slot(meta, block, n_blk):
    r = jnp.bitwise_xor(meta[PLACE], block)
    low = lax.rem(r, TENSOR)
    split = lax.rem(r, n_blk // 2) // TENSOR
    return split * QUADS + (r // (n_blk // 2)) * 4 + lax.rem(low, 2) * 2 + low // 2


def doc_start(meta, index, n_docs):
    start = jnp.zeros_like(index)
    for d in range(n_docs):
        first = meta[DOCS + d]
        start = jnp.where(index >= first, first, start)
    return start


def token_index(block, rows):
    return block * rows + lax.broadcasted_iota(jnp.int32, (1, rows), 1)


def angles(meta, block, rows, n_docs):
    index = token_index(block, rows)
    position = (index - doc_start(meta, index, n_docs)).astype(F32)
    order = lax.broadcasted_iota(jnp.int32, (ROT // 2, 1), 0)
    frequency = jnp.ones((ROT // 2, 1), F32)
    for i in range(1, ROT // 2):
        frequency = jnp.where(order == i, 10000.0 ** (-2.0 * i / ROT), frequency)
    phases = position * frequency
    return jnp.cos(phases), jnp.sin(phases)


def turned(head, cos, sin):
    a, b = head[: ROT // 2], head[ROT // 2 : ROT]
    return jnp.concatenate([a * cos - b * sin, b * cos + a * sin, head[ROT:]], axis=0)


def cut_kernel(wide, meta, *refs):
    srcs, out_ref, hold_ref = refs[:3], refs[3], refs[4]
    first = pl.multiple_of(lax.rem(meta[QUARTER], 2) * wide, 16)
    for third in range(3):
        hold_ref[...] = srcs[third][...].astype(F32).T
        out_ref[third * wide : (third + 1) * wide, :] = hold_ref[pl.ds(first, wide), :].astype(BF16)


def cut(meta, w_qkv, wide):
    width = w_qkv.shape[0]
    per = w_qkv.shape[1] // 3 // (2 * wide)

    def spec(third):
        return pl.BlockSpec((width, 2 * wide), lambda i, s: (0, third * per + s[QUARTER] // 2))

    return call(
        partial(cut_kernel, wide),
        "cut",
        meta,
        (1,),
        [w_qkv] * 3,
        [spec(third) for third in range(3)],
        sds((3 * wide, width), BF16),
        whole((3 * wide, width)),
        0,
        18 * wide * width,
        scratch=[pltpu.VMEM((2 * wide, width), F32)],
    )


def pick_kernel(meta, src_ref, out_ref):
    out_ref[...] = src_ref[0]


def pick(meta, array, other, after=()):
    _, rows, width = array.shape
    return call(
        pick_kernel,
        "pick",
        meta,
        (1,),
        [array],
        [pl.BlockSpec((1, rows, width), lambda i, s: ((1 - s[HALF]) if other else s[HALF], 0, 0))],
        sds((rows, width), array.dtype),
        whole((rows, width)),
        0,
        4 * rows * width,
        after=after,
    )


def project_kernel(n_heads, n_blk, n_docs, base, meta, *refs):
    pieces, (gain_ref, bias_ref, w_ref) = refs[:4], refs[4:7]
    x_ref, normed_ref, q_ref, k_ref, v_ref, kn_ref, vn_ref = refs[-7:]
    i = pl.program_id(0)
    rows = x_ref.shape[1]
    wide = n_heads * HEAD
    for k in range(4):

        @pl.when(i == k // 2)
        def _():
            x_ref[k % 2] = pieces[k][...]

    for b in range(2):
        x = x_ref[b].astype(F32)
        mean = jnp.mean(x, axis=1, keepdims=True)
        centred = x - mean
        inverse = lax.rsqrt(jnp.mean(centred * centred, axis=1, keepdims=True) + norm_eps)
        normed_ref[b] = (centred * inverse * gain_ref[...] + bias_ref[...]).astype(BF16)
    flats = [mul(w_ref[...], normed_ref[b], NT) for b in range(2)]
    for b in range(2):
        flat = flats[b]
        cos, sin = angles(meta, q_block(meta, 2 * i + b + base, n_blk), rows, n_docs)
        for h in range(n_heads):
            at = slice(h * HEAD, (h + 1) * HEAD)
            q_ref[b, at] = (turned(flat[at], cos, sin) * HEAD**-0.5).astype(BF16)
            key = turned(flat[wide + h * HEAD : wide + (h + 1) * HEAD], cos, sin)
            k_ref[b, at] = key.astype(BF16)
            kn_ref[b, h] = key.T.astype(BF16)
            value = flat[2 * wide + h * HEAD : 2 * wide + (h + 1) * HEAD]
            v_ref[b, at] = value.astype(BF16)
            vn_ref[b, h] = value.T.astype(BF16)


def project(meta, pieces, base, total, gain, bias, w_cut, n_blk, n_docs, earlier, after=()):
    rows, width = pieces[0].shape
    wide = w_cut.shape[0] // 3
    n_heads = wide // HEAD
    outs = [
        sds((total, rows, width), BF16),
        sds((total, rows, width), BF16),
        sds((total, wide, rows), BF16),
        sds((total, wide, rows), BF16),
        sds((total, wide, rows), BF16),
        sds((total, n_heads, rows, HEAD), BF16),
        sds((total, n_heads, rows, HEAD), BF16),
    ]
    operands = list(pieces) + [gain, bias, w_cut]
    specs = [whole(o.shape) for o in operands]
    aliases = {}
    if earlier is not None:
        aliases = {1 + len(operands) + k: k for k in range(len(outs))}
        operands += list(earlier)
        specs += [pl.BlockSpec(memory_space=pl.ANY)] * len(outs)
    return call(
        partial(project_kernel, n_heads, n_blk, n_docs, base),
        "project",
        meta,
        (2,),
        operands,
        specs,
        outs,
        [rows_at(o.shape, base // 2, 2) for o in outs],
        8 * rows * width * 3 * wide,
        4 * rows * width * 10,
        aliases=aliases,
        after=after,
    )


def list_pairs(meta, base, count, rows, n_blk, n_docs, q_list, k_list):
    def of_block(j, found):
        block = q_block(meta, base + j, n_blk)
        first = doc_start(meta, block * rows, n_docs) // rows

        def put(kb, at):
            q_list[at] = j
            k_list[at] = kb
            return at + 1

        return lax.fori_loop(first, block + 1, put, found)

    return lax.fori_loop(0, count, of_block, jnp.int32(0))


def seen(meta, kb, block, rows, n_docs):
    index = token_index(block, rows)
    k_index = kb * rows + lax.broadcasted_iota(jnp.int32, (rows, rows), 0)
    return (k_index >= doc_start(meta, index, n_docs)) & (k_index <= index)


def attend_kernel(n_heads, n_blk, n_docs, meta, q_ref, kn_ref, v_ref, att_ref, attf_ref, lse_ref, s_ref, acc_ref, top_ref, sum_ref, q_list, k_list):
    count, _, rows = q_ref.shape
    heads = range(n_heads)
    base = pl.program_id(0) * count
    found = list_pairs(meta, base, count, rows, n_blk, n_docs, q_list, k_list)
    q_list[found] = count
    k_list[found] = 0
    steps = (found + 1) // 2
    top_ref[...] = jnp.full_like(top_ref, masked_score)
    sum_ref[...] = jnp.zeros_like(sum_ref)
    acc_ref[...] = jnp.zeros_like(acc_ref)

    def fold(tile, how):
        return how(tile.reshape(rows // 8, 8, rows), axis=0)

    def score(n, _):
        for at in (2 * n, 2 * n + 1):
            j, kb = q_list[at], k_list[at]
            jq = jnp.minimum(j, count - 1)
            ka = k_slot(meta, kb, n_blk)
            allowed = seen(meta, kb, q_block(meta, base + jq, n_blk), rows, n_docs)
            scores = [mul(kn_ref[ka, h], q_ref[jq, h * HEAD : (h + 1) * HEAD]) for h in heads]
            for h in heads:
                s = jnp.where(allowed, scores[h], masked_score)
                s_ref[at, h] = s
                top_ref[j, h] = jnp.maximum(top_ref[j, h], fold(s, jnp.max))
        return 0

    lax.fori_loop(0, steps, score, 0)

    def settle(j, _):
        for h in heads:
            top_ref[j, h, 0:1] = jnp.max(top_ref[j, h], axis=0, keepdims=True)
        return 0

    lax.fori_loop(0, count + 1, settle, 0)

    def weigh(n, _):
        both = (2 * n, 2 * n + 1)
        weights = []
        for at in both:
            j = q_list[at]
            for h in heads:
                p = jnp.exp(s_ref[at, h] - top_ref[j, h, 0:1])
                sum_ref[j, h] += fold(p, jnp.sum)
                weights.append(p.astype(BF16))
        for m, at in enumerate(both):
            j, ka = q_list[at], k_slot(meta, k_list[at], n_blk)
            for h in heads:
                acc_ref[j, h] += mul(v_ref[ka, h * HEAD : (h + 1) * HEAD], weights[m * n_heads + h])
        return 0

    lax.fori_loop(0, steps, weigh, 0)
    lse_ref[...] = jnp.zeros_like(lse_ref)

    def finish(j, _):
        for h in heads:
            at = slice(h * HEAD, (h + 1) * HEAD)
            total = jnp.sum(sum_ref[j, h], axis=0, keepdims=True)
            out = acc_ref[j, h] / total
            attf_ref[j, at] = out
            att_ref[j, at] = out.astype(BF16)
            lse_ref[j, h : h + 1] = top_ref[j, h, 0:1] + jnp.log(total)
        return 0

    lax.fori_loop(0, count, finish, 0)


def attend(meta, q, kn, v, n_blk, n_docs, after=()):
    n, wide, rows = q.shape
    n_k, n_heads = kn.shape[:2]
    pairs = 0.56 * n * n_k
    count = n if n_k == n else 1
    most = (n * (n + 1) // 2 if n_k == n else n_k) + 2
    outs = [sds((n, wide, rows), BF16), sds((n, wide, rows), F32), sds((n, 8, rows), F32)]

    def some(shape):
        zeros = (0,) * (len(shape) - 1)
        return pl.BlockSpec((count,) + tuple(shape[1:]), lambda i, s: (i,) + zeros)

    return call(
        partial(attend_kernel, n_heads, n_blk, n_docs),
        "attend",
        meta,
        (n // count,),
        [q, kn, v],
        [some(q.shape), once(kn.shape), once(v.shape)],
        outs,
        [some(o.shape) for o in outs],
        pairs * n_heads * rows * rows * 256 * 2,
        16 * n * rows * wide,
        pairs * n_heads * rows * rows,
        scratch=[
            pltpu.VMEM((most, n_heads, rows, rows), F32),
            pltpu.VMEM((count + 1, n_heads, HEAD, rows), F32),
            pltpu.VMEM((count + 1, n_heads, 8, rows), F32),
            pltpu.VMEM((count + 1, n_heads, 8, rows), F32),
            pltpu.SMEM((most,), jnp.int32),
            pltpu.SMEM((most,), jnp.int32),
        ],
        after=after,
    )


def gelu_pair(hidden):
    bell = jnp.exp(hidden * hidden * -0.5)
    t = 1.0 / (1.0 + (0.3275911 * 0.5**0.5) * jnp.abs(hidden))
    tail = ((((0.5 * 1.061405429 * t - 0.5 * 1.453152027) * t + 0.5 * 1.421413741) * t - 0.5 * 0.284496736) * t + 0.5 * 0.254829592) * t * bell
    cdf = jnp.where(hidden >= 0, 1.0 - tail, tail)
    return hidden * cdf, cdf + hidden * bell * 0.3989422804014327


def put_pieces(scratch, meta, outs, slot):
    rows = scratch.shape[0] // 4
    for k, out in enumerate(outs):
        cx, cy = jnp.bitwise_xor(meta[X_POS], k % 2), jnp.bitwise_xor(meta[Y_POS], k // 2)
        out[slot] = scratch[pl.ds(pl.multiple_of((cx * 2 + cy) * rows, 16), rows), :].astype(BF16)


def put_halves(scratch, meta, outs, slot):
    x, y = meta[X_POS], meta[Y_POS]
    rows = scratch.shape[0] // 8

    def part(cx, cy, b):
        return scratch[pl.ds(pl.multiple_of(((cx * 2 + cy) * 2 + b) * rows, 16), rows), :].astype(BF16)

    for other in range(2):
        cx, cy = jnp.bitwise_xor(x, other), jnp.bitwise_xor(y, other)
        outs[0][other, slot] = part(1 - x, cy, 0)
        outs[1][other, slot] = part(x, cy, 0)
        outs[2][other, slot] = part(cx, 1 - y, 1)
        outs[3][other, slot] = part(cx, y, 1)


def feed_kernel(meta, *refs):
    pieces, (normed_ref, up_ref, down_ref), (cot_ref, mo_ref, ng_ref), outs, (gup_ref, gdn_ref) = (
        refs[:QUADS],
        refs[QUADS : QUADS + 3],
        refs[QUADS + 3 : QUADS + 6],
        refs[QUADS + 6 : -2],
        refs[-2:],
    )
    i = pl.program_id(0)
    rows, width = pieces[0].shape
    for k in range(QUADS):

        @pl.when(i == k // 2)
        def _():
            cot_ref[k % 2] = pieces[k][...]

    @pl.when(i == 0)
    def _():
        gup_ref[...] = jnp.zeros_like(gup_ref)
        gdn_ref[...] = jnp.zeros_like(gdn_ref)

    normed = normed_ref[...].reshape(2 * rows, width)
    cot = cot_ref[...].reshape(2 * rows, width)
    inner = up_ref.shape[1]
    chunk = inner // 3 if inner % 768 == 0 else inner
    spans = [slice(c, c + chunk) for c in range(0, inner, chunk)]

    def open_up(at):
        return mul(normed, up_ref[:, at]), mul(cot, down_ref[at, :], NT)

    opened = [open_up(at) for at in spans[:2]]
    mo = ng = None
    for c, at in enumerate(spans):
        hidden, active_grad = opened[c]
        active, slope = gelu_pair(hidden)
        active = active.astype(BF16)
        hidden_grad = (active_grad * slope).astype(BF16)
        if c + 2 < len(spans):
            opened.append(open_up(spans[c + 2]))
        part, back = mul(active, down_ref[at, :]), mul(hidden_grad, up_ref[:, at], NT)
        mo, ng = (part, back) if c == 0 else (mo + part, ng + back)
        gdn_ref[at, :] += mul(active, cot, TN)
        gup_ref[:, at] += mul(normed, hidden_grad, TN)
    mo_ref[...] = mo.astype(BF16).reshape(2, rows, width)
    ng_ref[...] = ng.astype(BF16).reshape(2, rows, width)

    @pl.when(i == QUADS // 2 - 1)
    def _():
        put_halves(gup_ref, meta, outs, 0)
        put_halves(gdn_ref, meta, outs, 1)


def feed(meta, normed, pieces, w_up, w_down, after=()):
    rows, width = pieces[0].shape
    inner = w_up.shape[1] // TENSOR
    two = rows_at(normed.shape, 0, 2)
    piece = sds((2, 2, inner // 8, width), BF16)
    return call(
        feed_kernel,
        "feed",
        meta,
        (QUADS // 2,),
        list(pieces) + [normed, w_up, w_down],
        [whole(p.shape) for p in pieces]
        + [
            two,
            pl.BlockSpec((width, inner), lambda i, s: (0, s[QUARTER])),
            pl.BlockSpec((inner, width), lambda i, s: (s[QUARTER], 0)),
        ],
        [sds(normed.shape, BF16)] * 3 + [piece] * 4,
        [two] * 3 + [whole(piece.shape)] * 4,
        12 * QUADS * rows * width * inner,
        8 * QUADS * rows * width + 8 * width * inner,
        scratch=[pltpu.VMEM((width, inner), F32), pltpu.VMEM((inner, width), F32)],
        after=after,
    )


def mix_kernel(n_heads, meta, att_ref, attf_ref, cot_ref, mo_ref, w_ref, out_ref, do_ref, delta_ref, go_ref):
    i = pl.program_id(0)
    w = w_ref[...]
    both = range(2)
    grads = [mul(w, cot_ref[b], NT).astype(BF16) for b in both]
    outs = [mul(att_ref[b], w, TN) for b in both]
    go = mul(att_ref[0], cot_ref[0]) + mul(att_ref[1], cot_ref[1])
    delta_ref[...] = jnp.zeros_like(delta_ref)
    for b in both:
        out_ref[b] = (mo_ref[b].astype(F32) + outs[b]).astype(BF16)
        do_ref[b] = grads[b]
        product = grads[b].astype(F32) * attf_ref[b]
        for h in range(n_heads):
            delta_ref[b, h : h + 1] = jnp.sum(product[h * HEAD : (h + 1) * HEAD], axis=0, keepdims=True)

    @pl.when(i == 0)
    def _():
        go_ref[...] = go

    @pl.when(i > 0)
    def _():
        go_ref[...] += go


def mix(meta, att, attf, cot, mo, w_out, after=()):
    n, rows, width = cot.shape
    wide = att.shape[1]
    outs = [
        sds((n, rows, width), BF16),
        sds((n, wide, rows), BF16),
        sds((n, 8, rows), F32),
        sds((wide, width), F32),
    ]
    return call(
        partial(mix_kernel, wide // HEAD),
        "mix",
        meta,
        (n // 2,),
        [att, attf, cot, mo, w_out],
        [rows_at(a.shape, 0, 2) for a in (att, attf, cot, mo)]
        + [pl.BlockSpec((wide, width), lambda i, s: (s[QUARTER], 0))],
        outs,
        [rows_at(o.shape, 0, 2) for o in outs[:3]] + [whole((wide, width))],
        6 * n * rows * width * wide,
        10 * n * rows * width,
        after=after,
    )


def back_kernel(heads, n_blk, n_docs, n_q, n_k, meta, q_ref, do_ref, lse_ref, delta_ref, kn_ref, vn_ref, k_ref, *refs):
    rest, (dq_ref, dk_ref, dv_ref, p_ref, ds_ref, q_list, k_list) = refs[:-7], refs[-7:]
    if len(rest) > 3:
        joins, (jq_ref, jk_ref, jv_ref) = rest[:-3], rest[-3:]
    else:
        joins, (jq_ref, jk_ref, jv_ref) = (), rest
    rows = k_ref.shape[2]
    spots = [slice(h * HEAD, (h + 1) * HEAD) for h in heads]
    dq_ref[...] = jnp.zeros_like(dq_ref)
    dk_ref[...] = jnp.zeros_like(dk_ref)
    dv_ref[...] = jnp.zeros_like(dv_ref)
    found = list_pairs(meta, 0, n_q, rows, n_blk, n_docs, q_list, k_list)

    q_list[found] = n_q - 1
    k_list[found] = q_block(meta, n_q - 1, n_blk) + 1

    def parts(n):
        for at in (2 * n, 2 * n + 1):
            j, ka = q_list[at], k_slot(meta, jnp.minimum(k_list[at], n_k - 1), n_blk)
            for m, h in enumerate(heads):
                yield at, j, ka, m, h, spots[m]

    def weigh(n):
        slot = lax.rem(n, 2)
        allowed = [seen(meta, k_list[at], q_block(meta, q_list[at], n_blk), rows, n_docs) for at in (2 * n, 2 * n + 1)]
        scores = [mul(kn_ref[ka, h], q_ref[j, at]) for _, j, ka, _, h, at in parts(n)]
        grads = [mul(vn_ref[ka, h], do_ref[j, at]) for _, j, ka, _, h, at in parts(n)]
        for c, (_, j, ka, m, h, at) in enumerate(parts(n)):
            p = jnp.where(allowed[c // len(heads)], jnp.exp(scores[c] - lse_ref[j, h : h + 1]), 0.0)
            p_ref[slot, c] = p.astype(BF16)
            ds_ref[slot, c] = (p * (grads[c] - delta_ref[j, h : h + 1])).astype(BF16)

    def gather(n):
        slot = lax.rem(n, 2)
        for c, (_, j, ka, m, h, at) in enumerate(parts(n)):
            dv_ref[ka, m] += mul(do_ref[j, at], p_ref[slot, c], NT)
            dk_ref[ka, m] += mul(q_ref[j, at], ds_ref[slot, c], NT)
            dq_ref[j, m] += mul(k_ref[ka, at], ds_ref[slot, c])

    weigh(0)

    def both(n, _):
        gather(n - 1)
        weigh(n)
        return 0

    steps = (found + 1) // 2
    lax.fori_loop(1, steps, both, 0)
    gather(steps - 1)

    def finish_k(i, _):
        cos, sin = angles(meta, k_block(meta, i, n_blk), rows, n_docs)
        for n in range(len(heads)):
            at = slice(n * HEAD, (n + 1) * HEAD)
            jk_ref[i, at] = turned(dk_ref[i, n], cos, -sin).astype(BF16)
            jv_ref[i, at] = dv_ref[i, n].astype(BF16)
        return 0

    def finish_q(j, _):
        cos, sin = angles(meta, q_block(meta, j, n_blk), rows, n_docs)
        for n in range(len(heads)):
            jq_ref[j, n * HEAD : (n + 1) * HEAD] = (turned(dq_ref[j, n], cos, -sin) * HEAD**-0.5).astype(BF16)
        return 0

    lax.fori_loop(0, n_k, finish_k, 0)
    lax.fori_loop(0, n_q, finish_q, 0)
    if joins:
        join_kernel(meta, jq_ref, jk_ref, jv_ref, *joins)


def join_kernel(meta, jq_ref, jk_ref, jv_ref, normed_ref, x_ref, ngm_ref, w_ref, go_ref, ng_ref, sums_ref, *refs):
    outs, all_ref = refs[:4], refs[4]
    wide = go_ref.shape[0]
    for third, ref in enumerate((jq_ref, jk_ref, jv_ref)):
        total = mul(ref[0], normed_ref[0])
        for j in range(1, QUADS):
            total = total + mul(ref[j], normed_ref[j])
        all_ref[third * wide : (third + 1) * wide] = total
    all_ref[3 * wide :] = go_ref[...]
    put_pieces(all_ref, meta, outs, 0)
    sums_ref[...] = jnp.zeros_like(sums_ref)

    def block(n, _):
        for j in (2 * n, 2 * n + 1):
            joined = jnp.concatenate([jq_ref[j], jk_ref[j], jv_ref[j]], axis=0)
            ng = ngm_ref[j].astype(F32) + mul(joined, w_ref[...], TN)
            ng_ref[j] = ng.astype(BF16)
            x = x_ref[j].astype(F32)
            centred = x - jnp.mean(x, axis=1, keepdims=True)
            xhat = centred * lax.rsqrt(jnp.mean(centred * centred, axis=1, keepdims=True) + norm_eps)
            sums_ref[0:1] += jnp.sum(ng * xhat, axis=0, keepdims=True)
            sums_ref[1:2] += jnp.sum(ng, axis=0, keepdims=True)
        return 0

    lax.fori_loop(0, QUADS // 2, block, 0)


def join_parts(normed, x, ngm, w_cut, grad_out):
    wide, width = grad_out.shape
    results = [sds(x.shape, BF16), sds((8, width), F32)] + [sds((1, wide, width), BF16)] * 4
    return [normed, x, ngm, w_cut, grad_out], results, [pltpu.VMEM((4 * wide, width), F32)]


def join(meta, grads, *rest):
    operands, outs, scratch = join_parts(*rest)
    operands = list(grads) + operands
    return call(
        join_kernel,
        "join",
        meta,
        (1,),
        operands,
        [once(a.shape) for a in operands],
        outs,
        [once(o.shape) for o in outs],
        0,
        0,
        scratch=scratch,
    )


def attend_back(meta, q, do, lse, delta, kn, vn, k, n_blk, n_docs, rest):
    n_q, wide, rows = q.shape
    n_k = k.shape[0]
    n_heads = wide // HEAD
    pairs = 0.56 * n_q * n_k
    outs = [sds((n_q, wide, rows), BF16), sds((n_k, wide, rows), BF16), sds((n_k, wide, rows), BF16)]
    grads = [pltpu.VMEM(o.shape, BF16) for o in outs] if rest else []
    operands = [q, do, lse, delta, kn, vn, k]
    scratch = []
    if rest:
        more, outs, scratch = join_parts(*rest)
        operands += more

    def body(meta_ref, *refs):
        back_kernel(range(n_heads), n_blk, n_docs, n_q, n_k, meta_ref, *refs[: len(refs) - 7 - len(grads)], *refs[len(refs) - len(grads) :], *refs[len(refs) - 7 - len(grads) : len(refs) - len(grads)])

    return call(
        body,
        "attend_back",
        meta,
        (1,),
        operands,
        [once(a.shape) for a in operands],
        outs,
        [once(o.shape) for o in outs],
        pairs * n_heads * rows * rows * 256 * 2 * 2.5,
        16 * n_q * rows * wide,
        pairs * n_heads * rows * rows,
        scratch=scratch
        + [
            pltpu.VMEM((n_q, n_heads, HEAD, rows), F32),
            pltpu.VMEM((n_k, n_heads, HEAD, rows), F32),
            pltpu.VMEM((n_k, n_heads, HEAD, rows), F32),
            pltpu.VMEM((2, 2 * n_heads, rows, rows), BF16),
            pltpu.VMEM((2, 2 * n_heads, rows, rows), BF16),
            pltpu.SMEM((n_q * n_k + 2,), jnp.int32),
            pltpu.SMEM((n_q * n_k + 2,), jnp.int32),
        ]
        + grads,
    )


def swap(x, axis, size, mask):
    return lax.ppermute(x, axis, [(i, i ^ mask) for i in range(size)])


def add(a, b):
    return a.astype(F32) + b.astype(F32)


class Order:
    def __init__(self, sizes):
        self.sizes = sizes
        self.token = []

    def hold(self, arrays):
        arrays = list(arrays)
        held = lax.optimization_barrier(tuple(arrays) + tuple(self.token))
        return list(held[: len(arrays)])

    def done(self, results):
        self.token = jax.tree.leaves(results)[:1]
        return results

    def send(self, exchanges):
        if not isinstance(exchanges[0], tuple):
            return exchanges
        sent = self.hold([array for array, _, _ in exchanges])
        self.token = sent
        return [swap(a, axis, self.sizes[axis], mask) for a, (_, axis, mask) in zip(sent, exchanges)]

    def start(self, generator):
        return Steps(generator, self)

    def advance(self, *chains):
        for chain in chains:
            chain.advance()


class Steps:
    def __init__(self, generator, order):
        self.generator, self.order = generator, order
        self.held = order.send(next(generator))

    def advance(self):
        self.held = self.order.send(self.generator.send(self.order.hold(self.held)))

    def end(self):
        try:
            while True:
                self.advance()
        except StopIteration:
            return self.held


def reduce_pieces(parts):
    got = yield [(part, "dp", k + 1) for k, part in enumerate(parts[1:])]
    return [(add(parts[0], got[0]) + add(got[1], got[2])).astype(BF16)]


def reduce_halves(parts, n_blk):
    send_a, keep_a, send_b, keep_b = parts
    got_a, got_b = yield [(send_a, "dp", 1), (send_b, "dp", 2)]
    sum_a, sum_b = add(keep_a, got_a).astype(BF16), add(keep_b, got_b).astype(BF16)
    got_a, got_b = yield [(sum_a[1], "dp", 2), (sum_b[1], "dp", 1)]
    own = jnp.stack([add(sum_a[0], got_a), add(sum_b[0], got_b)]).astype(BF16)
    (got,) = yield [(own, "blk", n_blk // 2)]
    yield [add(own, got).astype(BF16)]


def sum_halves(own, n_blk):
    (got,) = yield [(own, "blk", n_blk // 2)]
    total = add(own, got).astype(BF16)
    yield from spread_pieces(total.reshape(2, -1, total.shape[1]))


def spread_pieces(total):
    (near,) = yield [(total, "blk", 2)]
    pair_a, pair_b = jnp.stack([total[0], near[0]]), jnp.stack([total[1], near[1]])
    got_a, got_b = yield [(pair_a, "dp", 1), (pair_b, "dp", 2)]
    two = [jnp.stack([pair_a, got_a]), jnp.stack([pair_b, got_b])]
    *far, twin_a, twin_b = yield [(two[0], "dp", 2), (two[1], "dp", 1)] + [(o, "blk", 1) for o in two]
    far_twins = yield [(o, "blk", 1) for o in far]
    yield two + far + [twin_a, twin_b] + far_twins


def placed(k, outer, meta, rows):
    b, far = k % 2, (k // 2) % 2
    cx = jnp.bitwise_xor(meta[X_POS], far if b else outer)
    cy = jnp.bitwise_xor(meta[Y_POS], outer if b else far)
    return ((cx * 2 + cy) * 2 + b) * rows


def fill_kernel(meta, *refs):
    srcs, out_ref = refs[:8], refs[8]
    rows = srcs[0].shape[2]
    for core in range(2):

        @pl.when(pl.program_id(0) // 2 == core)
        def _():
            for k in range(4):
                for outer in range(2):
                    at = pl.multiple_of(placed(k, outer, meta, rows), 16)
                    out_ref[pl.ds(at, rows), :] = srcs[k + 4 * core][outer, 0].astype(F32)


def fill(meta, arrays, shape):
    _, _, rows, width = arrays[0].shape
    across = shape[1] > shape[0]

    def at(i, s):
        shard = jnp.bitwise_xor(s[QUARTER], lax.rem(i, 2) * 2 + i // 2)
        return (0, shard) if across else (shard, 0)

    def source(k):
        return pl.BlockSpec((2, 1, rows, width), lambda i, s: (0, jnp.clip(i - 2 * (k // 4), 0, 1), 0, 0))

    return call(
        fill_kernel,
        "fill",
        meta,
        (TENSOR,),
        list(arrays),
        [source(k) for k in range(8)],
        sds(shape, F32),
        pl.BlockSpec((8 * rows, width), at),
        0,
        6 * 8 * 4 * rows * width,
    )


def tail_kernel(wide, meta, *refs):
    srcs, (gq_ref, go_ref, hold_ref) = refs[:8], refs[8:]
    rows = srcs[0].shape[2]
    i = pl.program_id(0)

    @pl.when(i == 0)
    def _():
        for k, src in enumerate(srcs):
            for outer in range(2):
                row = placed(k % 4, outer, meta, rows)
                for rt1 in range(2):
                    shard = jnp.bitwise_xor(meta[QUARTER], rt1 * 2 + k // 4)
                    at = pl.multiple_of(shard * 4 * wide + row, 16)
                    hold_ref[pl.ds(at, rows), :] = src[outer, rt1].astype(F32)

    def block(part):
        return jnp.concatenate([hold_ref[(4 * s + part) * wide : (4 * s + part + 1) * wide, :] for s in range(TENSOR)], axis=0)

    for third in range(3):

        @pl.when(i == third)
        def _():
            gq_ref[...] = block(third).T

    @pl.when(i == 3)
    def _():
        go_ref[...] = block(3)


def tail(meta, arrays, width, wide):
    outs = [sds((width, 3 * TENSOR * wide), F32), sds((TENSOR * wide, width), F32)]
    return call(
        partial(tail_kernel, wide),
        "tail",
        meta,
        (4,),
        list(arrays),
        [once(a.shape) for a in arrays],
        outs,
        [pl.BlockSpec((width, TENSOR * wide), lambda i, s: (0, jnp.minimum(i, 2))), whole(outs[1].shape)],
        0,
        6 * 4 * width * width,
        scratch=[pltpu.VMEM((TENSOR * 4 * wide, width), F32)],
    )


def natural(parts):
    own, to_x, to_y, across = parts
    return jnp.concatenate([own, to_y, to_x, across], axis=1)


def natural_halves(parts):
    send_a, keep_a, send_b, keep_b = parts
    a = jnp.stack([keep_a, send_a])
    b = jnp.stack([keep_b, send_b], axis=1)
    both = jnp.moveaxis(jnp.stack([a, b], axis=2), 3, 0)
    return both.reshape(both.shape[0], -1, both.shape[-1])


def xor_gather(x, n_blk, masks):
    for mask in reversed(masks):
        x = jnp.concatenate([x, swap(x, "blk", n_blk, mask)])
    return x


def scatter_blocks(blocks, n_blk):
    (got,) = yield [(jnp.concatenate([blocks[6:8], blocks[2:4]]), "blk", 1)]
    far = add(blocks[4:6], got[0:2]).astype(BF16)
    near = add(blocks[0:2], got[2:4]).astype(BF16)
    (far_got,) = yield [(far[1], "blk", 2)]
    far_sum = add(far[0], far_got).astype(BF16)
    other, near_got = yield [(far_sum, "blk", n_blk // 2), (near[1], "blk", 2)]
    yield [add(near[0], near_got).astype(BF16), other]


def local(n_dp, n_blk, tokens, cotangent, lengths, norm_gain, norm_bias, w_qkv, w_out, w_up, w_down):
    micro_count, rows, width = tokens.shape
    n_docs = lengths.shape[2]
    n_heads = width // HEAD // TENSOR
    wide = n_heads * HEAD
    inner = w_up.shape[1] // TENSOR
    splits = n_blk // (2 * TENSOR)
    s_masks = [TENSOR << b for b in reversed(range(splits.bit_length() - 1))]
    fast = n_dp == 4 and splits == 1
    me = lax.axis_index("blk")
    dp = lax.axis_index("dp")
    half = me // (n_blk // 2)
    quarter = lax.rem(me, TENSOR)
    x_pos, y_pos = (lax.rem(dp, 2), dp // 2) if fast else (0 * dp, 0 * dp)
    docs = lax.dynamic_index_in_dim(lengths, half, 0, False)[0]
    firsts = jnp.cumsum(docs, dtype=jnp.int32) - docs
    meta = jnp.concatenate([jnp.stack([quarter, x_pos, y_pos, me, half]).astype(jnp.int32), firsts])

    gain = norm_gain.astype(F32).reshape(1, width)
    bias = norm_bias.astype(F32).reshape(1, width)

    def mine(array):
        return lax.dynamic_index_in_dim(array, half, 0, False), lax.dynamic_index_in_dim(array, 1 - half, 0, False)

    def fourfold(own):
        near, twin = yield [(own, "blk", 2), (own, "blk", 1)]
        (far_twin,) = yield [(near, "blk", 1)]
        yield [own, near, twin, far_twin]

    def cross(array):
        (got,) = yield [(array, "blk", n_blk // 2)]
        yield from fourfold(got)

    order = Order({"dp": n_dp, "blk": n_blk})
    x_mine, x_other = mine(tokens)
    c_mine, c_other = mine(cotangent)
    x_far = order.start(cross(x_other))
    x_near = order.start(fourfold(x_mine))
    w_cut = order.done(cut(meta, w_qkv, wide))
    order.advance(x_near, x_far)
    c_far = order.start(cross(c_other))
    order.advance(x_near)
    stage = order.done(project(meta, order.hold(x_near.held), 0, QUADS, gain, bias, w_cut, n_blk, n_docs, None))
    order.advance(x_far)
    c_near = order.start(fourfold(c_mine))
    order.advance(c_far, x_far)
    stage = order.done(project(meta, order.hold(x_far.held), 4, QUADS, gain, bias, w_cut, n_blk, n_docs, stage))
    x_all, normed, q, k, v, kn, vn = stage
    if splits > 1:
        k, v, kn, vn = (xor_gather(a, n_blk, s_masks) for a in (k, v, kn, vn))
    order.advance(c_near)
    order.advance(c_far, c_near, c_far)
    cot, mo, ngm, *mlp_parts = order.done(feed(meta, normed, order.hold(c_near.held + c_far.held), w_up, w_down))
    if fast:
        mlp = order.start(reduce_halves(mlp_parts, n_blk))
    att, attf, lse = order.done(attend(meta, *order.hold([q]), kn, v, n_blk, n_docs))
    if fast:
        order.advance(mlp)
    out_part, do, delta, grad_out_part = order.done(mix(meta, *order.hold([att, attf, cot, mo]), w_out))
    out_steps = order.start(scatter_blocks(out_part, n_blk))
    if fast:
        order.advance(mlp)
    rest = (normed, x_all, ngm, w_cut, grad_out_part)
    q, do = order.hold([q, do])
    grads = order.done(attend_back(meta, q, do, lse, delta, kn, vn, k, n_blk, n_docs, rest if splits == 1 else None))
    if splits > 1:
        grads = list(grads)
        for at, mask in [(at, mask) for at in (1, 2) for mask in s_masks]:
            count = grads[at].shape[0] // 2
            grads[at] = add(grads[at][:count], swap(grads[at][count:], "blk", n_blk, mask)).astype(BF16)
        grads = order.done(join(meta, grads, *rest))
    ng_part, sums, *rest_parts = grads

    def gather_sums():
        total = sums
        for axis, mask in (("blk", 1), ("dp", 1), ("dp", 2), ("blk", 2), ("blk", n_blk // 2)):
            (got,) = yield [(total, axis, mask)]
            total = total + got
        yield [total]

    if fast:
        order.advance(mlp)
        (total,) = mlp.held

        def of_rest():
            (own,) = yield from reduce_pieces(rest_parts)
            yield from sum_halves(own[0], n_blk)

        makers = {
            "Q": of_rest(),
            "U": spread_pieces(total[:, 0]),
            "D": spread_pieces(total[:, 1]),
            "N": scatter_blocks(ng_part, n_blk),
            "S": gather_sums(),
            "O": out_steps,
        }
        chains = {"O": out_steps}
        for name in TAIL:
            if name == "u":
                grad_up = order.done(fill(meta, order.hold(chains["U"].end()), w_up.shape))
            elif name == "d":
                grad_down = order.done(fill(meta, order.hold(chains["D"].end()), w_down.shape))
            elif name in chains:
                order.advance(chains[name])
            else:
                chains[name] = order.start(makers[name])
        ng_steps, norm_steps, rest = (chains[name] for name in "NSQ")
    else:
        ng_steps = order.start(scatter_blocks(ng_part, n_blk))

    def ordered(own, other):
        return jnp.where(half == 0, jnp.stack([own, other]), jnp.stack([other, own])).astype(F32)

    output = (tokens.astype(F32) + ordered(*out_steps.end())).astype(BF16)
    normed_grad = ordered(*ng_steps.end())
    x_rows = tokens.astype(F32)
    centred = x_rows - jnp.mean(x_rows, axis=2, keepdims=True)
    inverse = lax.rsqrt(jnp.mean(centred * centred, axis=2, keepdims=True) + norm_eps)
    scaled = centred * inverse
    scaled_grad = normed_grad * norm_gain.astype(F32)
    input_grad = cotangent.astype(F32) + inverse * (
        scaled_grad
        - jnp.mean(scaled_grad, axis=2, keepdims=True)
        - scaled * jnp.mean(scaled_grad * scaled, axis=2, keepdims=True)
    )

    if fast:
        grad_qkv, grad_out = tail(meta, rest.end(), width, wide)
        (norm_sums,) = norm_steps.end()
    else:
        up, down = natural_halves(mlp_parts)
        (rest,) = natural(rest_parts)
        turn = rest[: 3 * wide].T.reshape(width, 3, wide)
        zeros = partial(jnp.zeros, dtype=BF16)
        up = lax.dynamic_update_slice_in_dim(zeros(w_up.shape), up, quarter * inner, 1)
        down = lax.dynamic_update_slice_in_dim(zeros(w_down.shape), down, quarter * inner, 0)
        turn = lax.dynamic_update_slice_in_dim(zeros((width, 3, TENSOR * wide)), turn, quarter * wide, 2)
        out = lax.dynamic_update_slice_in_dim(zeros(w_out.shape), rest[3 * wide :], quarter * wide, 0)
        grads = lax.psum((up, down, turn, out), ("dp", "blk"))
        grad_up, grad_down, turn, grad_out = (g.astype(F32) for g in grads)
        grad_qkv = turn.reshape(w_qkv.shape)
        norm_sums = lax.psum(sums, ("dp", "blk"))
    return (output, input_grad, norm_sums[0], norm_sums[1], grad_qkv, grad_out, grad_up, grad_down)


def solution(mesh):
    tokens = P(None, ("dp", "blk"), None)
    return jax.shard_map(
        partial(local, mesh.shape["dp"], mesh.shape["blk"]),
        mesh=mesh,
        in_specs=(tokens, tokens, P(None, "dp", None)) + (P(),) * 6,
        out_specs=(tokens, tokens) + (P(),) * 6,
        check_vma=False,
    )
```

time: 1320 us -> 313 us (0.24)
  blocking collectives: 502 us -> 0 us
  matrix products: 283 us -> 0 us
  waiting for transfers between devices: 272 us -> 95.6 us
  local copies, waits for them, and re-layouts: 158 us -> 15.1 us
  Pallas kernels: 0 us -> 131 us
  other arithmetic: 71 us -> 17.8 us
  starting transfers between devices: 0.67 us -> 51.1 us
  between operations: 15.4 us -> 1.55 us
    unnamed x2 -> x0, blocking collectives: 502 us -> none
    dot_general x80 -> x0, matrix products: 283 us -> none  [the longest x8 43.1 us: grad_step(): jnp.einsum('qhd,khd->hqk', out_grad, value_rows, preferred_element_type=j...]
    all_gather x8 -> x0, waiting for transfers between devices: 252 us -> none  [the longest x1 58.2 us: local(): lax.all_gather(shares[3].astype(jnp.bfloat16), ('dp', 'blk'), axis=0, til...]
    pallas_call x0 -> x10, Pallas kernels: none -> 131 us  [call(): pl.pallas_call(kernel, out_shape=out_shapes, grid_spec=pltpu.PrefetchScal...]
    ppermute x0 -> x63, waiting for transfers between devices: none -> 95.6 us  [swap(): return lax.ppermute(x, axis, [(i, i ^ mask) for i in range(size)])]
    reshape x12 -> x2, local copies, waits for them, and re-layouts: 73.2 us -> 1.16 us  [the longest x1 0.58 us: local(): bias = norm_bias.astype(F32).reshape(1, width)]
    ppermute x0 -> x63, starting transfers between devices: none -> 51.1 us  [swap(): return lax.ppermute(x, axis, [(i, i ^ mask) for i in range(size)])]
    reduce_sum x29 -> x3, other arithmetic: 39.9 us -> 1.23 us  [the longest x1 0.68 us: local(): jnp.mean(scaled_grad, axis=2, keepdims=True)]
  transfers between devices with their start and end apart: 12 -> 63, of which waited for: 7 -> 25; matrix products, arithmetic and copies ran while one was open for 23% -> 8% of each run, Pallas kernels for 0% -> 31%
where the time goes in v2:
time: 313 us; the launch traced here: 312 us
  Pallas kernels  131 us (42%)
  waiting for transfers between devices  95.6 us (31%)
  starting transfers between devices  51.1 us (16%)
  other arithmetic  17.8 us (6%)
  local copies, waits for them, and re-layouts  15.1 us (5%)
    pallas_call x10, Pallas kernels, call(): pl.pallas_call(kernel, out_shape=out_shapes, grid_spec=pltpu.PrefetchScal...  131 us
    ppermute x63, waiting for transfers between devices, swap(): return lax.ppermute(x, axis, [(i, i ^ mask) for i in range(size)])  95.6 us
    ppermute x63, starting transfers between devices, swap(): return lax.ppermute(x, axis, [(i, i ^ mask) for i in range(size)])  51.1 us
  transfers between devices with their start and end apart: 63, of which 25 were waited for; matrix products, arithmetic and copies ran while one was open for 8% of the time, Pallas kernels for 31%

profile of v2, /device:TPU:0, one launch (start us, length us, event | category | flops | bytes accessed | tf_op | source)
XLA Modules:
  0.0 312.3 jit_solution(16043295396438238839)
XLA Ops:
  2.2 3.1 collective-permute-start.1
  5.2 2.6 collective-permute-start
  8.6 4.0 %cut.1.refs_6_.refs_10_ = bf16[576,768]{1,0:T(8,128)(2,1)} custom-call(s32[9]{0:T(128)} %concatenate.9.meta_ref, bf16[768,2304]{1,0:T(8,128)(2,1)} %refs_2_.1, bf16[768,2304]{1,0:T(8,128)(2,1)} %refs_2_.1, bf16[768,2304]{1,0:T(8,128)(2,1)} %refs_2_.1), custom_call_target="tpu_custom_call" | custom-call | bytes 53084 | tf_op jit(solution)/shard_map/cut/pallas_call | solution.py:57
  12.6 9.1 %collective-permute-done.1.refs_1_ = bf16[256,768]{1,0:T(8,128)(2,1)S(1)} collective-permute-done((bf16[256,768]{1,0:T(8,128)(2,1)S(1)}, bf16[256,768]{1,0:T(8,128)(2,1)S(1)}, u32[]{:S(2)}, u32[]{:S(2)}) %collective-permute-start.1) | collective-permute-done | bytes 393248 | tf_op jit(solution)/shard_map/ppermute | solution.py:689
  21.8 4.3 %collective-permute-done.refs_0_ = bf16[256,768]{1,0:T(8,128)(2,1)S(1)} collective-permute-done((bf16[256,768]{1,0:T(8,128)(2,1)S(1)}, bf16[256,768]{1,0:T(8,128)(2,1)S(1)}, u32[]{:S(2)}, u32[]{:S(2)}) %collective-permute-start) | collective-permute-done | bytes 393248 | tf_op jit(solution)/shard_map/ppermute | solution.py:689
  26.2 3.0 collective-permute-start.7
  31.2 6.1 %project.2 = (bf16[8,256,768]{2,1,0:T(8,128)(2,1)}, bf16[8,256,768]{2,1,0:T(8,128)(2,1)}, bf16[8,192,256]{2,1,0:T(8,128)(2,1)}, bf16[8,192,256]{2,1,0:T(8,128)(2...) custom-call(s32[9]{0:T(128)} %concatenate.9.meta_ref, ...), custom_call_target="tpu_custom_call" | custom-call | flops 18119392 | bytes 157286 | tf_op jit(solution)/shard_map/project/pallas_call | solution.py:57
  37.3 6.7 %collective-permute-done.3.refs_1_ = bf16[256,768]{1,0:T(8,128)(2,1)S(1)} collective-permute-done((bf16[256,768]{1,0:T(8,128)(2,1)S(1)}, bf16[256,768]{1,0:T(8,128)(2,1)S(1)}, u32[]{:S(2)}, u32[]{:S(2)}) %collective-permute-start.3) | collective-permute-done | bytes 393248 | tf_op jit(solution)/shard_map/ppermute | solution.py:689
  44.6 2.9 collective-permute-done.7.refs_4_
  48.4 6.1 %project.3 = (bf16[8,256,768]{2,1,0:T(8,128)(2,1)}, bf16[8,256,768]{2,1,0:T(8,128)(2,1)}, bf16[8,192,256]{2,1,0:T(8,128)(2,1)}, bf16[8,192,256]{2,1,0:T(8,128)(2...) custom-call(s32[9]{0:T(128)} %concatenate.9.meta_ref, ...), custom_call_target="tpu_custom_call", output_to_operand_aliasing={{0}: (8, {}), {1}: (9, {}), {2}: (10, {}), {3}: (11, {}), {... | custom-call | flops 18119392 | bytes 157286 | tf_op jit(solution)/shard_map/project/pallas_call | solution.py:57
  56.2 8.1 %collective-permute-done.11.refs_5_ = bf16[256,768]{1,0:T(8,128)(2,1)S(1)} collective-permute-done((bf16[256,768]{1,0:T(8,128)(2,1)S(1)}, bf16[256,768]{1,0:T(8,128)(2,1)S(1)}, u32[]{:S(2)}, u32[]{:S(2)}) %collective-permute-start.11) | collective-permute-done | bytes 393248 | tf_op jit(solution)/shard_map/ppermute | solution.py:689
  67.4 24.7 %feed.1 = (bf16[8,256,768]{2,1,0:T(8,128)(2,1)}, bf16[8,256,768]{2,1,0:T(8,128)(2,1)}, bf16[8,256,768]{2,1,0:T(8,128)(2,1)}, bf16[2,2,96,768]{3,2,1,0:T(8,128)(2...) custom-call(s32[9]{0:T(128)} %concatenate.9.meta_ref, ...), custom_call_target="tpu_custom_call" | custom-call | flops 289910304 | bytes 346030 | tf_op jit(solution)/shard_map/feed/pallas_call | solution.py:57
  95.1 18.9 %attend.1 = (bf16[8,192,256]{2,1,0:T(8,128)(2,1)}, f32[8,192,256]{2,1,0:T(8,128)}, f32[8,8,256]{2,1,0:T(8,128)}) custom-call(s32[9]{0:T(128)} %concatenate.9.meta_ref, bf16[8,192,256]{2,1,0:T(8,128)(2,1)} %get-tuple-element.288.refs_0_, bf16[8,3,256,64]{3,2,1,0:T(8,128)(2,1)} %get-tuple-element.267.refs_1_.refs_4_, ...), custom_call_target="tpu_custom_call" | custom-call | flops 72155448 | bytes 125829 | tf_op jit(solution)/shard_map/attend/pallas_call | solution.py:57
  116.3 8.5 %mix.1 = (bf16[8,256,768]{2,1,0:T(8,128)(2,1)}, bf16[8,192,256]{2,1,0:T(8,128)(2,1)}, f32[8,8,256]{2,1,0:T(8,128)}, f32[192,768]{1,0:T(8,128)}) custom-call(s32[9]{0:T(128)} %concatenate.9.meta_ref, bf16[8,192,256]{2,1,0:T(8,128)(2,1)} %get-tuple-element.278.refs_0_, f32[8,192,256]{2,1,0:T(8,128)} %get-tuple-element.279.refs_1_, ...), custom_call_target="tpu_custom_call" | custom-call | flops 36238784 | bytes 314572 | tf_op jit(solution)/shard_map/mix/pallas_call | solution.py:57
  128.3 38.7 %attend_back.1 = (bf16[8,256,768]{2,1,0:T(8,128)(2,1)}, f32[8,768]{1,0:T(8,128)}, bf16[1,192,768]{2,1,0:T(8,128)(2,1)}, bf16[1,192,768]{2,1,0:T(8,128)(2,1)}, bf...) custom-call(s32[9]{0:T(128)} %concatenate.9.meta_ref, bf16[8,192,256]{2,1,0:T(8,128)(2,1)} %get-tuple-element.288.refs_0_, ...), custom_call_target="tpu_custom_call" | custom-call | flops 180388624 | bytes 125829 | tf_op jit(solution)/shard_map/attend_back/pallas_call | solution.py:57
  168.9 2.3 collective-permute-start.23
  175.9 2.9 collective-permute-done.23
  181.1 6.8 %collective-permute-done.20 = bf16[1,192,768]{2,1,0:T(8,128)(2,1)S(1)} collective-permute-done((bf16[1,192,768]{2,1,0:T(8,128)(2,1)S(1)}, bf16[1,192,768]{2,1,0:T(8,128)(2,1)S(1)}, u32[]{:S(2)}, u32[]{:S(2)}) %collective-permute-start.20) | collective-permute-done | bytes 294944 | tf_op jit(solution)/shard_map/ppermute | solution.py:689
  205.1 4.4 %collective-permute-done.34 = bf16[2,96,768]{2,1,0:T(8,128)(2,1)S(1)} collective-permute-done((bf16[2,96,768]{2,1,0:T(8,128)(2,1)S(1)}, bf16[2,96,768]{2,1,0:T(8,128)(2,1)S(1)}, u32[]{:S(2)}, u32[]{:S(2)}) %collective-permute-start.34) | collective-permute-done | bytes 294944 | tf_op jit(solution)/shard_map/ppermute | solution.py:689
  210.5 5.7 %collective-permute-done.32 = bf16[2,96,768]{2,1,0:T(8,128)(2,1)S(1)} collective-permute-done((bf16[2,96,768]{2,1,0:T(8,128)(2,1)S(1)}, bf16[2,96,768]{2,1,0:T(8,128)(2,1)S(1)}, u32[]{:S(2)}, u32[]{:S(2)}) %collective-permute-start.32) | collective-permute-done | bytes 294944 | tf_op jit(solution)/shard_map/ppermute | solution.py:689
  224.8 8.7 %collective-permute-done.49 = bf16[256,768]{1,0:T(8,128)(2,1)S(1)} collective-permute-done((bf16[256,768]{1,0:T(8,128)(2,1)S(1)}, bf16[256,768]{1,0:T(8,128)(2,1)S(1)}, u32[]{:S(2)}, u32[]{:S(2)}) %collective-permute-start.49) | collective-permute-done | bytes 393248 | tf_op jit(solution)/shard_map/ppermute | solution.py:689
  237.9 7.7 %fill.2 = f32[768,3072]{1,0:T(8,128)} custom-call(s32[9]{0:T(128)} %concatenate.9.meta_ref, bf16[2,2,96,768]{3,2,1,0:T(8,128)(2,1)} %copy-done.7, bf16[2,2,96,768]{3,2,1,0:T(8,128)(2,1)} %copy-done.8, bf16[2,2,96,768]{3,2,1,0:T(8,128)(2,1)} %copy-done.16, bf16[2,2,96,768]{3,2,1,0:T(8,128)(2,1)} %copy-done.19, bf16[2,2,96,768]{3,2,1,0:T(8,128)(2,1)} %copy-done.22, ...), custom_call_target="tpu_custom_call" | custom-call | bytes 283115 | tf_op jit(solution)/shard_map/fill/pallas_call | solution.py:57
  247.4 2.1 pad_maximum_fusion.8.refs_1_
  252.6 2.2 collective-permute-done.60
  258.2 3.1 %collective-permute-start.58 = (bf16[256,768]{1,0:T(8,128)(2,1)}, bf16[256,768]{1,0:T(8,128)(2,1)S(1)}, u32[]{:S(2)}, u32[]{:S(2)}) collective-permute-start(bf16[256,768]{1,0:T(8,128)(2,1)} %fusion.12), channel_id=1, source_target_pairs={{0,4},{1,5},{2,6},{3,7},{4,0},{5,1},{6,2},{7,3},{8,12},{9,13},{10,... | collective-permute-start | bytes 1179656 | tf_op jit(solution)/shard_map/ppermute | solution.py:689
  261.3 4.4 %collective-permute-done.52.refs_2_ = bf16[2,2,96,768]{3,2,1,0:T(8,128)(2,1)S(1)} collective-permute-done((bf16[2,2,96,768]{3,2,1,0:T(8,128)(2,1)S(1)}, bf16[2,2,96,768]{3,2,1,0:T(8,128)(2,1)S(1)}, u32[]{:S(2)}, u32[]{:S(2)}) %collective-permute-start.52) | collective-permute-done | bytes 589856 | tf_op jit(solution)/shard_map/ppermute | solution.py:689
  266.6 2.4 collective-permute-done.53.refs_3_
  269.1 3.1 collective-permute-start.50
  274.4 7.6 %fill.3 = f32[3072,768]{1,0:T(8,128)} custom-call(s32[9]{0:T(128)} %concatenate.9.meta_ref, bf16[2,2,96,768]{3,2,1,0:T(8,128)(2,1)} %copy-done.4, bf16[2,2,96,768]{3,2,1,0:T(8,128)(2,1)} %copy-done.5, bf16[2,2,96,768]{3,2,1,0:T(8,128)(2,1)} %copy-done.13, bf16[2,2,96,768]{3,2,1,0:T(8,128)(2,1)} %copy-done.17, bf16[2,2,96,768]{3,2,1,0:T(8,128)(2,1)} %copy-done.18, ...), custom_call_target="tpu_custom_call" | custom-call | bytes 283115 | tf_op jit(solution)/shard_map/fill/pallas_call | solution.py:57
  283.7 13.0 %collective-permute-done.50 = bf16[256,768]{1,0:T(8,128)(2,1)} collective-permute-done((bf16[256,768]{1,0:T(8,128)(2,1)}, bf16[256,768]{1,0:T(8,128)(2,1)}, u32[]{:S(2)}, u32[]{:S(2)}) %collective-permute-start.50) | collective-permute-done | bytes 393248 | tf_op jit(solution)/shard_map/ppermute | solution.py:689
  298.5 3.3 %fusion.7 = (f32[2,256,768]{2,1,0:T(8,128)}, bf16[2,256,768]{2,1,0:T(8,128)(2,1)}) fusion(bf16[2,256,768]{2,1,0:T(8,128)(2,1)S(1)} %copy-done, bf16[2,256,768]{2,1,0:T(8,128)(2,1)S(1)} %copy-done.1, f32[2,256]{1,0:T(2,128)S(1)} %broadcast_multiply_fusion, f32[2,256]{1,0:T(2,128)S(1)} %broadcast_multiply_fusion.1, f32[768]{0:T(1024)S(1)} %convert_element_type.176, ...), kind=kLoop, calls=%fused_computation.10 | loop fusion | flops 7864320 | bytes 5516289 | tf_op jit(solution)/shard_map/add | solution.py:1012
  303.5 8.8 %tail.1 = (f32[768,2304]{1,0:T(8,128)}, f32[768,768]{1,0:T(8,128)}) custom-call(s32[9]{0:T(128)} %concatenate.9.meta_ref, bf16[2,2,96,768]{3,2,1,0:T(8,128)(2,1)} %copy-done.6, bf16[2,2,96,768]{3,2,1,0:T(8,128)(2,1)} %pad_maximum_fusion.8.refs_1_, bf16[2,2,96,768]{3,2,1,0:T(8,128)(2,1)} %copy-done.14, bf16[2,2,96,768]{3,2,1,0:T(8,128)(2,1)} %copy-done.21, ...), custom_call_target="tpu_custom_call" | custom-call | bytes 283115 | tf_op jit(solution)/shard_map/tail/pallas_call | solution.py:57
  (286 shorter events, 75.5 us)
Async XLA Ops:
  2.2 19.6 %collective-permute-start.1 = (bf16[256,768]{1,0:T(8,128)(2,1)S(1)}, bf16[256,768]{1,0:T(8,128)(2,1)S(1)}, u32[]{:S(2)}, u32[]{:S(2)}) collective-permute-start(bf16[256,768]{1,0:T(8,128)(2,1)S(1)} %get-tuple-element.218.refs_0_), channel_id=1, source_target_pairs={{0,2},{1,3},{2,0},{3,1},{4,6},{5,7},{6,4},{7,5},{8,10},{9,11},{10,... | collective-permute-start | bytes 1179656 | tf_op jit(solution)/shard_map/ppermute | solution.py:689
  5.2 16.5 %collective-permute-start.2 = (bf16[256,768]{1,0:T(8,128)(2,1)S(1)}, bf16[256,768]{1,0:T(8,128)(2,1)S(1)}, u32[]{:S(2)}, u32[]{:S(2)}) collective-permute-start(bf16[256,768]{1,0:T(8,128)(2,1)S(1)} %get-tuple-element.218.refs_0_), channel_id=1, source_target_pairs={{0,1},{1,0},{2,3},{3,2},{4,5},{5,4},{6,7},{7,6},{8,9},{9,8},{10,11... | collective-permute-start | bytes 1179656 | tf_op jit(solution)/shard_map/ppermute | solution.py:689
  5.2 20.9 %collective-permute-start = (bf16[256,768]{1,0:T(8,128)(2,1)S(1)}, bf16[256,768]{1,0:T(8,128)(2,1)S(1)}, u32[]{:S(2)}, u32[]{:S(2)}) collective-permute-start(bf16[256,768]{1,0:T(8,128)(2,1)S(1)} %get-tuple-element.452), channel_id=1, source_target_pairs={{0,4},{1,5},{2,6},{3,7},{4,0},{5,1},{6,2},{7,3},{8,12},{9,13},{10,... | collective-permute-start | bytes 1179656 | tf_op jit(solution)/shard_map/ppermute | solution.py:689
  26.1 17.9 %collective-permute-start.3 = (bf16[256,768]{1,0:T(8,128)(2,1)S(1)}, bf16[256,768]{1,0:T(8,128)(2,1)S(1)}, u32[]{:S(2)}, u32[]{:S(2)}) collective-permute-start(bf16[256,768]{1,0:T(8,128)(2,1)S(1)} %collective-permute-done.refs_0_), channel_id=1, source_target_pairs={{0,2},{1,3},{2,0},{3,1},{4,6},{5,7},{6,4},{7,5},{8,10},{9,11},{10,... | collective-permute-start | bytes 1179656 | tf_op jit(solution)/shard_map/ppermute | solution.py:689
  26.1 17.9 %collective-permute-start.4 = (bf16[256,768]{1,0:T(8,128)(2,1)S(1)}, bf16[256,768]{1,0:T(8,128)(2,1)S(1)}, u32[]{:S(2)}, u32[]{:S(2)}) collective-permute-start(bf16[256,768]{1,0:T(8,128)(2,1)S(1)} %collective-permute-done.refs_0_), channel_id=1, source_target_pairs={{0,1},{1,0},{2,3},{3,2},{4,5},{5,4},{6,7},{7,6},{8,9},{9,8},{10,11... | collective-permute-start | bytes 1179656 | tf_op jit(solution)/shard_map/ppermute | solution.py:689
  26.2 21.3 %collective-permute-start.7 = (bf16[256,768]{1,0:T(8,128)(2,1)S(1)}, bf16[256,768]{1,0:T(8,128)(2,1)S(1)}, u32[]{:S(2)}, u32[]{:S(2)}) collective-permute-start(bf16[256,768]{1,0:T(8,128)(2,1)S(1)} %get-tuple-element.216), channel_id=1, source_target_pairs={{0,4},{1,5},{2,6},{3,7},{4,0},{5,1},{6,2},{7,3},{8,12},{9,13},{10,... | collective-permute-start | bytes 1179656 | tf_op jit(solution)/shard_map/ppermute | solution.py:689
  47.5 16.8 %collective-permute-start.11 = (bf16[256,768]{1,0:T(8,128)(2,1)S(1)}, bf16[256,768]{1,0:T(8,128)(2,1)S(1)}, u32[]{:S(2)}, u32[]{:S(2)}) collective-permute-start(bf16[256,768]{1,0:T(8,128)(2,1)S(1)} %collective-permute-done.7.refs_4_), channel_id=1, source_target_pairs={{0,2},{1,3},{2,0},{3,1},{4,6},{5,7},{6,4},{7,5},{8,10},{9,11},{10,... | collective-permute-start | bytes 1179656 | tf_op jit(solution)/shard_map/ppermute | solution.py:689
  47.5 16.8 %collective-permute-start.12 = (bf16[256,768]{1,0:T(8,128)(2,1)S(1)}, bf16[256,768]{1,0:T(8,128)(2,1)S(1)}, u32[]{:S(2)}, u32[]{:S(2)}) collective-permute-start(bf16[256,768]{1,0:T(8,128)(2,1)S(1)} %collective-permute-done.7.refs_4_), channel_id=1, source_target_pairs={{0,1},{1,0},{2,3},{3,2},{4,5},{5,4},{6,7},{7,6},{8,9},{9,8},{10,11... | collective-permute-start | bytes 1179656 | tf_op jit(solution)/shard_map/ppermute | solution.py:689
  92.1 21.9 %collective-permute-start.14 = (bf16[2,2,96,768]{3,2,1,0:T(8,128)(2,1)}, bf16[2,2,96,768]{3,2,1,0:T(8,128)(2,1)S(1)}, u32[]{:S(2)}, u32[]{:S(2)}) collective-permute-start(bf16[2,2,96,768]{3,2,1,0:T(8,128)(2,1)} %get-tuple-element.264), channel_id=1, source_target_pairs={{0,8},{8,0},{16,24},{24,16},{1,9},{9,1},{17,25},{25,17},{2,10},{10... | collective-permute-start | bytes 1769480 | tf_op jit(solution)/shard_map/ppermute | solution.py:689
  93.6 20.4 %collective-permute-start.15 = (bf16[2,2,96,768]{3,2,1,0:T(8,128)(2,1)}, bf16[2,2,96,768]{3,2,1,0:T(8,128)(2,1)S(1)}, u32[]{:S(2)}, u32[]{:S(2)}) collective-permute-start(bf16[2,2,96,768]{3,2,1,0:T(8,128)(2,1)} %get-tuple-element.265), channel_id=1, source_target_pairs={{0,16},{8,24},{16,0},{24,8},{1,17},{9,25},{17,1},{25,9},{2,18},{10... | collective-permute-start | bytes 1769480 | tf_op jit(solution)/shard_map/ppermute | solution.py:689
  127.9 40.7 %collective-permute-start.22 = (bf16[2,2,96,768]{3,2,1,0:T(8,128)(2,1)S(1)}, bf16[2,2,96,768]{3,2,1,0:T(8,128)(2,1)S(1)}, u32[]{:S(2)}, u32[]{:S(2)}) collective-permute-start(bf16[2,2,96,768]{3,2,1,0:T(8,128)(2,1)S(1)} %pad_maximum_fusion.2), channel_id=1, source_target_pairs={{0,4},{1,5},{2,6},{3,7},{4,0},{5,1},{6,2},{7,3},{8,12},{9,13},{10,... | collective-permute-start | bytes 1769480 | tf_op jit(solution)/shard_map/ppermute | solution.py:689
  168.8 24.7 %collective-permute-start.31 = (bf16[4,256,768]{2,1,0:T(8,128)(2,1)S(1)}, bf16[4,256,768]{2,1,0:T(8,128)(2,1)S(1)}, u32[]{:S(2)}, u32[]{:S(2)}) collective-permute-start(bf16[4,256,768]{2,1,0:T(8,128)(2,1)S(1)} %pad_maximum_fusion.1), channel_id=1, source_target_pairs={{0,1},{1,0},{2,3},{3,2},{4,5},{5,4},{6,7},{7,6},{8,9},{9,8},{10,11... | collective-permute-start | bytes 4718600 | tf_op jit(solution)/shard_map/ppermute | solution.py:689
  172.7 15.1 %collective-permute-start.20 = (bf16[1,192,768]{2,1,0:T(8,128)(2,1)S(1)}, bf16[1,192,768]{2,1,0:T(8,128)(2,1)S(1)}, u32[]{:S(2)}, u32[]{:S(2)}) collective-permute-start(bf16[1,192,768]{2,1,0:T(8,128)(2,1)S(1)} %copy-done.57), channel_id=1, source_target_pairs={{0,16},{8,24},{16,0},{24,8},{1,17},{9,25},{17,1},{25,9},{2,18},{10... | collective-permute-start | bytes 884744 | tf_op jit(solution)/shard_map/ppermute | solution.py:689
  181.1 36.8 %collective-permute-start.16 = (bf16[4,256,768]{2,1,0:T(8,128)(2,1)}, bf16[4,256,768]{2,1,0:T(8,128)(2,1)S(1)}, u32[]{:S(2)}, u32[]{:S(2)}) collective-permute-start(bf16[4,256,768]{2,1,0:T(8,128)(2,1)} %pad_maximum_fusion), channel_id=1, source_target_pairs={{0,1},{1,0},{2,3},{3,2},{4,5},{5,4},{6,7},{7,6},{8,9},{9,8},{10,11... | collective-permute-start | bytes 4718600 | tf_op jit(solution)/shard_map/ppermute | solution.py:689
  190.0 13.8 %collective-permute-start.25 = (bf16[192,768]{1,0:T(8,128)(2,1)S(1)}, bf16[192,768]{1,0:T(8,128)(2,1)S(1)}, u32[]{:S(2)}, u32[]{:S(2)}) collective-permute-start(bf16[192,768]{1,0:T(8,128)(2,1)S(1)} %fusion.19), channel_id=1, source_target_pairs={{0,4},{1,5},{2,6},{3,7},{4,0},{5,1},{6,2},{7,3},{8,12},{9,13},{10,... | collective-permute-start | bytes 884744 | tf_op jit(solution)/shard_map/ppermute | solution.py:689
  201.7 20.0 %collective-permute-start.42 = (bf16[2,2,96,768]{3,2,1,0:T(8,128)(2,1)S(1)}, bf16[2,2,96,768]{3,2,1,0:T(8,128)(2,1)S(1)}, u32[]{:S(2)}, u32[]{:S(2)}) collective-permute-start(bf16[2,2,96,768]{3,2,1,0:T(8,128)(2,1)S(1)} %pad_maximum_fusion.3.refs_0_), channel_id=1, source_target_pairs={{0,16},{8,24},{16,0},{24,8},{1,17},{9,25},{17,1},{25,9},{2,18},{10... | collective-permute-start | bytes 1769480 | tf_op jit(solution)/shard_map/ppermute | solution.py:689
  203.9 17.9 %collective-permute-start.43 = (bf16[2,2,96,768]{3,2,1,0:T(8,128)(2,1)S(1)}, bf16[2,2,96,768]{3,2,1,0:T(8,128)(2,1)S(1)}, u32[]{:S(2)}, u32[]{:S(2)}) collective-permute-start(bf16[2,2,96,768]{3,2,1,0:T(8,128)(2,1)S(1)} %pad_maximum_fusion.4.refs_1_), channel_id=1, source_target_pairs={{0,8},{8,0},{16,24},{24,16},{1,9},{9,1},{17,25},{25,17},{2,10},{10... | collective-permute-start | bytes 1769480 | tf_op jit(solution)/shard_map/ppermute | solution.py:689
  205.1 16.7 %collective-permute-start.44 = (bf16[2,2,96,768]{3,2,1,0:T(8,128)(2,1)S(1)}, bf16[2,2,96,768]{3,2,1,0:T(8,128)(2,1)S(1)}, u32[]{:S(2)}, u32[]{:S(2)}) collective-permute-start(bf16[2,2,96,768]{3,2,1,0:T(8,128)(2,1)S(1)} %pad_maximum_fusion.3.refs_0_), channel_id=1, source_target_pairs={{0,1},{1,0},{2,3},{3,2},{4,5},{5,4},{6,7},{7,6},{8,9},{9,8},{10,11... | collective-permute-start | bytes 1769480 | tf_op jit(solution)/shard_map/ppermute | solution.py:689
  223.5 26.0 %collective-permute-start.36 = (bf16[2,2,96,768]{3,2,1,0:T(8,128)(2,1)S(1)}, bf16[2,2,96,768]{3,2,1,0:T(8,128)(2,1)S(1)}, u32[]{:S(2)}, u32[]{:S(2)}) collective-permute-start(bf16[2,2,96,768]{3,2,1,0:T(8,128)(2,1)S(1)} %pad_maximum_fusion.5.refs_0_), channel_id=1, source_target_pairs={{0,16},{8,24},{16,0},{24,8},{1,17},{9,25},{17,1},{25,9},{2,18},{10... | collective-permute-start | bytes 1769480 | tf_op jit(solution)/shard_map/ppermute | solution.py:689
  233.5 17.7 %collective-permute-start.37 = (bf16[2,2,96,768]{3,2,1,0:T(8,128)(2,1)S(1)}, bf16[2,2,96,768]{3,2,1,0:T(8,128)(2,1)S(1)}, u32[]{:S(2)}, u32[]{:S(2)}) collective-permute-start(bf16[2,2,96,768]{3,2,1,0:T(8,128)(2,1)S(1)} %pad_maximum_fusion.6.refs_1_), channel_id=1, source_target_pairs={{0,8},{8,0},{16,24},{24,16},{1,9},{9,1},{17,25},{25,17},{2,10},{10... | collective-permute-start | bytes 1769480 | tf_op jit(solution)/shard_map/ppermute | solution.py:689
  233.5 18.4 %collective-permute-start.38 = (bf16[2,2,96,768]{3,2,1,0:T(8,128)(2,1)S(1)}, bf16[2,2,96,768]{3,2,1,0:T(8,128)(2,1)S(1)}, u32[]{:S(2)}, u32[]{:S(2)}) collective-permute-start(bf16[2,2,96,768]{3,2,1,0:T(8,128)(2,1)S(1)} %pad_maximum_fusion.5.refs_0_), channel_id=1, source_target_pairs={{0,1},{1,0},{2,3},{3,2},{4,5},{5,4},{6,7},{7,6},{8,9},{9,8},{10,11... | collective-permute-start | bytes 1769480 | tf_op jit(solution)/shard_map/ppermute | solution.py:689
  233.6 18.3 %collective-permute-start.39 = (bf16[2,2,96,768]{3,2,1,0:T(8,128)(2,1)S(1)}, bf16[2,2,96,768]{3,2,1,0:T(8,128)(2,1)S(1)}, u32[]{:S(2)}, u32[]{:S(2)}) collective-permute-start(bf16[2,2,96,768]{3,2,1,0:T(8,128)(2,1)S(1)} %pad_maximum_fusion.6.refs_1_), channel_id=1, source_target_pairs={{0,1},{1,0},{2,3},{3,2},{4,5},{5,4},{6,7},{7,6},{8,9},{9,8},{10,11... | collective-permute-start | bytes 1769480 | tf_op jit(solution)/shard_map/ppermute | solution.py:689
  251.2 14.5 %collective-permute-start.52 = (bf16[2,2,96,768]{3,2,1,0:T(8,128)(2,1)S(1)}, bf16[2,2,96,768]{3,2,1,0:T(8,128)(2,1)S(1)}, u32[]{:S(2)}, u32[]{:S(2)}) collective-permute-start(bf16[2,2,96,768]{3,2,1,0:T(8,128)(2,1)S(1)} %pad_maximum_fusion.7.refs_0_), channel_id=1, source_target_pairs={{0,16},{8,24},{16,0},{24,8},{1,17},{9,25},{17,1},{25,9},{2,18},{10... | collective-permute-start | bytes 1769480 | tf_op jit(solution)/shard_map/ppermute | solution.py:689
  254.8 14.3 %collective-permute-start.53 = (bf16[2,2,96,768]{3,2,1,0:T(8,128)(2,1)}, bf16[2,2,96,768]{3,2,1,0:T(8,128)(2,1)S(1)}, u32[]{:S(2)}, u32[]{:S(2)}) collective-permute-start(bf16[2,2,96,768]{3,2,1,0:T(8,128)(2,1)} %pad_maximum_fusion.8.refs_1_), channel_id=1, source_target_pairs={{0,8},{8,0},{16,24},{24,16},{1,9},{9,1},{17,25},{25,17},{2,10},{10... | collective-permute-start | bytes 1769480 | tf_op jit(solution)/shard_map/ppermute | solution.py:689
  257.0 15.2 %collective-permute-start.54 = (bf16[2,2,96,768]{3,2,1,0:T(8,128)(2,1)S(1)}, bf16[2,2,96,768]{3,2,1,0:T(8,128)(2,1)S(1)}, u32[]{:S(2)}, u32[]{:S(2)}) collective-permute-start(bf16[2,2,96,768]{3,2,1,0:T(8,128)(2,1)S(1)} %pad_maximum_fusion.7.refs_0_), channel_id=1, source_target_pairs={{0,1},{1,0},{2,3},{3,2},{4,5},{5,4},{6,7},{7,6},{8,9},{9,8},{10,11... | collective-permute-start | bytes 1769480 | tf_op jit(solution)/shard_map/ppermute | solution.py:689
  258.2 24.0 %collective-permute-start.58 = (bf16[256,768]{1,0:T(8,128)(2,1)}, bf16[256,768]{1,0:T(8,128)(2,1)S(1)}, u32[]{:S(2)}, u32[]{:S(2)}) collective-permute-start(bf16[256,768]{1,0:T(8,128)(2,1)} %fusion.12), channel_id=1, source_target_pairs={{0,4},{1,5},{2,6},{3,7},{4,0},{5,1},{6,2},{7,3},{8,12},{9,13},{10,... | collective-permute-start | bytes 1179656 | tf_op jit(solution)/shard_map/ppermute | solution.py:689
  261.3 21.3 %collective-permute-start.59 = (bf16[256,768]{1,0:T(8,128)(2,1)}, bf16[256,768]{1,0:T(8,128)(2,1)}, u32[]{:S(2)}, u32[]{:S(2)}) collective-permute-start(bf16[256,768]{1,0:T(8,128)(2,1)} %slice_bitcast_fusion.2), channel_id=1, source_target_pairs={{0,2},{1,3},{2,0},{3,1},{4,6},{5,7},{6,4},{7,5},{8,10},{9,11},{10,... | collective-permute-start | bytes 1179656 | tf_op jit(solution)/shard_map/ppermute | solution.py:689
  265.7 16.4 %collective-permute-start.55 = (bf16[2,2,96,768]{3,2,1,0:T(8,128)(2,1)}, bf16[2,2,96,768]{3,2,1,0:T(8,128)(2,1)}, u32[]{:S(2)}, u32[]{:S(2)}) collective-permute-start(bf16[2,2,96,768]{3,2,1,0:T(8,128)(2,1)} %pad_maximum_fusion.8.refs_1_), channel_id=1, source_target_pairs={{0,1},{1,0},{2,3},{3,2},{4,5},{5,4},{6,7},{7,6},{8,9},{9,8},{10,11... | collective-permute-start | bytes 1769480 | tf_op jit(solution)/shard_map/ppermute | solution.py:689
  269.1 27.6 %collective-permute-start.50 = (bf16[256,768]{1,0:T(8,128)(2,1)}, bf16[256,768]{1,0:T(8,128)(2,1)}, u32[]{:S(2)}, u32[]{:S(2)}) collective-permute-start(bf16[256,768]{1,0:T(8,128)(2,1)} %fusion.13), channel_id=1, source_target_pairs={{0,4},{1,5},{2,6},{3,7},{4,0},{5,1},{6,2},{7,3},{8,12},{9,13},{10,... | collective-permute-start | bytes 1179656 | tf_op jit(solution)/shard_map/ppermute | solution.py:689
  272.2 24.6 %collective-permute-start.51 = (bf16[256,768]{1,0:T(8,128)(2,1)}, bf16[256,768]{1,0:T(8,128)(2,1)}, u32[]{:S(2)}, u32[]{:S(2)}) collective-permute-start(bf16[256,768]{1,0:T(8,128)(2,1)} %slice_bitcast_fusion.1), channel_id=1, source_target_pairs={{0,2},{1,3},{2,0},{3,1},{4,6},{5,7},{6,4},{7,5},{8,10},{9,11},{10,... | collective-permute-start | bytes 1179656 | tf_op jit(solution)/shard_map/ppermute | solution.py:689
  282.0 19.8 %collective-permute-start.61 = (bf16[2,2,96,768]{3,2,1,0:T(8,128)(2,1)S(1)}, bf16[2,2,96,768]{3,2,1,0:T(8,128)(2,1)S(1)}, u32[]{:S(2)}, u32[]{:S(2)}) collective-permute-start(bf16[2,2,96,768]{3,2,1,0:T(8,128)(2,1)S(1)} %copy-done.15), channel_id=1, source_target_pairs={{0,1},{1,0},{2,3},{3,2},{4,5},{5,4},{6,7},{7,6},{8,9},{9,8},{10,11... | collective-permute-start | bytes 1769480 | tf_op jit(solution)/shard_map/ppermute | solution.py:689
  282.1 19.7 %collective-permute-start.62 = (bf16[2,2,96,768]{3,2,1,0:T(8,128)(2,1)S(1)}, bf16[2,2,96,768]{3,2,1,0:T(8,128)(2,1)S(1)}, u32[]{:S(2)}, u32[]{:S(2)}) collective-permute-start(bf16[2,2,96,768]{3,2,1,0:T(8,128)(2,1)S(1)} %collective-permute-done.53.refs_3_), channel_id=1, source_target_pairs={{0,1},{1,0},{2,3},{3,2},{4,5},{5,4},{6,7},{7,6},{8,9},{9,8},{10,11... | collective-permute-start | bytes 1769480 | tf_op jit(solution)/shard_map/ppermute | solution.py:689
  (90 other events, 919.4 us)

commit v3 on v2

--- a/solution.py
+++ b/solution.py
@@ -17,7 +17,9 @@
 BF16 = jnp.bfloat16
 VMEM_LIMIT = 56 * 1024 * 1024
 COST = 0.02
-TAIL = "QUNSSDUQDSNUSQDQOSUNuQDSOdQON"
+ATTEND_PAIRS = 9
+BACK_PAIRS = 3
+TAIL = "NMQONMQQOMMNQmNQnQ"
 
 NN = (((1,), (0,)), ((), ()))
 NT = (((1,), (1,)), ((), ()))
@@ -261,14 +263,15 @@
     return (k_index >= doc_start(meta, index, n_docs)) & (k_index <= index)
 
 
-def attend_kernel(n_heads, n_blk, n_docs, meta, q_ref, kn_ref, v_ref, att_ref, attf_ref, lse_ref, s_ref, acc_ref, top_ref, sum_ref, q_list, k_list):
+def attend_kernel(n_heads, n_blk, n_docs, meta, q_ref, kn_ref, v_ref, att_ref, lse_ref, s_ref, acc_ref, top_ref, sum_ref, q_list, k_list):
     count, _, rows = q_ref.shape
     heads = range(n_heads)
     base = pl.program_id(0) * count
     found = list_pairs(meta, base, count, rows, n_blk, n_docs, q_list, k_list)
-    q_list[found] = count
-    k_list[found] = 0
-    steps = (found + 1) // 2
+    for extra in range(ATTEND_PAIRS - 1):
+        q_list[found + extra] = count
+        k_list[found + extra] = 0
+    steps = (found + ATTEND_PAIRS - 1) // ATTEND_PAIRS
     top_ref[...] = jnp.full_like(top_ref, masked_score)
     sum_ref[...] = jnp.zeros_like(sum_ref)
     acc_ref[...] = jnp.zeros_like(acc_ref)
@@ -277,7 +280,7 @@
         return how(tile.reshape(rows // 8, 8, rows), axis=0)
 
     def score(n, _):
-        for at in (2 * n, 2 * n + 1):
+        for at in [ATTEND_PAIRS * n + e for e in range(ATTEND_PAIRS)]:
             j, kb = q_list[at], k_list[at]
             jq = jnp.minimum(j, count - 1)
             ka = k_slot(meta, kb, n_blk)
@@ -299,15 +302,15 @@
     lax.fori_loop(0, count + 1, settle, 0)
 
     def weigh(n, _):
-        both = (2 * n, 2 * n + 1)
+        many = [ATTEND_PAIRS * n + e for e in range(ATTEND_PAIRS)]
         weights = []
-        for at in both:
+        for at in many:
             j = q_list[at]
             for h in heads:
                 p = jnp.exp(s_ref[at, h] - top_ref[j, h, 0:1])
                 sum_ref[j, h] += fold(p, jnp.sum)
                 weights.append(p.astype(BF16))
-        for m, at in enumerate(both):
+        for m, at in enumerate(many):
             j, ka = q_list[at], k_slot(meta, k_list[at], n_blk)
             for h in heads:
                 acc_ref[j, h] += mul(v_ref[ka, h * HEAD : (h + 1) * HEAD], weights[m * n_heads + h])
@@ -320,9 +323,7 @@
         for h in heads:
             at = slice(h * HEAD, (h + 1) * HEAD)
             total = jnp.sum(sum_ref[j, h], axis=0, keepdims=True)
-            out = acc_ref[j, h] / total
-            attf_ref[j, at] = out
-            att_ref[j, at] = out.astype(BF16)
+            att_ref[j, at] = (acc_ref[j, h] / total).astype(BF16)
             lse_ref[j, h : h + 1] = top_ref[j, h, 0:1] + jnp.log(total)
         return 0
 
@@ -334,8 +335,8 @@
     n_k, n_heads = kn.shape[:2]
     pairs = 0.56 * n * n_k
     count = n if n_k == n else 1
-    most = (n * (n + 1) // 2 if n_k == n else n_k) + 2
-    outs = [sds((n, wide, rows), BF16), sds((n, wide, rows), F32), sds((n, 8, rows), F32)]
+    most = (n * (n + 1) // 2 if n_k == n else n_k) + ATTEND_PAIRS
+    outs = [sds((n, wide, rows), BF16), sds((n, 8, rows), F32)]
 
     def some(shape):
         zeros = (0,) * (len(shape) - 1)
@@ -473,7 +474,7 @@
     )
 
 
-def mix_kernel(n_heads, meta, att_ref, attf_ref, cot_ref, mo_ref, w_ref, out_ref, do_ref, delta_ref, go_ref):
+def mix_kernel(n_heads, meta, att_ref, cot_ref, mo_ref, w_ref, out_ref, do_ref, delta_ref, go_ref):
     i = pl.program_id(0)
     w = w_ref[...]
     both = range(2)
@@ -484,7 +485,7 @@
     for b in both:
         out_ref[b] = (mo_ref[b].astype(F32) + outs[b]).astype(BF16)
         do_ref[b] = grads[b]
-        product = grads[b].astype(F32) * attf_ref[b]
+        product = grads[b].astype(F32) * att_ref[b].astype(F32)
         for h in range(n_heads):
             delta_ref[b, h : h + 1] = jnp.sum(product[h * HEAD : (h + 1) * HEAD], axis=0, keepdims=True)
 
@@ -497,7 +498,7 @@
         go_ref[...] += go
 
 
-def mix(meta, att, attf, cot, mo, w_out, after=()):
+def mix(meta, att, cot, mo, w_out, after=()):
     n, rows, width = cot.shape
     wide = att.shape[1]
     outs = [
@@ -511,8 +512,8 @@
         "mix",
         meta,
         (n // 2,),
-        [att, attf, cot, mo, w_out],
-        [rows_at(a.shape, 0, 2) for a in (att, attf, cot, mo)]
+        [att, cot, mo, w_out],
+        [rows_at(a.shape, 0, 2) for a in (att, cot, mo)]
         + [pl.BlockSpec((wide, width), lambda i, s: (s[QUARTER], 0))],
         outs,
         [rows_at(o.shape, 0, 2) for o in outs[:3]] + [whole((wide, width))],
@@ -535,18 +536,22 @@
     dv_ref[...] = jnp.zeros_like(dv_ref)
     found = list_pairs(meta, 0, n_q, rows, n_blk, n_docs, q_list, k_list)
 
-    q_list[found] = n_q - 1
-    k_list[found] = q_block(meta, n_q - 1, n_blk) + 1
+    for extra in range(BACK_PAIRS - 1):
+        q_list[found + extra] = n_q - 1
+        k_list[found + extra] = q_block(meta, n_q - 1, n_blk) + 1
+
+    def step_pairs(n):
+        return [BACK_PAIRS * n + e for e in range(BACK_PAIRS)]
 
     def parts(n):
-        for at in (2 * n, 2 * n + 1):
+        for at in step_pairs(n):
             j, ka = q_list[at], k_slot(meta, jnp.minimum(k_list[at], n_k - 1), n_blk)
             for m, h in enumerate(heads):
                 yield at, j, ka, m, h, spots[m]
 
     def weigh(n):
         slot = lax.rem(n, 2)
-        allowed = [seen(meta, k_list[at], q_block(meta, q_list[at], n_blk), rows, n_docs) for at in (2 * n, 2 * n + 1)]
+        allowed = [seen(meta, k_list[at], q_block(meta, q_list[at], n_blk), rows, n_docs) for at in step_pairs(n)]
         scores = [mul(kn_ref[ka, h], q_ref[j, at]) for _, j, ka, _, h, at in parts(n)]
         grads = [mul(vn_ref[ka, h], do_ref[j, at]) for _, j, ka, _, h, at in parts(n)]
         for c, (_, j, ka, m, h, at) in enumerate(parts(n)):
@@ -568,7 +573,7 @@
         weigh(n)
         return 0
 
-    steps = (found + 1) // 2
+    steps = (found + BACK_PAIRS - 1) // BACK_PAIRS
     lax.fori_loop(1, steps, both, 0)
     gather(steps - 1)
 
@@ -589,10 +594,10 @@
     lax.fori_loop(0, n_k, finish_k, 0)
     lax.fori_loop(0, n_q, finish_q, 0)
     if joins:
-        join_kernel(meta, jq_ref, jk_ref, jv_ref, *joins)
-
-
-def join_kernel(meta, jq_ref, jk_ref, jv_ref, normed_ref, x_ref, ngm_ref, w_ref, go_ref, ng_ref, sums_ref, *refs):
+        shard_kernel(meta, jq_ref, jk_ref, jv_ref, *joins)
+
+
+def shard_kernel(meta, jq_ref, jk_ref, jv_ref, normed_ref, go_ref, *refs):
     outs, all_ref = refs[:4], refs[4]
     wide = go_ref.shape[0]
     for third, ref in enumerate((jq_ref, jk_ref, jv_ref)):
@@ -602,35 +607,19 @@
         all_ref[third * wide : (third + 1) * wide] = total
     all_ref[3 * wide :] = go_ref[...]
     put_pieces(all_ref, meta, outs, 0)
-    sums_ref[...] = jnp.zeros_like(sums_ref)
-
-    def block(n, _):
-        for j in (2 * n, 2 * n + 1):
-            joined = jnp.concatenate([jq_ref[j], jk_ref[j], jv_ref[j]], axis=0)
-            ng = ngm_ref[j].astype(F32) + mul(joined, w_ref[...], TN)
-            ng_ref[j] = ng.astype(BF16)
-            x = x_ref[j].astype(F32)
-            centred = x - jnp.mean(x, axis=1, keepdims=True)
-            xhat = centred * lax.rsqrt(jnp.mean(centred * centred, axis=1, keepdims=True) + norm_eps)
-            sums_ref[0:1] += jnp.sum(ng * xhat, axis=0, keepdims=True)
-            sums_ref[1:2] += jnp.sum(ng, axis=0, keepdims=True)
-        return 0
-
-    lax.fori_loop(0, QUADS // 2, block, 0)
-
-
-def join_parts(normed, x, ngm, w_cut, grad_out):
+
+
+def shard_parts(normed, grad_out):
     wide, width = grad_out.shape
-    results = [sds(x.shape, BF16), sds((8, width), F32)] + [sds((1, wide, width), BF16)] * 4
-    return [normed, x, ngm, w_cut, grad_out], results, [pltpu.VMEM((4 * wide, width), F32)]
-
-
-def join(meta, grads, *rest):
-    operands, outs, scratch = join_parts(*rest)
+    return [normed, grad_out], [sds((1, wide, width), BF16)] * 4, [pltpu.VMEM((4 * wide, width), F32)]
+
+
+def shard(meta, grads, *rest):
+    operands, outs, scratch = shard_parts(*rest)
     operands = list(grads) + operands
     return call(
-        join_kernel,
-        "join",
+        shard_kernel,
+        "shard",
         meta,
         (1,),
         operands,
@@ -643,21 +632,62 @@
     )
 
 
+def join_kernel(meta, jq_ref, jk_ref, jv_ref, x_ref, ngm_ref, w_ref, ng_ref, sums_ref):
+    joined = [jnp.concatenate([jq_ref[b], jk_ref[b], jv_ref[b]], axis=0) for b in range(2)]
+    parts = [mul(j, w_ref[...], TN) for j in joined]
+    gain = bias = 0.0
+    for b in range(2):
+        ng = ngm_ref[b].astype(F32) + parts[b]
+        ng_ref[b] = ng.astype(BF16)
+        x = x_ref[b].astype(F32)
+        centred = x - jnp.mean(x, axis=1, keepdims=True)
+        xhat = centred * lax.rsqrt(jnp.mean(centred * centred, axis=1, keepdims=True) + norm_eps)
+        gain = gain + jnp.sum(ng * xhat, axis=0, keepdims=True)
+        bias = bias + jnp.sum(ng, axis=0, keepdims=True)
+
+    @pl.when(pl.program_id(0) == 0)
+    def _():
+        sums_ref[...] = jnp.zeros_like(sums_ref)
+
+    sums_ref[0:1] += gain
+    sums_ref[1:2] += bias
+
+
+def join(meta, grads, x, ngm, w_cut):
+    n, rows, width = x.shape
+    tiled = list(grads) + [x, ngm]
+    return call(
+        join_kernel,
+        "join",
+        meta,
+        (n // 2,),
+        tiled + [w_cut],
+        [rows_at(a.shape, 0, 2) for a in tiled] + [whole(w_cut.shape)],
+        [sds((n, rows, width), BF16), sds((16, width), F32)],
+        [rows_at(x.shape, 0, 2), whole((16, width))],
+        2 * n * rows * width * w_cut.shape[0],
+        10 * n * rows * width,
+    )
+
+
 def attend_back(meta, q, do, lse, delta, kn, vn, k, n_blk, n_docs, rest):
     n_q, wide, rows = q.shape
     n_k = k.shape[0]
     n_heads = wide // HEAD
     pairs = 0.56 * n_q * n_k
-    outs = [sds((n_q, wide, rows), BF16), sds((n_k, wide, rows), BF16), sds((n_k, wide, rows), BF16)]
-    grads = [pltpu.VMEM(o.shape, BF16) for o in outs] if rest else []
+    grads = [sds((n_q, wide, rows), BF16), sds((n_k, wide, rows), BF16), sds((n_k, wide, rows), BF16)]
     operands = [q, do, lse, delta, kn, vn, k]
-    scratch = []
+    outs, scratch = grads, []
     if rest:
-        more, outs, scratch = join_parts(*rest)
+        more, pieces, scratch = shard_parts(*rest)
         operands += more
+        outs = pieces + grads
 
     def body(meta_ref, *refs):
-        back_kernel(range(n_heads), n_blk, n_docs, n_q, n_k, meta_ref, *refs[: len(refs) - 7 - len(grads)], *refs[len(refs) - len(grads) :], *refs[len(refs) - 7 - len(grads) : len(refs) - len(grads)])
+        ins, refs = refs[: len(operands)], refs[len(operands) :]
+        given, held = refs[: len(outs)], refs[len(outs) :]
+        joins = ins[7:] + given[:-3] + held[: len(scratch)]
+        back_kernel(range(n_heads), n_blk, n_docs, n_q, n_k, meta_ref, *ins[:7], *joins, *given[-3:], *held[len(scratch) :])
 
     return call(
         body,
@@ -676,12 +706,11 @@
             pltpu.VMEM((n_q, n_heads, HEAD, rows), F32),
             pltpu.VMEM((n_k, n_heads, HEAD, rows), F32),
             pltpu.VMEM((n_k, n_heads, HEAD, rows), F32),
-            pltpu.VMEM((2, 2 * n_heads, rows, rows), BF16),
-            pltpu.VMEM((2, 2 * n_heads, rows, rows), BF16),
-            pltpu.SMEM((n_q * n_k + 2,), jnp.int32),
-            pltpu.SMEM((n_q * n_k + 2,), jnp.int32),
-        ]
-        + grads,
+            pltpu.VMEM((2, BACK_PAIRS * n_heads, rows, rows), BF16),
+            pltpu.VMEM((2, BACK_PAIRS * n_heads, rows, rows), BF16),
+            pltpu.SMEM((n_q * n_k + BACK_PAIRS,), jnp.int32),
+            pltpu.SMEM((n_q * n_k + BACK_PAIRS,), jnp.int32),
+        ],
     )
 
 
@@ -753,10 +782,11 @@
     yield [add(own, got).astype(BF16)]
 
 
-def sum_halves(own, n_blk):
+def sum_halves(own, sums, n_blk):
+    a, b = own.reshape(2, -1, own.shape[1])
+    own = jnp.stack([jnp.concatenate([sums, a]), jnp.concatenate([sums, b])])
     (got,) = yield [(own, "blk", n_blk // 2)]
-    total = add(own, got).astype(BF16)
-    yield from spread_pieces(total.reshape(2, -1, total.shape[1]))
+    yield from spread_pieces(add(own, got).astype(BF16))
 
 
 def spread_pieces(total):
@@ -777,29 +807,29 @@
 
 
 def fill_kernel(meta, *refs):
-    srcs, out_ref = refs[:8], refs[8]
-    rows = srcs[0].shape[2]
+    srcs, (up_ref, down_ref) = refs[:8], refs[8:]
+    rows = srcs[0].shape[3]
     for core in range(2):
 
         @pl.when(pl.program_id(0) // 2 == core)
         def _():
             for k in range(4):
                 for outer in range(2):
-                    at = pl.multiple_of(placed(k, outer, meta, rows), 16)
-                    out_ref[pl.ds(at, rows), :] = srcs[k + 4 * core][outer, 0].astype(F32)
-
-
-def fill(meta, arrays, shape):
-    _, _, rows, width = arrays[0].shape
-    across = shape[1] > shape[0]
-
-    def at(i, s):
-        shard = jnp.bitwise_xor(s[QUARTER], lax.rem(i, 2) * 2 + i // 2)
-        return (0, shard) if across else (shard, 0)
+                    at = pl.ds(pl.multiple_of(placed(k, outer, meta, rows), 16), rows)
+                    up_ref[at, :] = srcs[k + 4 * core][outer, 0, 0].astype(F32)
+                    down_ref[at, :] = srcs[k + 4 * core][outer, 0, 1].astype(F32)
+
+
+def fill(meta, arrays, shapes):
+    _, _, _, rows, width = arrays[0].shape
+
+    def shard(i, s):
+        return jnp.bitwise_xor(s[QUARTER], lax.rem(i, 2) * 2 + i // 2)
 
     def source(k):
-        return pl.BlockSpec((2, 1, rows, width), lambda i, s: (0, jnp.clip(i - 2 * (k // 4), 0, 1), 0, 0))
-
+        return pl.BlockSpec((2, 1, 2, rows, width), lambda i, s: (0, jnp.clip(i - 2 * (k // 4), 0, 1), 0, 0, 0))
+
+    block = (8 * rows, width)
     return call(
         fill_kernel,
         "fill",
@@ -807,16 +837,16 @@
         (TENSOR,),
         list(arrays),
         [source(k) for k in range(8)],
-        sds(shape, F32),
-        pl.BlockSpec((8 * rows, width), at),
+        [sds(shape, F32) for shape in shapes],
+        [pl.BlockSpec(block, lambda i, s: (0, shard(i, s))), pl.BlockSpec(block, lambda i, s: (shard(i, s), 0))],
         0,
-        6 * 8 * 4 * rows * width,
+        12 * 8 * 4 * rows * width,
     )
 
 
 def tail_kernel(wide, meta, *refs):
-    srcs, (gq_ref, go_ref, hold_ref) = refs[:8], refs[8:]
-    rows = srcs[0].shape[2]
+    srcs, (gq_ref, go_ref, gain_ref, bias_ref, hold_ref, part_ref) = refs[:8], refs[8:]
+    rows = srcs[0].shape[2] - 16
     i = pl.program_id(0)
 
     @pl.when(i == 0)
@@ -827,7 +857,14 @@
                 for rt1 in range(2):
                     shard = jnp.bitwise_xor(meta[QUARTER], rt1 * 2 + k // 4)
                     at = pl.multiple_of(shard * 4 * wide + row, 16)
-                    hold_ref[pl.ds(at, rows), :] = src[outer, rt1].astype(F32)
+                    hold_ref[pl.ds(at, rows), :] = src[outer, rt1, 16:].astype(F32)
+                    if k % 2 == 0:
+                        part_ref[shard * 4 + row // (2 * rows)] = src[outer, rt1, 0:16].astype(F32)
+        total = part_ref[0]
+        for n in range(1, 4 * TENSOR):
+            total = total + part_ref[n]
+        gain_ref[...] = total[0]
+        bias_ref[...] = total[1]
 
     def block(part):
         return jnp.concatenate([hold_ref[(4 * s + part) * wide : (4 * s + part + 1) * wide, :] for s in range(TENSOR)], axis=0)
@@ -844,7 +881,7 @@
 
 
 def tail(meta, arrays, width, wide):
-    outs = [sds((width, 3 * TENSOR * wide), F32), sds((TENSOR * wide, width), F32)]
+    outs = [sds((width, 3 * TENSOR * wide), F32), sds((TENSOR * wide, width), F32), sds((width,), F32), sds((width,), F32)]
     return call(
         partial(tail_kernel, wide),
         "tail",
@@ -853,10 +890,10 @@
         list(arrays),
         [once(a.shape) for a in arrays],
         outs,
-        [pl.BlockSpec((width, TENSOR * wide), lambda i, s: (0, jnp.minimum(i, 2))), whole(outs[1].shape)],
+        [pl.BlockSpec((width, TENSOR * wide), lambda i, s: (0, jnp.minimum(i, 2)))] + [whole(o.shape) for o in outs[1:]],
         0,
         6 * 4 * width * width,
-        scratch=[pltpu.VMEM((TENSOR * 4 * wide, width), F32)],
+        scratch=[pltpu.VMEM((TENSOR * 4 * wide, width), F32), pltpu.VMEM((4 * TENSOR, 16, width), F32)],
     )
 
 
@@ -944,81 +981,67 @@
     cot, mo, ngm, *mlp_parts = order.done(feed(meta, normed, order.hold(c_near.held + c_far.held), w_up, w_down))
     if fast:
         mlp = order.start(reduce_halves(mlp_parts, n_blk))
-    att, attf, lse = order.done(attend(meta, *order.hold([q]), kn, v, n_blk, n_docs))
+    att, lse = order.done(attend(meta, *order.hold([q]), kn, v, n_blk, n_docs))
     if fast:
         order.advance(mlp)
-    out_part, do, delta, grad_out_part = order.done(mix(meta, *order.hold([att, attf, cot, mo]), w_out))
+    out_part, do, delta, grad_out_part = order.done(mix(meta, *order.hold([att, cot, mo]), w_out))
     out_steps = order.start(scatter_blocks(out_part, n_blk))
     if fast:
         order.advance(mlp)
-    rest = (normed, x_all, ngm, w_cut, grad_out_part)
+    rest = (normed, grad_out_part)
     q, do = order.hold([q, do])
-    grads = order.done(attend_back(meta, q, do, lse, delta, kn, vn, k, n_blk, n_docs, rest if splits == 1 else None))
+    back = order.done(attend_back(meta, q, do, lse, delta, kn, vn, k, n_blk, n_docs, rest if splits == 1 else None))
+    rest_parts, grads = list(back[:-3]), list(back[-3:])
     if splits > 1:
-        grads = list(grads)
         for at, mask in [(at, mask) for at in (1, 2) for mask in s_masks]:
             count = grads[at].shape[0] // 2
             grads[at] = add(grads[at][:count], swap(grads[at][count:], "blk", n_blk, mask)).astype(BF16)
-        grads = order.done(join(meta, grads, *rest))
-    ng_part, sums, *rest_parts = grads
-
-    def gather_sums():
-        total = sums
-        for axis, mask in (("blk", 1), ("dp", 1), ("dp", 2), ("blk", 2), ("blk", n_blk // 2)):
-            (got,) = yield [(total, axis, mask)]
-            total = total + got
-        yield [total]
-
+        rest_parts = order.done(shard(meta, grads, *rest))
+    chains = {"O": out_steps}
     if fast:
-        order.advance(mlp)
-        (total,) = mlp.held
 
         def of_rest():
             (own,) = yield from reduce_pieces(rest_parts)
-            yield from sum_halves(own[0], n_blk)
-
-        makers = {
-            "Q": of_rest(),
-            "U": spread_pieces(total[:, 0]),
-            "D": spread_pieces(total[:, 1]),
-            "N": scatter_blocks(ng_part, n_blk),
-            "S": gather_sums(),
-            "O": out_steps,
-        }
-        chains = {"O": out_steps}
+            yield from sum_halves(own[0], sums.astype(BF16), n_blk)
+
+        order.advance(mlp)
+        chains["M"] = order.start(spread_pieces(mlp.held[0]))
+        chains["Q"] = order.start(of_rest())
+    order.advance(out_steps)
+    ng_part, sums = order.done(join(meta, order.hold(grads), x_all, ngm, w_cut))
+
+    def finish():
+        def ordered(own, other):
+            return jnp.where(half == 0, jnp.stack([own, other]), jnp.stack([other, own])).astype(F32)
+
+        output = (tokens.astype(F32) + ordered(*chains["O"].end())).astype(BF16)
+        normed_grad = ordered(*chains["N"].end())
+        x_rows = tokens.astype(F32)
+        centred = x_rows - jnp.mean(x_rows, axis=2, keepdims=True)
+        inverse = lax.rsqrt(jnp.mean(centred * centred, axis=2, keepdims=True) + norm_eps)
+        scaled = centred * inverse
+        scaled_grad = normed_grad * norm_gain.astype(F32)
+        input_grad = cotangent.astype(F32) + inverse * (
+            scaled_grad
+            - jnp.mean(scaled_grad, axis=2, keepdims=True)
+            - scaled * jnp.mean(scaled_grad * scaled, axis=2, keepdims=True)
+        )
+        return output, input_grad
+
+    if fast:
         for name in TAIL:
-            if name == "u":
-                grad_up = order.done(fill(meta, order.hold(chains["U"].end()), w_up.shape))
-            elif name == "d":
-                grad_down = order.done(fill(meta, order.hold(chains["D"].end()), w_down.shape))
+            if name == "m":
+                grad_up, grad_down = order.done(fill(meta, order.hold(chains["M"].end()), [w_up.shape, w_down.shape]))
+            elif name == "n":
+                output, input_grad = order.done(finish())
             elif name in chains:
                 order.advance(chains[name])
             else:
-                chains[name] = order.start(makers[name])
-        ng_steps, norm_steps, rest = (chains[name] for name in "NSQ")
+                chains[name] = order.start(scatter_blocks(ng_part, n_blk))
+        grad_qkv, grad_out, *norm_sums = tail(meta, chains["Q"].end(), width, wide)
     else:
-        ng_steps = order.start(scatter_blocks(ng_part, n_blk))
-
-    def ordered(own, other):
-        return jnp.where(half == 0, jnp.stack([own, other]), jnp.stack([other, own])).astype(F32)
-
-    output = (tokens.astype(F32) + ordered(*out_steps.end())).astype(BF16)
-    normed_grad = ordered(*ng_steps.end())
-    x_rows = tokens.astype(F32)
-    centred = x_rows - jnp.mean(x_rows, axis=2, keepdims=True)
-    inverse = lax.rsqrt(jnp.mean(centred * centred, axis=2, keepdims=True) + norm_eps)
-    scaled = centred * inverse
-    scaled_grad = normed_grad * norm_gain.astype(F32)
-    input_grad = cotangent.astype(F32) + inverse * (
-        scaled_grad
-        - jnp.mean(scaled_grad, axis=2, keepdims=True)
-        - scaled * jnp.mean(scaled_grad * scaled, axis=2, keepdims=True)
-    )
-
-    if fast:
-        grad_qkv, grad_out = tail(meta, rest.end(), width, wide)
-        (norm_sums,) = norm_steps.end()
-    else:
+        chains["N"] = order.start(scatter_blocks(ng_part, n_blk))
+        output, input_grad = finish()
         up, down = natural_halves(mlp_parts)
         (rest,) = natural(rest_parts)
         turn = rest[: 3 * wide].T.reshape(width, 3, wide)
@@ -1027,8 +1050,8 @@
         down = lax.dynamic_update_slice_in_dim(zeros(w_down.shape), down, quarter * inner, 0)
         turn = lax.dynamic_update_slice_in_dim(zeros((width, 3, TENSOR * wide)), turn, quarter * wide, 2)
         out = lax.dynamic_update_slice_in_dim(zeros(w_out.shape), rest[3 * wide :], quarter * wide, 0)
-        grads = lax.psum((up, down, turn, out), ("dp", "blk"))
-        grad_up, grad_down, turn, grad_out = (g.astype(F32) for g in grads)
+        summed = lax.psum((up, down, turn, out), ("dp", "blk"))
+        grad_up, grad_down, turn, grad_out = (g.astype(F32) for g in summed)
         grad_qkv = turn.reshape(w_qkv.shape)
         norm_sums = lax.psum(sums, ("dp", "blk"))
     return (output, input_grad, norm_sums[0], norm_sums[1], grad_qkv, grad_out, grad_up, grad_down)

time: 313 us -> 281 us (0.90)
  starting transfers between devices: 51.1 us -> 40.5 us
  other arithmetic: 17.8 us -> 9.64 us
  Pallas kernels: 131 us -> 124 us
  waiting for transfers between devices: 95.6 us -> 91.8 us
    ppermute x63 -> x49, starting transfers between devices: 51.1 us -> 40.5 us  [swap(): return lax.ppermute(x, axis, [(i, i ^ mask) for i in range(size)])]
    pallas_call x10, Pallas kernels: 131 us -> 124 us  [call(): pl.pallas_call(kernel, out_shape=out_shapes, grid_spec=pltpu.PrefetchScal...]
    another operation x12 -> x8, other arithmetic: 5.11 us -> 0.61 us  [spread_pieces(): two = [jnp.stack([pair_a, got_a]), jnp.stack([pair_b, got_b])]]
    ppermute x63 -> x49, waiting for transfers between devices: 95.6 us -> 91.8 us  [swap(): return lax.ppermute(x, axis, [(i, i ^ mask) for i in range(size)])]
  transfers between devices with their start and end apart: 63 -> 49, of which waited for: 25 -> 19; matrix products, arithmetic and copies ran while one was open for 8% -> 5% of each run, Pallas kernels for 31% -> 32%
where the time goes in v3:
time: 281 us; the launch traced here: 280 us
  Pallas kernels  124 us (44%)
  waiting for transfers between devices  91.8 us (33%)
  starting transfers between devices  40.5 us (14%)
  local copies, waits for them, and re-layouts  13 us (5%)
  other arithmetic  9.64 us (3%)
    pallas_call x10, Pallas kernels, call(): pl.pallas_call(kernel, out_shape=out_shapes, grid_spec=pltpu.PrefetchScal...  124 us
    ppermute x49, waiting for transfers between devices, swap(): return lax.ppermute(x, axis, [(i, i ^ mask) for i in range(size)])  91.8 us
    ppermute x49, starting transfers between devices, swap(): return lax.ppermute(x, axis, [(i, i ^ mask) for i in range(size)])  40.5 us
    unnamed x84, local copies, waits for them, and re-layouts  5.69 us
  transfers between devices with their start and end apart: 49, of which 19 were waited for; matrix products, arithmetic and copies ran while one was open for 5% of the time, Pallas kernels for 32%

profile of v3, /device:TPU:0, one launch (start us, length us, event | category | flops | bytes accessed | tf_op | source)
XLA Modules:
  0.0 280.2 jit_solution(7463344846557697604)
XLA Ops:
  2.2 3.1 %collective-permute-start.1 = (bf16[256,768]{1,0:T(8,128)(2,1)S(1)}, bf16[256,768]{1,0:T(8,128)(2,1)S(1)}, u32[]{:S(2)}, u32[]{:S(2)}) collective-permute-start(bf16[256,768]{1,0:T(8,128)(2,1)S(1)} %get-tuple-element.190.refs_0_), channel_id=1, source_target_pairs={{0,2},{1,3},{2,0},{3,1},{4,6},{5,7},{6,4},{7,5},{8,10},{9,11},{10,... | collective-permute-start | bytes 1179656 | tf_op jit(solution)/shard_map/ppermute | solution.py:718
  5.2 2.6 collective-permute-start
  8.7 4.0 %cut.1.refs_6_.refs_5_ = bf16[576,768]{1,0:T(8,128)(2,1)} custom-call(s32[9]{0:T(128)} %concatenate.15.meta_ref, bf16[768,2304]{1,0:T(8,128)(2,1)} %refs_2_.1, bf16[768,2304]{1,0:T(8,128)(2,1)} %refs_2_.1, bf16[768,2304]{1,0:T(8,128)(2,1)} %refs_2_.1), custom_call_target="tpu_custom_call" | custom-call | bytes 53084 | tf_op jit(solution)/shard_map/cut/pallas_call | solution.py:59
  12.7 9.0 %collective-permute-done.1.refs_1_ = bf16[256,768]{1,0:T(8,128)(2,1)S(1)} collective-permute-done((bf16[256,768]{1,0:T(8,128)(2,1)S(1)}, bf16[256,768]{1,0:T(8,128)(2,1)S(1)}, u32[]{:S(2)}, u32[]{:S(2)}) %collective-permute-start.1) | collective-permute-done | bytes 393248 | tf_op jit(solution)/shard_map/ppermute | solution.py:718
  21.8 4.3 %collective-permute-done.refs_0_ = bf16[256,768]{1,0:T(8,128)(2,1)S(1)} collective-permute-done((bf16[256,768]{1,0:T(8,128)(2,1)S(1)}, bf16[256,768]{1,0:T(8,128)(2,1)S(1)}, u32[]{:S(2)}, u32[]{:S(2)}) %collective-permute-start) | collective-permute-done | bytes 393248 | tf_op jit(solution)/shard_map/ppermute | solution.py:718
  26.2 3.0 %collective-permute-start.7 = (bf16[256,768]{1,0:T(8,128)(2,1)S(1)}, bf16[256,768]{1,0:T(8,128)(2,1)S(1)}, u32[]{:S(2)}, u32[]{:S(2)}) collective-permute-start(bf16[256,768]{1,0:T(8,128)(2,1)S(1)} %get-tuple-element.188), channel_id=1, source_target_pairs={{0,4},{1,5},{2,6},{3,7},{4,0},{5,1},{6,2},{7,3},{8,12},{9,13},{10,... | collective-permute-start | bytes 1179656 | tf_op jit(solution)/shard_map/ppermute | solution.py:718
  31.2 6.1 %project.2 = (bf16[8,256,768]{2,1,0:T(8,128)(2,1)}, bf16[8,256,768]{2,1,0:T(8,128)(2,1)}, bf16[8,192,256]{2,1,0:T(8,128)(2,1)}, bf16[8,192,256]{2,1,0:T(8,128)(2...) custom-call(s32[9]{0:T(128)} %concatenate.15.meta_ref, ...), custom_call_target="tpu_custom_call" | custom-call | flops 18119392 | bytes 157286 | tf_op jit(solution)/shard_map/project/pallas_call | solution.py:59
  37.3 6.8 %collective-permute-done.3.refs_1_ = bf16[256,768]{1,0:T(8,128)(2,1)S(1)} collective-permute-done((bf16[256,768]{1,0:T(8,128)(2,1)S(1)}, bf16[256,768]{1,0:T(8,128)(2,1)S(1)}, u32[]{:S(2)}, u32[]{:S(2)}) %collective-permute-start.3) | collective-permute-done | bytes 393248 | tf_op jit(solution)/shard_map/ppermute | solution.py:718
  44.6 2.9 %collective-permute-done.7.refs_4_ = bf16[256,768]{1,0:T(8,128)(2,1)S(1)} collective-permute-done((bf16[256,768]{1,0:T(8,128)(2,1)S(1)}, bf16[256,768]{1,0:T(8,128)(2,1)S(1)}, u32[]{:S(2)}, u32[]{:S(2)}) %collective-permute-start.7) | collective-permute-done | bytes 393248 | tf_op jit(solution)/shard_map/ppermute | solution.py:718
  48.3 6.1 %project.3 = (bf16[8,256,768]{2,1,0:T(8,128)(2,1)}, bf16[8,256,768]{2,1,0:T(8,128)(2,1)}, bf16[8,192,256]{2,1,0:T(8,128)(2,1)}, bf16[8,192,256]{2,1,0:T(8,128)(2...) custom-call(s32[9]{0:T(128)} %concatenate.15.meta_ref, ...), custom_call_target="tpu_custom_call", output_to_operand_aliasing={{0}: (8, {}), {1}: (9, {}), {2}: (10, {}), {3}: (11, {}), {... | custom-call | flops 18119392 | bytes 157286 | tf_op jit(solution)/shard_map/project/pallas_call | solution.py:59
  54.5 1.7 collective-permute-done.8.refs_1_
  56.2 8.1 %collective-permute-done.11.refs_5_ = bf16[256,768]{1,0:T(8,128)(2,1)S(1)} collective-permute-done((bf16[256,768]{1,0:T(8,128)(2,1)S(1)}, bf16[256,768]{1,0:T(8,128)(2,1)S(1)}, u32[]{:S(2)}, u32[]{:S(2)}) %collective-permute-start.11) | collective-permute-done | bytes 393248 | tf_op jit(solution)/shard_map/ppermute | solution.py:718
  67.4 24.6 %feed.1 = (bf16[8,256,768]{2,1,0:T(8,128)(2,1)}, bf16[8,256,768]{2,1,0:T(8,128)(2,1)}, bf16[8,256,768]{2,1,0:T(8,128)(2,1)}, bf16[2,2,96,768]{3,2,1,0:T(8,128)(2...) custom-call(s32[9]{0:T(128)} %concatenate.15.meta_ref, ...), custom_call_target="tpu_custom_call" | custom-call | flops 289910304 | bytes 346030 | tf_op jit(solution)/shard_map/feed/pallas_call | solution.py:59
  95.1 14.4 %attend.1 = (bf16[8,192,256]{2,1,0:T(8,128)(2,1)}, f32[8,8,256]{2,1,0:T(8,128)}) custom-call(s32[9]{0:T(128)} %concatenate.15.meta_ref, bf16[8,192,256]{2,1,0:T(8,128)(2,1)} %get-tuple-element.258.refs_0_, bf16[8,3,256,64]{3,2,1,0:T(8,128)(2,1)} %get-tuple-element.239.refs_1_.refs_4_, bf16[8,192,256]{2,1,0:T(8,128)(2,1)} %get-tuple-element.240.refs_2_), custom_call_target="tpu_custom_call" | custom-call | flops 72155448 | bytes 125829 | tf_op jit(solution)/shard_map/attend/pallas_call | solution.py:59
  111.8 8.1 %mix.1 = (bf16[8,256,768]{2,1,0:T(8,128)(2,1)}, bf16[8,192,256]{2,1,0:T(8,128)(2,1)}, f32[8,8,256]{2,1,0:T(8,128)}, f32[192,768]{1,0:T(8,128)}) custom-call(s32[9]{0:T(128)} %concatenate.15.meta_ref, bf16[8,192,256]{2,1,0:T(8,128)(2,1)} %get-tuple-element.249.refs_0_, bf16[8,256,768]{2,1,0:T(8,128)(2,1)} %get-tuple-element.250.refs_1_, ...), custom_call_target="tpu_custom_call" | custom-call | flops 36238784 | bytes 314572 | tf_op jit(solution)/shard_map/mix/pallas_call | solution.py:59
  122.2 31.3 %attend_back.1 = (bf16[1,192,768]{2,1,0:T(8,128)(2,1)}, bf16[1,192,768]{2,1,0:T(8,128)(2,1)}, bf16[1,192,768]{2,1,0:T(8,128)(2,1)}, bf16[1,192,768]{2,1,0:T(8,12...) custom-call(s32[9]{0:T(128)} %concatenate.15.meta_ref, ...), custom_call_target="tpu_custom_call" | custom-call | flops 180388624 | bytes 125829 | tf_op jit(solution)/shard_map/attend_back/pallas_call | solution.py:59
  153.7 2.4 collective-permute-start.24
  159.6 1.7 add_convert_fusion.3
  161.5 8.8 %join.1 = (bf16[8,256,768]{2,1,0:T(8,128)(2,1)}, f32[16,768]{1,0:T(8,128)}) custom-call(s32[9]{0:T(128)} %concatenate.15.meta_ref, bf16[8,192,256]{2,1,0:T(8,128)(2,1)} %get-tuple-element.279.refs_0_, bf16[8,192,256]{2,1,0:T(8,128)(2,1)} %get-tuple-element.280.refs_1_, bf16[8,192,256]{2,1,0:T(8,128)(2,1)} %get-tuple-element.281.refs_2_, ...), custom_call_target="tpu_custom_call" | custom-call | flops 36238784 | bytes 314572 | tf_op jit(solution)/shard_map/join/pallas_call | solution.py:59
  176.1 2.3 collective-permute-start.27
  179.1 9.0 %collective-permute-done.28 = bf16[2,2,96,768]{3,2,1,0:T(8,128)(2,1)S(1)} collective-permute-done((bf16[2,2,96,768]{3,2,1,0:T(8,128)(2,1)S(1)}, bf16[2,2,96,768]{3,2,1,0:T(8,128)(2,1)S(1)}, u32[]{:S(2)}, u32[]{:S(2)}) %collective-permute-start.28) | collective-permute-done | bytes 589856 | tf_op jit(solution)/shard_map/ppermute | solution.py:718
  194.3 8.2 %collective-permute-done.31 = bf16[2,112,768]{2,1,0:T(8,128)(2,1)S(1)} collective-permute-done((bf16[2,112,768]{2,1,0:T(8,128)(2,1)S(1)}, bf16[2,112,768]{2,1,0:T(8,128)(2,1)S(1)}, u32[]{:S(2)}, u32[]{:S(2)}) %collective-permute-start.31) | collective-permute-done | bytes 344096 | tf_op jit(solution)/shard_map/ppermute | solution.py:718
  202.6 1.7 collective-permute-start.32
  204.4 12.0 %collective-permute-done.33.refs_2_ = bf16[2,2,2,96,768]{4,3,2,1,0:T(8,128)(2,1)} collective-permute-done((bf16[2,2,2,96,768]{4,3,2,1,0:T(8,128)(2,1)S(1)}, bf16[2,2,2,96,768]{4,3,2,1,0:T(8,128)(2,1)}, u32[]{:S(2)}, u32[]{:S(2)}) %collective-permute-start.33) | collective-permute-done | bytes 1179680 | tf_op jit(solution)/shard_map/ppermute | solution.py:718
  220.9 4.0 %collective-permute-done.41 = bf16[2,112,768]{2,1,0:T(8,128)(2,1)S(1)} collective-permute-done((bf16[2,112,768]{2,1,0:T(8,128)(2,1)S(1)}, bf16[2,112,768]{2,1,0:T(8,128)(2,1)S(1)}, u32[]{:S(2)}, u32[]{:S(2)}) %collective-permute-start.41) | collective-permute-done | bytes 344096 | tf_op jit(solution)/shard_map/ppermute | solution.py:718
  226.8 2.3 collective-permute-start.25
  229.3 14.0 %collective-permute-done.25 = bf16[256,768]{1,0:T(8,128)(2,1)S(1)} collective-permute-done((bf16[256,768]{1,0:T(8,128)(2,1)S(1)}, bf16[256,768]{1,0:T(8,128)(2,1)S(1)}, u32[]{:S(2)}, u32[]{:S(2)}) %collective-permute-start.25) | collective-permute-done | bytes 393248 | tf_op jit(solution)/shard_map/ppermute | solution.py:718
  247.2 1.7 collective-permute-start.38
  250.0 11.4 %fill.1 = (f32[768,3072]{1,0:T(8,128)}, f32[3072,768]{1,0:T(8,128)}) custom-call(s32[9]{0:T(128)} %concatenate.15.meta_ref, bf16[2,2,2,96,768]{4,3,2,1,0:T(8,128)(2,1)} %copy-done.1, bf16[2,2,2,96,768]{4,3,2,1,0:T(8,128)(2,1)} %copy-done.2, bf16[2,2,2,96,768]{4,3,2,1,0:T(8,128)(2,1)} %collective-permute-done.33.refs_2_, ...), custom_call_target="tpu_custom_call" | custom-call | bytes 566231 | tf_op jit(solution)/shard_map/fill/pallas_call | solution.py:59
  261.5 5.1 %collective-permute-done.37 = bf16[256,768]{1,0:T(8,128)(2,1)S(1)} collective-permute-done((bf16[256,768]{1,0:T(8,128)(2,1)}, bf16[256,768]{1,0:T(8,128)(2,1)S(1)}, u32[]{:S(2)}, u32[]{:S(2)}) %collective-permute-start.37) | collective-permute-done | bytes 393248 | tf_op jit(solution)/shard_map/ppermute | solution.py:718
  268.0 2.0 fusion.7
  271.1 9.1 %tail.1 = (f32[768,2304]{1,0:T(8,128)}, f32[768,768]{1,0:T(8,128)}, f32[768]{0:T(1024)}, f32[768]{0:T(1024)}) custom-call(s32[9]{0:T(128)} %concatenate.15.meta_ref, bf16[2,2,112,768]{3,2,1,0:T(8,128)(2,1)} %copy-done.10, bf16[2,2,112,768]{3,2,1,0:T(8,128)(2,1)} %copy-done.11, bf16[2,2,112,768]{3,2,1,0:T(8,128)(2,1)} %copy-done.16, ...), custom_call_target="tpu_custom_call" | custom-call | bytes 283115 | tf_op jit(solution)/shard_map/tail/pallas_call | solution.py:59
  (216 shorter events, 46.8 us)
Async XLA Ops:
  2.2 19.6 %collective-permute-start.1 = (bf16[256,768]{1,0:T(8,128)(2,1)S(1)}, bf16[256,768]{1,0:T(8,128)(2,1)S(1)}, u32[]{:S(2)}, u32[]{:S(2)}) collective-permute-start(bf16[256,768]{1,0:T(8,128)(2,1)S(1)} %get-tuple-element.190.refs_0_), channel_id=1, source_target_pairs={{0,2},{1,3},{2,0},{3,1},{4,6},{5,7},{6,4},{7,5},{8,10},{9,11},{10,... | collective-permute-start | bytes 1179656 | tf_op jit(solution)/shard_map/ppermute | solution.py:718
  5.2 16.5 %collective-permute-start.2 = (bf16[256,768]{1,0:T(8,128)(2,1)S(1)}, bf16[256,768]{1,0:T(8,128)(2,1)S(1)}, u32[]{:S(2)}, u32[]{:S(2)}) collective-permute-start(bf16[256,768]{1,0:T(8,128)(2,1)S(1)} %get-tuple-element.190.refs_0_), channel_id=1, source_target_pairs={{0,1},{1,0},{2,3},{3,2},{4,5},{5,4},{6,7},{7,6},{8,9},{9,8},{10,11... | collective-permute-start | bytes 1179656 | tf_op jit(solution)/shard_map/ppermute | solution.py:718
  5.2 20.9 %collective-permute-start = (bf16[256,768]{1,0:T(8,128)(2,1)S(1)}, bf16[256,768]{1,0:T(8,128)(2,1)S(1)}, u32[]{:S(2)}, u32[]{:S(2)}) collective-permute-start(bf16[256,768]{1,0:T(8,128)(2,1)S(1)} %get-tuple-element.388), channel_id=1, source_target_pairs={{0,4},{1,5},{2,6},{3,7},{4,0},{5,1},{6,2},{7,3},{8,12},{9,13},{10,... | collective-permute-start | bytes 1179656 | tf_op jit(solution)/shard_map/ppermute | solution.py:718
  26.1 17.9 %collective-permute-start.3 = (bf16[256,768]{1,0:T(8,128)(2,1)S(1)}, bf16[256,768]{1,0:T(8,128)(2,1)S(1)}, u32[]{:S(2)}, u32[]{:S(2)}) collective-permute-start(bf16[256,768]{1,0:T(8,128)(2,1)S(1)} %collective-permute-done.refs_0_), channel_id=1, source_target_pairs={{0,2},{1,3},{2,0},{3,1},{4,6},{5,7},{6,4},{7,5},{8,10},{9,11},{10,... | collective-permute-start | bytes 1179656 | tf_op jit(solution)/shard_map/ppermute | solution.py:718
  26.1 17.9 %collective-permute-start.4 = (bf16[256,768]{1,0:T(8,128)(2,1)S(1)}, bf16[256,768]{1,0:T(8,128)(2,1)S(1)}, u32[]{:S(2)}, u32[]{:S(2)}) collective-permute-start(bf16[256,768]{1,0:T(8,128)(2,1)S(1)} %collective-permute-done.refs_0_), channel_id=1, source_target_pairs={{0,1},{1,0},{2,3},{3,2},{4,5},{5,4},{6,7},{7,6},{8,9},{9,8},{10,11... | collective-permute-start | bytes 1179656 | tf_op jit(solution)/shard_map/ppermute | solution.py:718
  26.2 21.3 %collective-permute-start.7 = (bf16[256,768]{1,0:T(8,128)(2,1)S(1)}, bf16[256,768]{1,0:T(8,128)(2,1)S(1)}, u32[]{:S(2)}, u32[]{:S(2)}) collective-permute-start(bf16[256,768]{1,0:T(8,128)(2,1)S(1)} %get-tuple-element.188), channel_id=1, source_target_pairs={{0,4},{1,5},{2,6},{3,7},{4,0},{5,1},{6,2},{7,3},{8,12},{9,13},{10,... | collective-permute-start | bytes 1179656 | tf_op jit(solution)/shard_map/ppermute | solution.py:718
  47.5 16.8 %collective-permute-start.11 = (bf16[256,768]{1,0:T(8,128)(2,1)S(1)}, bf16[256,768]{1,0:T(8,128)(2,1)S(1)}, u32[]{:S(2)}, u32[]{:S(2)}) collective-permute-start(bf16[256,768]{1,0:T(8,128)(2,1)S(1)} %collective-permute-done.7.refs_4_), channel_id=1, source_target_pairs={{0,2},{1,3},{2,0},{3,1},{4,6},{5,7},{6,4},{7,5},{8,10},{9,11},{10,... | collective-permute-start | bytes 1179656 | tf_op jit(solution)/shard_map/ppermute | solution.py:718
  47.5 16.8 %collective-permute-start.12 = (bf16[256,768]{1,0:T(8,128)(2,1)S(1)}, bf16[256,768]{1,0:T(8,128)(2,1)S(1)}, u32[]{:S(2)}, u32[]{:S(2)}) collective-permute-start(bf16[256,768]{1,0:T(8,128)(2,1)S(1)} %collective-permute-done.7.refs_4_), channel_id=1, source_target_pairs={{0,1},{1,0},{2,3},{3,2},{4,5},{5,4},{6,7},{7,6},{8,9},{9,8},{10,11... | collective-permute-start | bytes 1179656 | tf_op jit(solution)/shard_map/ppermute | solution.py:718
  92.0 17.5 %collective-permute-start.14 = (bf16[2,2,96,768]{3,2,1,0:T(8,128)(2,1)}, bf16[2,2,96,768]{3,2,1,0:T(8,128)(2,1)S(1)}, u32[]{:S(2)}, u32[]{:S(2)}) collective-permute-start(bf16[2,2,96,768]{3,2,1,0:T(8,128)(2,1)} %get-tuple-element.236), channel_id=1, source_target_pairs={{0,8},{8,0},{16,24},{24,16},{1,9},{9,1},{17,25},{25,17},{2,10},{10... | collective-permute-start | bytes 1769480 | tf_op jit(solution)/shard_map/ppermute | solution.py:718
  93.6 15.9 %collective-permute-start.15 = (bf16[2,2,96,768]{3,2,1,0:T(8,128)(2,1)}, bf16[2,2,96,768]{3,2,1,0:T(8,128)(2,1)S(1)}, u32[]{:S(2)}, u32[]{:S(2)}) collective-permute-start(bf16[2,2,96,768]{3,2,1,0:T(8,128)(2,1)} %get-tuple-element.237), channel_id=1, source_target_pairs={{0,16},{8,24},{16,0},{24,8},{1,17},{9,25},{17,1},{25,9},{2,18},{10... | collective-permute-start | bytes 1769480 | tf_op jit(solution)/shard_map/ppermute | solution.py:718
  121.5 38.0 %collective-permute-start.16 = (bf16[4,256,768]{2,1,0:T(8,128)(2,1)S(1)}, bf16[4,256,768]{2,1,0:T(8,128)(2,1)}, u32[]{:S(2)}, u32[]{:S(2)}) collective-permute-start(bf16[4,256,768]{2,1,0:T(8,128)(2,1)S(1)} %pad_maximum_fusion), channel_id=1, source_target_pairs={{0,1},{1,0},{2,3},{3,2},{4,5},{5,4},{6,7},{7,6},{8,9},{9,8},{10,11... | collective-permute-start | bytes 4718600 | tf_op jit(solution)/shard_map/ppermute | solution.py:718
  121.9 31.7 %collective-permute-start.19 = (bf16[2,2,96,768]{3,2,1,0:T(8,128)(2,1)S(1)}, bf16[2,2,96,768]{3,2,1,0:T(8,128)(2,1)S(1)}, u32[]{:S(2)}, u32[]{:S(2)}) collective-permute-start(bf16[2,2,96,768]{3,2,1,0:T(8,128)(2,1)S(1)} %pad_maximum_fusion.6), channel_id=1, source_target_pairs={{0,4},{1,5},{2,6},{3,7},{4,0},{5,1},{6,2},{7,3},{8,12},{9,13},{10,... | collective-permute-start | bytes 1769480 | tf_op jit(solution)/shard_map/ppermute | solution.py:718
  153.7 18.3 %collective-permute-start.24 = (bf16[2,2,96,768]{3,2,1,0:T(8,128)(2,1)S(1)}, bf16[2,2,96,768]{3,2,1,0:T(8,128)(2,1)S(1)}, u32[]{:S(2)}, u32[]{:S(2)}) collective-permute-start(bf16[2,2,96,768]{3,2,1,0:T(8,128)(2,1)S(1)} %add_convert_fusion.4), channel_id=1, source_target_pairs={{0,2},{1,3},{2,0},{3,1},{4,6},{5,7},{6,4},{7,5},{8,10},{9,11},{10,... | collective-permute-start | bytes 1769480 | tf_op jit(solution)/shard_map/ppermute | solution.py:718
  156.0 16.7 %collective-permute-start.21 = (bf16[1,192,768]{2,1,0:T(8,128)(2,1)}, bf16[1,192,768]{2,1,0:T(8,128)(2,1)S(1)}, u32[]{:S(2)}, u32[]{:S(2)}) collective-permute-start(bf16[1,192,768]{2,1,0:T(8,128)(2,1)} %get-tuple-element.271), channel_id=1, source_target_pairs={{0,8},{8,0},{16,24},{24,16},{1,9},{9,1},{17,25},{25,17},{2,10},{10... | collective-permute-start | bytes 884744 | tf_op jit(solution)/shard_map/ppermute | solution.py:718
  157.5 16.8 %collective-permute-start.22 = (bf16[1,192,768]{2,1,0:T(8,128)(2,1)}, bf16[1,192,768]{2,1,0:T(8,128)(2,1)S(1)}, u32[]{:S(2)}, u32[]{:S(2)}) collective-permute-start(bf16[1,192,768]{2,1,0:T(8,128)(2,1)} %get-tuple-element.272), channel_id=1, source_target_pairs={{0,16},{8,24},{16,0},{24,8},{1,17},{9,25},{17,1},{25,9},{2,18},{10... | collective-permute-start | bytes 884744 | tf_op jit(solution)/shard_map/ppermute | solution.py:718
  159.1 16.8 %collective-permute-start.23 = (bf16[1,192,768]{2,1,0:T(8,128)(2,1)}, bf16[1,192,768]{2,1,0:T(8,128)(2,1)S(1)}, u32[]{:S(2)}, u32[]{:S(2)}) collective-permute-start(bf16[1,192,768]{2,1,0:T(8,128)(2,1)} %get-tuple-element.273), channel_id=1, source_target_pairs={{0,24},{8,16},{16,8},{24,0},{1,25},{9,17},{17,9},{25,1},{2,26},{10... | collective-permute-start | bytes 884744 | tf_op jit(solution)/shard_map/ppermute | solution.py:718
  161.4 17.1 %collective-permute-start.20 = (bf16[256,768]{1,0:T(8,128)(2,1)S(1)}, bf16[256,768]{1,0:T(8,128)(2,1)S(1)}, u32[]{:S(2)}, u32[]{:S(2)}) collective-permute-start(bf16[256,768]{1,0:T(8,128)(2,1)S(1)} %slice_bitcast_fusion.5), channel_id=1, source_target_pairs={{0,2},{1,3},{2,0},{3,1},{4,6},{5,7},{6,4},{7,5},{8,10},{9,11},{10,... | collective-permute-start | bytes 1179656 | tf_op jit(solution)/shard_map/ppermute | solution.py:718
  176.1 17.8 %collective-permute-start.27 = (bf16[2,112,768]{2,1,0:T(8,128)(2,1)S(1)}, bf16[2,112,768]{2,1,0:T(8,128)(2,1)S(1)}, u32[]{:S(2)}, u32[]{:S(2)}) collective-permute-start(bf16[2,112,768]{2,1,0:T(8,128)(2,1)S(1)} %pad_maximum_fusion.9), channel_id=1, source_target_pairs={{0,4},{1,5},{2,6},{3,7},{4,0},{5,1},{6,2},{7,3},{8,12},{9,13},{10,... | collective-permute-start | bytes 1032200 | tf_op jit(solution)/shard_map/ppermute | solution.py:718
  189.6 26.9 %collective-permute-start.33 = (bf16[2,2,2,96,768]{4,3,2,1,0:T(8,128)(2,1)S(1)}, bf16[2,2,2,96,768]{4,3,2,1,0:T(8,128)(2,1)}, u32[]{:S(2)}, u32[]{:S(2)}) collective-permute-start(bf16[2,2,2,96,768]{4,3,2,1,0:T(8,128)(2,1)S(1)} %pad_maximum_fusion.2.refs_0_), channel_id=1, source_target_pairs={{0,16},{8,24},{16,0},{24,8},{1,17},{9,25},{17,1},{25,9},{2,18},{10... | collective-permute-start | bytes 3538952 | tf_op jit(solution)/shard_map/ppermute | solution.py:718
  191.1 27.1 %collective-permute-start.34 = (bf16[2,2,2,96,768]{4,3,2,1,0:T(8,128)(2,1)S(1)}, bf16[2,2,2,96,768]{4,3,2,1,0:T(8,128)(2,1)}, u32[]{:S(2)}, u32[]{:S(2)}) collective-permute-start(bf16[2,2,2,96,768]{4,3,2,1,0:T(8,128)(2,1)S(1)} %pad_maximum_fusion.3.refs_1_), channel_id=1, source_target_pairs={{0,8},{8,0},{16,24},{24,16},{1,9},{9,1},{17,25},{25,17},{2,10},{10... | collective-permute-start | bytes 3538952 | tf_op jit(solution)/shard_map/ppermute | solution.py:718
  191.7 27.7 %collective-permute-start.35 = (bf16[2,2,2,96,768]{4,3,2,1,0:T(8,128)(2,1)S(1)}, bf16[2,2,2,96,768]{4,3,2,1,0:T(8,128)(2,1)S(1)}, u32[]{:S(2)}, u32[]{:S(2)}) collective-permute-start(bf16[2,2,2,96,768]{4,3,2,1,0:T(8,128)(2,1)S(1)} %pad_maximum_fusion.2.refs_0_), channel_id=1, source_target_pairs={{0,1},{1,0},{2,3},{3,2},{4,5},{5,4},{6,7},{7,6},{8,9},{9,8},{10,11... | collective-permute-start | bytes 3538952 | tf_op jit(solution)/shard_map/ppermute | solution.py:718
  191.7 27.7 %collective-permute-start.36 = (bf16[2,2,2,96,768]{4,3,2,1,0:T(8,128)(2,1)S(1)}, bf16[2,2,2,96,768]{4,3,2,1,0:T(8,128)(2,1)S(1)}, u32[]{:S(2)}, u32[]{:S(2)}) collective-permute-start(bf16[2,2,2,96,768]{4,3,2,1,0:T(8,128)(2,1)S(1)} %pad_maximum_fusion.3.refs_1_), channel_id=1, source_target_pairs={{0,1},{1,0},{2,3},{3,2},{4,5},{5,4},{6,7},{7,6},{8,9},{9,8},{10,11... | collective-permute-start | bytes 3538952 | tf_op jit(solution)/shard_map/ppermute | solution.py:718
  202.6 17.4 %collective-permute-start.32 = (bf16[256,768]{1,0:T(8,128)(2,1)S(1)}, bf16[256,768]{1,0:T(8,128)(2,1)S(1)}, u32[]{:S(2)}, u32[]{:S(2)}) collective-permute-start(bf16[256,768]{1,0:T(8,128)(2,1)S(1)} %slice_bitcast_fusion.3), channel_id=1, source_target_pairs={{0,2},{1,3},{2,0},{3,1},{4,6},{5,7},{6,4},{7,5},{8,10},{9,11},{10,... | collective-permute-start | bytes 1179656 | tf_op jit(solution)/shard_map/ppermute | solution.py:718
  219.4 27.0 %collective-permute-start.39 = (bf16[2,2,2,96,768]{4,3,2,1,0:T(8,128)(2,1)}, bf16[2,2,2,96,768]{4,3,2,1,0:T(8,128)(2,1)}, u32[]{:S(2)}, u32[]{:S(2)}) collective-permute-start(bf16[2,2,2,96,768]{4,3,2,1,0:T(8,128)(2,1)} %collective-permute-done.33.refs_2_), channel_id=1, source_target_pairs={{0,1},{1,0},{2,3},{3,2},{4,5},{5,4},{6,7},{7,6},{8,9},{9,8},{10,11... | collective-permute-start | bytes 3538952 | tf_op jit(solution)/shard_map/ppermute | solution.py:718
  219.5 27.7 %collective-permute-start.40 = (bf16[2,2,2,96,768]{4,3,2,1,0:T(8,128)(2,1)}, bf16[2,2,2,96,768]{4,3,2,1,0:T(8,128)(2,1)}, u32[]{:S(2)}, u32[]{:S(2)}) collective-permute-start(bf16[2,2,2,96,768]{4,3,2,1,0:T(8,128)(2,1)} %collective-permute-done.34.refs_3_), channel_id=1, source_target_pairs={{0,1},{1,0},{2,3},{3,2},{4,5},{5,4},{6,7},{7,6},{8,9},{9,8},{10,11... | collective-permute-start | bytes 3538952 | tf_op jit(solution)/shard_map/ppermute | solution.py:718
  225.7 19.0 %collective-permute-start.43 = (bf16[2,2,112,768]{3,2,1,0:T(8,128)(2,1)S(1)}, bf16[2,2,112,768]{3,2,1,0:T(8,128)(2,1)S(1)}, u32[]{:S(2)}, u32[]{:S(2)}) collective-permute-start(bf16[2,2,112,768]{3,2,1,0:T(8,128)(2,1)S(1)} %pad_maximum_fusion.4.refs_0_), channel_id=1, source_target_pairs={{0,16},{8,24},{16,0},{24,8},{1,17},{9,25},{17,1},{25,9},{2,18},{10... | collective-permute-start | bytes 2064392 | tf_op jit(solution)/shard_map/ppermute | solution.py:718
  226.8 16.6 %collective-permute-start.25 = (bf16[256,768]{1,0:T(8,128)(2,1)S(1)}, bf16[256,768]{1,0:T(8,128)(2,1)S(1)}, u32[]{:S(2)}, u32[]{:S(2)}) collective-permute-start(bf16[256,768]{1,0:T(8,128)(2,1)S(1)} %fusion.13), channel_id=1, source_target_pairs={{0,4},{1,5},{2,6},{3,7},{4,0},{5,1},{6,2},{7,3},{8,12},{9,13},{10,... | collective-permute-start | bytes 1179656 | tf_op jit(solution)/shard_map/ppermute | solution.py:718
  243.4 18.1 %collective-permute-start.44 = (bf16[2,2,112,768]{3,2,1,0:T(8,128)(2,1)S(1)}, bf16[2,2,112,768]{3,2,1,0:T(8,128)(2,1)}, u32[]{:S(2)}, u32[]{:S(2)}) collective-permute-start(bf16[2,2,112,768]{3,2,1,0:T(8,128)(2,1)S(1)} %pad_maximum_fusion.5.refs_1_), channel_id=1, source_target_pairs={{0,8},{8,0},{16,24},{24,16},{1,9},{9,1},{17,25},{25,17},{2,10},{10... | collective-permute-start | bytes 2064392 | tf_op jit(solution)/shard_map/ppermute | solution.py:718
  244.7 16.9 %collective-permute-start.45 = (bf16[2,2,112,768]{3,2,1,0:T(8,128)(2,1)S(1)}, bf16[2,2,112,768]{3,2,1,0:T(8,128)(2,1)}, u32[]{:S(2)}, u32[]{:S(2)}) collective-permute-start(bf16[2,2,112,768]{3,2,1,0:T(8,128)(2,1)S(1)} %pad_maximum_fusion.4.refs_0_), channel_id=1, source_target_pairs={{0,1},{1,0},{2,3},{3,2},{4,5},{5,4},{6,7},{7,6},{8,9},{9,8},{10,11... | collective-permute-start | bytes 2064392 | tf_op jit(solution)/shard_map/ppermute | solution.py:718
  245.6 16.0 %collective-permute-start.46 = (bf16[2,2,112,768]{3,2,1,0:T(8,128)(2,1)S(1)}, bf16[2,2,112,768]{3,2,1,0:T(8,128)(2,1)}, u32[]{:S(2)}, u32[]{:S(2)}) collective-permute-start(bf16[2,2,112,768]{3,2,1,0:T(8,128)(2,1)S(1)} %pad_maximum_fusion.5.refs_1_), channel_id=1, source_target_pairs={{0,1},{1,0},{2,3},{3,2},{4,5},{5,4},{6,7},{7,6},{8,9},{9,8},{10,11... | collective-permute-start | bytes 2064392 | tf_op jit(solution)/shard_map/ppermute | solution.py:718
  246.4 20.2 %collective-permute-start.37 = (bf16[256,768]{1,0:T(8,128)(2,1)}, bf16[256,768]{1,0:T(8,128)(2,1)S(1)}, u32[]{:S(2)}, u32[]{:S(2)}) collective-permute-start(bf16[256,768]{1,0:T(8,128)(2,1)} %fusion.11), channel_id=1, source_target_pairs={{0,4},{1,5},{2,6},{3,7},{4,0},{5,1},{6,2},{7,3},{8,12},{9,13},{10,... | collective-permute-start | bytes 1179656 | tf_op jit(solution)/shard_map/ppermute | solution.py:718
  247.2 19.4 %collective-permute-start.38 = (bf16[256,768]{1,0:T(8,128)(2,1)}, bf16[256,768]{1,0:T(8,128)(2,1)S(1)}, u32[]{:S(2)}, u32[]{:S(2)}) collective-permute-start(bf16[256,768]{1,0:T(8,128)(2,1)} %slice_bitcast_fusion), channel_id=1, source_target_pairs={{0,2},{1,3},{2,0},{3,1},{4,6},{5,7},{6,4},{7,5},{8,10},{9,11},{10,... | collective-permute-start | bytes 1179656 | tf_op jit(solution)/shard_map/ppermute | solution.py:718
  (59 other events, 611.3 us)

commit v4 on v3

--- a/solution.py
+++ b/solution.py
@@ -19,7 +19,7 @@
 COST = 0.02
 ATTEND_PAIRS = 9
 BACK_PAIRS = 3
-TAIL = "NMQONMQQOMMNQmNQnQ"
+TAIL = "QMNNMQNQMQMmQnQ"
 
 NN = (((1,), (0,)), ((), ()))
 NT = (((1,), (1,)), ((), ()))
@@ -916,14 +916,19 @@
     return x
 
 
-def scatter_blocks(blocks, n_blk):
-    (got,) = yield [(jnp.concatenate([blocks[6:8], blocks[2:4]]), "blk", 1)]
-    far = add(blocks[4:6], got[0:2]).astype(BF16)
-    near = add(blocks[0:2], got[2:4]).astype(BF16)
-    (far_got,) = yield [(far[1], "blk", 2)]
-    far_sum = add(far[0], far_got).astype(BF16)
-    other, near_got = yield [(far_sum, "blk", n_blk // 2), (near[1], "blk", 2)]
-    yield [add(near[0], near_got).astype(BF16), other]
+def scatter_blocks(arrays, n_blk):
+    n = len(arrays)
+
+    def cut(first):
+        return [a[first : first + 2] for a in arrays]
+
+    (got,) = yield [(jnp.concatenate(cut(6) + cut(2)), "blk", 1)]
+    far = add(jnp.stack(cut(4)), got[: 2 * n].reshape((n, 2) + got.shape[1:])).astype(BF16)
+    near = add(jnp.stack(cut(0)), got[2 * n :].reshape((n, 2) + got.shape[1:])).astype(BF16)
+    (far_got,) = yield [(far[:, 1], "blk", 2)]
+    far_sum = add(far[:, 0], far_got).astype(BF16)
+    other, near_got = yield [(far_sum, "blk", n_blk // 2), (near[:, 1], "blk", 2)]
+    yield [add(near[:, 0], near_got).astype(BF16), other]
 
 
 def local(n_dp, n_blk, tokens, cotangent, lengths, norm_gain, norm_bias, w_qkv, w_out, w_up, w_down):
@@ -985,7 +990,6 @@
     if fast:
         order.advance(mlp)
     out_part, do, delta, grad_out_part = order.done(mix(meta, *order.hold([att, cot, mo]), w_out))
-    out_steps = order.start(scatter_blocks(out_part, n_blk))
     if fast:
         order.advance(mlp)
     rest = (normed, grad_out_part)
@@ -997,7 +1001,7 @@
             count = grads[at].shape[0] // 2
             grads[at] = add(grads[at][:count], swap(grads[at][count:], "blk", n_blk, mask)).astype(BF16)
         rest_parts = order.done(shard(meta, grads, *rest))
-    chains = {"O": out_steps}
+    chains = {}
     if fast:
 
         def of_rest():
@@ -1007,15 +1011,15 @@
         order.advance(mlp)
         chains["M"] = order.start(spread_pieces(mlp.held[0]))
         chains["Q"] = order.start(of_rest())
-    order.advance(out_steps)
     ng_part, sums = order.done(join(meta, order.hold(grads), x_all, ngm, w_cut))
 
     def finish():
         def ordered(own, other):
             return jnp.where(half == 0, jnp.stack([own, other]), jnp.stack([other, own])).astype(F32)
 
-        output = (tokens.astype(F32) + ordered(*chains["O"].end())).astype(BF16)
-        normed_grad = ordered(*chains["N"].end())
+        own, other = chains["N"].end()
+        output = (tokens.astype(F32) + ordered(own[0], other[0])).astype(BF16)
+        normed_grad = ordered(own[1], other[1])
         x_rows = tokens.astype(F32)
         centred = x_rows - jnp.mean(x_rows, axis=2, keepdims=True)
         inverse = lax.rsqrt(jnp.mean(centred * centred, axis=2, keepdims=True) + norm_eps)
@@ -1037,10 +1041,10 @@
             elif name in chains:
                 order.advance(chains[name])
             else:
-                chains[name] = order.start(scatter_blocks(ng_part, n_blk))
+                chains[name] = order.start(scatter_blocks([out_part, ng_part], n_blk))
         grad_qkv, grad_out, *norm_sums = tail(meta, chains["Q"].end(), width, wide)
     else:
-        chains["N"] = order.start(scatter_blocks(ng_part, n_blk))
+        chains["N"] = order.start(scatter_blocks([out_part, ng_part], n_blk))
         output, input_grad = finish()
         up, down = natural_halves(mlp_parts)
         (rest,) = natural(rest_parts)

time: 281 us -> 280 us (level)
  starting transfers between devices: 40.5 us -> 37.6 us
    another operation x1 -> x3, local copies, waits for them, and re-layouts: 0.01 us -> 4.11 us  [the longest x2 4.11 us: scatter_blocks(): jnp.stack(cut(0))]
    ppermute x49 -> x45, starting transfers between devices: 40.5 us -> 37.6 us  [swap(): return lax.ppermute(x, axis, [(i, i ^ mask) for i in range(size)])]
    ppermute x49 -> x45, waiting for transfers between devices: 91.8 us -> 90.9 us  [swap(): return lax.ppermute(x, axis, [(i, i ^ mask) for i in range(size)])]
    unnamed x84 -> x82, local copies, waits for them, and re-layouts: 5.69 us -> 5.47 us
  transfers between devices with their start and end apart: 49 -> 45, of which waited for: 19 -> 20; matrix products, arithmetic and copies ran while one was open for 5% -> 6% of each run, Pallas kernels for 32% -> 32%
where the time goes in v4:
time: 280 us; the launch traced here: 279 us
  Pallas kernels  124 us (44%)
  waiting for transfers between devices  90.9 us (32%)
  starting transfers between devices  37.6 us (13%)
  local copies, waits for them, and re-layouts  15.5 us (6%)
  other arithmetic  9.69 us (3%)
    pallas_call x10, Pallas kernels, call(): pl.pallas_call(kernel, out_shape=out_shapes, grid_spec=pltpu.PrefetchScal...  124 us
    ppermute x45, waiting for transfers between devices, swap(): return lax.ppermute(x, axis, [(i, i ^ mask) for i in range(size)])  90.9 us
    ppermute x45, starting transfers between devices, swap(): return lax.ppermute(x, axis, [(i, i ^ mask) for i in range(size)])  37.6 us
  transfers between devices with their start and end apart: 45, of which 20 were waited for; matrix products, arithmetic and copies ran while one was open for 6% of the time, Pallas kernels for 32%

profile of v4, /device:TPU:0, one launch (start us, length us, event | category | flops | bytes accessed | tf_op | source)
XLA Modules:
  0.0 278.9 jit_solution(1089323419391565651)
XLA Ops:
  2.2 3.1 %collective-permute-start.1 = (bf16[256,768]{1,0:T(8,128)(2,1)S(1)}, bf16[256,768]{1,0:T(8,128)(2,1)S(1)}, u32[]{:S(2)}, u32[]{:S(2)}) collective-permute-start(bf16[256,768]{1,0:T(8,128)(2,1)S(1)} %get-tuple-element.182.refs_0_), channel_id=1, source_target_pairs={{0,2},{1,3},{2,0},{3,1},{4,6},{5,7},{6,4},{7,5},{8,10},{9,11},{10,... | collective-permute-start | bytes 1179656 | tf_op jit(solution)/shard_map/ppermute | solution.py:718
  5.2 2.6 collective-permute-start
  8.7 4.0 %cut.1.refs_6_.refs_5_ = bf16[576,768]{1,0:T(8,128)(2,1)} custom-call(s32[9]{0:T(128)} %concatenate.12.meta_ref, bf16[768,2304]{1,0:T(8,128)(2,1)} %refs_2_.1, bf16[768,2304]{1,0:T(8,128)(2,1)} %refs_2_.1, bf16[768,2304]{1,0:T(8,128)(2,1)} %refs_2_.1), custom_call_target="tpu_custom_call" | custom-call | bytes 53084 | tf_op jit(solution)/shard_map/cut/pallas_call | solution.py:59
  12.7 9.1 %collective-permute-done.1.refs_1_ = bf16[256,768]{1,0:T(8,128)(2,1)S(1)} collective-permute-done((bf16[256,768]{1,0:T(8,128)(2,1)S(1)}, bf16[256,768]{1,0:T(8,128)(2,1)S(1)}, u32[]{:S(2)}, u32[]{:S(2)}) %collective-permute-start.1) | collective-permute-done | bytes 393248 | tf_op jit(solution)/shard_map/ppermute | solution.py:718
  21.8 4.3 %collective-permute-done.refs_0_ = bf16[256,768]{1,0:T(8,128)(2,1)S(1)} collective-permute-done((bf16[256,768]{1,0:T(8,128)(2,1)S(1)}, bf16[256,768]{1,0:T(8,128)(2,1)S(1)}, u32[]{:S(2)}, u32[]{:S(2)}) %collective-permute-start) | collective-permute-done | bytes 393248 | tf_op jit(solution)/shard_map/ppermute | solution.py:718
  26.2 3.0 %collective-permute-start.7 = (bf16[256,768]{1,0:T(8,128)(2,1)S(1)}, bf16[256,768]{1,0:T(8,128)(2,1)S(1)}, u32[]{:S(2)}, u32[]{:S(2)}) collective-permute-start(bf16[256,768]{1,0:T(8,128)(2,1)S(1)} %get-tuple-element.180), channel_id=1, source_target_pairs={{0,4},{1,5},{2,6},{3,7},{4,0},{5,1},{6,2},{7,3},{8,12},{9,13},{10,... | collective-permute-start | bytes 1179656 | tf_op jit(solution)/shard_map/ppermute | solution.py:718
  31.1 6.1 %project.2 = (bf16[8,256,768]{2,1,0:T(8,128)(2,1)}, bf16[8,256,768]{2,1,0:T(8,128)(2,1)}, bf16[8,192,256]{2,1,0:T(8,128)(2,1)}, bf16[8,192,256]{2,1,0:T(8,128)(2...) custom-call(s32[9]{0:T(128)} %concatenate.12.meta_ref, ...), custom_call_target="tpu_custom_call" | custom-call | flops 18119392 | bytes 157286 | tf_op jit(solution)/shard_map/project/pallas_call | solution.py:59
  37.2 6.8 %collective-permute-done.3.refs_1_ = bf16[256,768]{1,0:T(8,128)(2,1)S(1)} collective-permute-done((bf16[256,768]{1,0:T(8,128)(2,1)S(1)}, bf16[256,768]{1,0:T(8,128)(2,1)S(1)}, u32[]{:S(2)}, u32[]{:S(2)}) %collective-permute-start.3) | collective-permute-done | bytes 393248 | tf_op jit(solution)/shard_map/ppermute | solution.py:718
  44.6 2.9 %collective-permute-done.7.refs_4_ = bf16[256,768]{1,0:T(8,128)(2,1)S(1)} collective-permute-done((bf16[256,768]{1,0:T(8,128)(2,1)S(1)}, bf16[256,768]{1,0:T(8,128)(2,1)S(1)}, u32[]{:S(2)}, u32[]{:S(2)}) %collective-permute-start.7) | collective-permute-done | bytes 393248 | tf_op jit(solution)/shard_map/ppermute | solution.py:718
  48.3 6.1 %project.3 = (bf16[8,256,768]{2,1,0:T(8,128)(2,1)}, bf16[8,256,768]{2,1,0:T(8,128)(2,1)}, bf16[8,192,256]{2,1,0:T(8,128)(2,1)}, bf16[8,192,256]{2,1,0:T(8,128)(2...) custom-call(s32[9]{0:T(128)} %concatenate.12.meta_ref, ...), custom_call_target="tpu_custom_call", output_to_operand_aliasing={{0}: (8, {}), {1}: (9, {}), {2}: (10, {}), {3}: (11, {}), {... | custom-call | flops 18119392 | bytes 157286 | tf_op jit(solution)/shard_map/project/pallas_call | solution.py:59
  54.4 1.7 collective-permute-done.8.refs_1_
  56.2 8.1 %collective-permute-done.11.refs_5_ = bf16[256,768]{1,0:T(8,128)(2,1)S(1)} collective-permute-done((bf16[256,768]{1,0:T(8,128)(2,1)S(1)}, bf16[256,768]{1,0:T(8,128)(2,1)S(1)}, u32[]{:S(2)}, u32[]{:S(2)}) %collective-permute-start.11) | collective-permute-done | bytes 393248 | tf_op jit(solution)/shard_map/ppermute | solution.py:718
  67.4 24.6 %feed.1 = (bf16[8,256,768]{2,1,0:T(8,128)(2,1)}, bf16[8,256,768]{2,1,0:T(8,128)(2,1)}, bf16[8,256,768]{2,1,0:T(8,128)(2,1)}, bf16[2,2,96,768]{3,2,1,0:T(8,128)(2...) custom-call(s32[9]{0:T(128)} %concatenate.12.meta_ref, ...), custom_call_target="tpu_custom_call" | custom-call | flops 289910304 | bytes 346030 | tf_op jit(solution)/shard_map/feed/pallas_call | solution.py:59
  95.1 14.4 %attend.1 = (bf16[8,192,256]{2,1,0:T(8,128)(2,1)}, f32[8,8,256]{2,1,0:T(8,128)}) custom-call(s32[9]{0:T(128)} %concatenate.12.meta_ref, bf16[8,192,256]{2,1,0:T(8,128)(2,1)} %get-tuple-element.249.refs_0_, bf16[8,3,256,64]{3,2,1,0:T(8,128)(2,1)} %get-tuple-element.231.refs_1_.refs_4_, bf16[8,192,256]{2,1,0:T(8,128)(2,1)} %get-tuple-element.232.refs_2_), custom_call_target="tpu_custom_call" | custom-call | flops 72155448 | bytes 125829 | tf_op jit(solution)/shard_map/attend/pallas_call | solution.py:59
  111.8 8.0 %mix.1 = (bf16[8,256,768]{2,1,0:T(8,128)(2,1)}, bf16[8,192,256]{2,1,0:T(8,128)(2,1)}, f32[8,8,256]{2,1,0:T(8,128)}, f32[192,768]{1,0:T(8,128)}) custom-call(s32[9]{0:T(128)} %concatenate.12.meta_ref, bf16[8,192,256]{2,1,0:T(8,128)(2,1)} %get-tuple-element.241.refs_0_, bf16[8,256,768]{2,1,0:T(8,128)(2,1)} %get-tuple-element.242.refs_1_, ...), custom_call_target="tpu_custom_call" | custom-call | flops 36238784 | bytes 314572 | tf_op jit(solution)/shard_map/mix/pallas_call | solution.py:59
  120.5 2.0 slice_bitcast_fusion.7
  122.6 31.2 %attend_back.1 = (bf16[1,192,768]{2,1,0:T(8,128)(2,1)}, bf16[1,192,768]{2,1,0:T(8,128)(2,1)}, bf16[1,192,768]{2,1,0:T(8,128)(2,1)}, bf16[1,192,768]{2,1,0:T(8,12...) custom-call(s32[9]{0:T(128)} %concatenate.12.meta_ref, ...), custom_call_target="tpu_custom_call" | custom-call | flops 180388624 | bytes 125829 | tf_op jit(solution)/shard_map/attend_back/pallas_call | solution.py:59
  154.0 2.4 collective-permute-start.19
  159.9 8.8 %join.1 = (bf16[8,256,768]{2,1,0:T(8,128)(2,1)}, f32[16,768]{1,0:T(8,128)}) custom-call(s32[9]{0:T(128)} %concatenate.12.meta_ref, bf16[8,192,256]{2,1,0:T(8,128)(2,1)} %get-tuple-element.268.refs_0_, bf16[8,192,256]{2,1,0:T(8,128)(2,1)} %get-tuple-element.269.refs_1_, bf16[8,192,256]{2,1,0:T(8,128)(2,1)} %get-tuple-element.270.refs_2_, ...), custom_call_target="tpu_custom_call" | custom-call | flops 36238784 | bytes 314572 | tf_op jit(solution)/shard_map/join/pallas_call | solution.py:59
  168.6 2.1 slice_bitcast_fusion.6
  176.3 1.6 collective-permute-done.23
  179.4 9.3 %collective-permute-done.26 = bf16[2,2,96,768]{3,2,1,0:T(8,128)(2,1)S(1)} collective-permute-done((bf16[2,2,96,768]{3,2,1,0:T(8,128)(2,1)S(1)}, bf16[2,2,96,768]{3,2,1,0:T(8,128)(2,1)S(1)}, u32[]{:S(2)}, u32[]{:S(2)}) %collective-permute-start.26) | collective-permute-done | bytes 589856 | tf_op jit(solution)/shard_map/ppermute | solution.py:718
  194.3 11.1 %collective-permute-done.24 = bf16[2,256,768]{2,1,0:T(8,128)(2,1)S(1)} collective-permute-done((bf16[2,256,768]{2,1,0:T(8,128)(2,1)S(1)}, bf16[2,256,768]{2,1,0:T(8,128)(2,1)S(1)}, u32[]{:S(2)}, u32[]{:S(2)}) %collective-permute-start.24) | collective-permute-done | bytes 786464 | tf_op jit(solution)/shard_map/ppermute | solution.py:718
  206.6 8.1 %collective-permute-done.30 = bf16[2,112,768]{2,1,0:T(8,128)(2,1)S(1)} collective-permute-done((bf16[2,112,768]{2,1,0:T(8,128)(2,1)S(1)}, bf16[2,112,768]{2,1,0:T(8,128)(2,1)S(1)}, u32[]{:S(2)}, u32[]{:S(2)}) %collective-permute-start.30) | collective-permute-done | bytes 344096 | tf_op jit(solution)/shard_map/ppermute | solution.py:718
  218.6 2.0 collective-permute-done.34.refs_3_
  221.2 4.5 %collective-permute-done.31 = bf16[2,112,768]{2,1,0:T(8,128)(2,1)S(1)} collective-permute-done((bf16[2,112,768]{2,1,0:T(8,128)(2,1)S(1)}, bf16[2,112,768]{2,1,0:T(8,128)(2,1)S(1)}, u32[]{:S(2)}, u32[]{:S(2)}) %collective-permute-start.31) | collective-permute-done | bytes 344096 | tf_op jit(solution)/shard_map/ppermute | solution.py:718
  227.8 2.0 collective-permute-start.28
  230.4 11.5 %collective-permute-done.37.refs_2_ = bf16[2,2,112,768]{3,2,1,0:T(8,128)(2,1)S(1)} collective-permute-done((bf16[2,2,112,768]{3,2,1,0:T(8,128)(2,1)S(1)}, bf16[2,2,112,768]{3,2,1,0:T(8,128)(2,1)S(1)}, u32[]{:S(2)}, u32[]{:S(2)}) %collective-permute-start.37) | collective-permute-done | bytes 688160 | tf_op jit(solution)/shard_map/ppermute | solution.py:718
  245.4 11.4 %fill.1 = (f32[768,3072]{1,0:T(8,128)}, f32[3072,768]{1,0:T(8,128)}) custom-call(s32[9]{0:T(128)} %concatenate.12.meta_ref, bf16[2,2,2,96,768]{4,3,2,1,0:T(8,128)(2,1)} %copy-done.1, bf16[2,2,2,96,768]{4,3,2,1,0:T(8,128)(2,1)} %copy-done.2, bf16[2,2,2,96,768]{4,3,2,1,0:T(8,128)(2,1)} %copy-done.7, bf16[2,2,2,96,768]{4,3,2,1,0:T(8,128)(2,1)} %copy-done.8, ...), custom_call_target="tpu_custom_call" | custom-call | bytes 566231 | tf_op jit(solution)/shard_map/fill/pallas_call | solution.py:59
  257.7 5.6 %collective-permute-done.28 = bf16[2,256,768]{2,1,0:T(8,128)(2,1)} collective-permute-done((bf16[2,256,768]{2,1,0:T(8,128)(2,1)}, bf16[2,256,768]{2,1,0:T(8,128)(2,1)}, u32[]{:S(2)}, u32[]{:S(2)}) %collective-permute-start.28) | collective-permute-done | bytes 786464 | tf_op jit(solution)/shard_map/ppermute | solution.py:718
  266.6 2.1 fusion.9
  269.8 9.1 %tail.1 = (f32[768,2304]{1,0:T(8,128)}, f32[768,768]{1,0:T(8,128)}, f32[768]{0:T(1024)}, f32[768]{0:T(1024)}) custom-call(s32[9]{0:T(128)} %concatenate.12.meta_ref, bf16[2,2,112,768]{3,2,1,0:T(8,128)(2,1)} %copy-done.4, bf16[2,2,112,768]{3,2,1,0:T(8,128)(2,1)} %pad_maximum_fusion.4.refs_1_, bf16[2,2,112,768]{3,2,1,0:T(8,128)(2,1)} %copy-done.13, ...), custom_call_target="tpu_custom_call" | custom-call | bytes 283115 | tf_op jit(solution)/shard_map/tail/pallas_call | solution.py:59
  (204 shorter events, 47.7 us)
Async XLA Ops:
  2.2 19.6 %collective-permute-start.1 = (bf16[256,768]{1,0:T(8,128)(2,1)S(1)}, bf16[256,768]{1,0:T(8,128)(2,1)S(1)}, u32[]{:S(2)}, u32[]{:S(2)}) collective-permute-start(bf16[256,768]{1,0:T(8,128)(2,1)S(1)} %get-tuple-element.182.refs_0_), channel_id=1, source_target_pairs={{0,2},{1,3},{2,0},{3,1},{4,6},{5,7},{6,4},{7,5},{8,10},{9,11},{10,... | collective-permute-start | bytes 1179656 | tf_op jit(solution)/shard_map/ppermute | solution.py:718
  5.2 16.5 %collective-permute-start.2 = (bf16[256,768]{1,0:T(8,128)(2,1)S(1)}, bf16[256,768]{1,0:T(8,128)(2,1)S(1)}, u32[]{:S(2)}, u32[]{:S(2)}) collective-permute-start(bf16[256,768]{1,0:T(8,128)(2,1)S(1)} %get-tuple-element.182.refs_0_), channel_id=1, source_target_pairs={{0,1},{1,0},{2,3},{3,2},{4,5},{5,4},{6,7},{7,6},{8,9},{9,8},{10,11... | collective-permute-start | bytes 1179656 | tf_op jit(solution)/shard_map/ppermute | solution.py:718
  5.2 20.9 %collective-permute-start = (bf16[256,768]{1,0:T(8,128)(2,1)S(1)}, bf16[256,768]{1,0:T(8,128)(2,1)S(1)}, u32[]{:S(2)}, u32[]{:S(2)}) collective-permute-start(bf16[256,768]{1,0:T(8,128)(2,1)S(1)} %get-tuple-element.378), channel_id=1, source_target_pairs={{0,4},{1,5},{2,6},{3,7},{4,0},{5,1},{6,2},{7,3},{8,12},{9,13},{10,... | collective-permute-start | bytes 1179656 | tf_op jit(solution)/shard_map/ppermute | solution.py:718
  26.1 17.9 %collective-permute-start.3 = (bf16[256,768]{1,0:T(8,128)(2,1)S(1)}, bf16[256,768]{1,0:T(8,128)(2,1)S(1)}, u32[]{:S(2)}, u32[]{:S(2)}) collective-permute-start(bf16[256,768]{1,0:T(8,128)(2,1)S(1)} %collective-permute-done.refs_0_), channel_id=1, source_target_pairs={{0,2},{1,3},{2,0},{3,1},{4,6},{5,7},{6,4},{7,5},{8,10},{9,11},{10,... | collective-permute-start | bytes 1179656 | tf_op jit(solution)/shard_map/ppermute | solution.py:718
  26.1 17.9 %collective-permute-start.4 = (bf16[256,768]{1,0:T(8,128)(2,1)S(1)}, bf16[256,768]{1,0:T(8,128)(2,1)S(1)}, u32[]{:S(2)}, u32[]{:S(2)}) collective-permute-start(bf16[256,768]{1,0:T(8,128)(2,1)S(1)} %collective-permute-done.refs_0_), channel_id=1, source_target_pairs={{0,1},{1,0},{2,3},{3,2},{4,5},{5,4},{6,7},{7,6},{8,9},{9,8},{10,11... | collective-permute-start | bytes 1179656 | tf_op jit(solution)/shard_map/ppermute | solution.py:718
  26.2 21.3 %collective-permute-start.7 = (bf16[256,768]{1,0:T(8,128)(2,1)S(1)}, bf16[256,768]{1,0:T(8,128)(2,1)S(1)}, u32[]{:S(2)}, u32[]{:S(2)}) collective-permute-start(bf16[256,768]{1,0:T(8,128)(2,1)S(1)} %get-tuple-element.180), channel_id=1, source_target_pairs={{0,4},{1,5},{2,6},{3,7},{4,0},{5,1},{6,2},{7,3},{8,12},{9,13},{10,... | collective-permute-start | bytes 1179656 | tf_op jit(solution)/shard_map/ppermute | solution.py:718
  44.1 12.1 %collective-permute-start.8 = (bf16[256,768]{1,0:T(8,128)(2,1)S(1)}, bf16[256,768]{1,0:T(8,128)(2,1)S(1)}, u32[]{:S(2)}, u32[]{:S(2)}) collective-permute-start(bf16[256,768]{1,0:T(8,128)(2,1)S(1)} %get-tuple-element.216.refs_0_), channel_id=1, source_target_pairs={{0,2},{1,3},{2,0},{3,1},{4,6},{5,7},{6,4},{7,5},{8,10},{9,11},{10,... | collective-permute-start | bytes 1179656 | tf_op jit(solution)/shard_map/ppermute | solution.py:718
  44.2 12.0 %collective-permute-start.9 = (bf16[256,768]{1,0:T(8,128)(2,1)S(1)}, bf16[256,768]{1,0:T(8,128)(2,1)S(1)}, u32[]{:S(2)}, u32[]{:S(2)}) collective-permute-start(bf16[256,768]{1,0:T(8,128)(2,1)S(1)} %get-tuple-element.216.refs_0_), channel_id=1, source_target_pairs={{0,1},{1,0},{2,3},{3,2},{4,5},{5,4},{6,7},{7,6},{8,9},{9,8},{10,11... | collective-permute-start | bytes 1179656 | tf_op jit(solution)/shard_map/ppermute | solution.py:718
  47.5 16.8 %collective-permute-start.11 = (bf16[256,768]{1,0:T(8,128)(2,1)S(1)}, bf16[256,768]{1,0:T(8,128)(2,1)S(1)}, u32[]{:S(2)}, u32[]{:S(2)}) collective-permute-start(bf16[256,768]{1,0:T(8,128)(2,1)S(1)} %collective-permute-done.7.refs_4_), channel_id=1, source_target_pairs={{0,2},{1,3},{2,0},{3,1},{4,6},{5,7},{6,4},{7,5},{8,10},{9,11},{10,... | collective-permute-start | bytes 1179656 | tf_op jit(solution)/shard_map/ppermute | solution.py:718
  47.5 16.8 %collective-permute-start.12 = (bf16[256,768]{1,0:T(8,128)(2,1)S(1)}, bf16[256,768]{1,0:T(8,128)(2,1)S(1)}, u32[]{:S(2)}, u32[]{:S(2)}) collective-permute-start(bf16[256,768]{1,0:T(8,128)(2,1)S(1)} %collective-permute-done.7.refs_4_), channel_id=1, source_target_pairs={{0,1},{1,0},{2,3},{3,2},{4,5},{5,4},{6,7},{7,6},{8,9},{9,8},{10,11... | collective-permute-start | bytes 1179656 | tf_op jit(solution)/shard_map/ppermute | solution.py:718
  92.0 17.5 %collective-permute-start.14 = (bf16[2,2,96,768]{3,2,1,0:T(8,128)(2,1)}, bf16[2,2,96,768]{3,2,1,0:T(8,128)(2,1)S(1)}, u32[]{:S(2)}, u32[]{:S(2)}) collective-permute-start(bf16[2,2,96,768]{3,2,1,0:T(8,128)(2,1)} %get-tuple-element.228), channel_id=1, source_target_pairs={{0,8},{8,0},{16,24},{24,16},{1,9},{9,1},{17,25},{25,17},{2,10},{10... | collective-permute-start | bytes 1769480 | tf_op jit(solution)/shard_map/ppermute | solution.py:718
  93.6 16.0 %collective-permute-start.15 = (bf16[2,2,96,768]{3,2,1,0:T(8,128)(2,1)}, bf16[2,2,96,768]{3,2,1,0:T(8,128)(2,1)S(1)}, u32[]{:S(2)}, u32[]{:S(2)}) collective-permute-start(bf16[2,2,96,768]{3,2,1,0:T(8,128)(2,1)} %get-tuple-element.229), channel_id=1, source_target_pairs={{0,16},{8,24},{16,0},{24,8},{1,17},{9,25},{17,1},{25,9},{2,18},{10... | collective-permute-start | bytes 1769480 | tf_op jit(solution)/shard_map/ppermute | solution.py:718
  120.1 33.6 %collective-permute-start.18 = (bf16[2,2,96,768]{3,2,1,0:T(8,128)(2,1)S(1)}, bf16[2,2,96,768]{3,2,1,0:T(8,128)(2,1)S(1)}, u32[]{:S(2)}, u32[]{:S(2)}) collective-permute-start(bf16[2,2,96,768]{3,2,1,0:T(8,128)(2,1)S(1)} %pad_maximum_fusion.5), channel_id=1, source_target_pairs={{0,4},{1,5},{2,6},{3,7},{4,0},{5,1},{6,2},{7,3},{8,12},{9,13},{10,... | collective-permute-start | bytes 1769480 | tf_op jit(solution)/shard_map/ppermute | solution.py:718
  154.0 18.0 %collective-permute-start.19 = (bf16[2,2,96,768]{3,2,1,0:T(8,128)(2,1)S(1)}, bf16[2,2,96,768]{3,2,1,0:T(8,128)(2,1)S(1)}, u32[]{:S(2)}, u32[]{:S(2)}) collective-permute-start(bf16[2,2,96,768]{3,2,1,0:T(8,128)(2,1)S(1)} %add_convert_fusion), channel_id=1, source_target_pairs={{0,2},{1,3},{2,0},{3,1},{4,6},{5,7},{6,4},{7,5},{8,10},{9,11},{10,... | collective-permute-start | bytes 1769480 | tf_op jit(solution)/shard_map/ppermute | solution.py:718
  156.4 14.8 %collective-permute-start.20 = (bf16[1,192,768]{2,1,0:T(8,128)(2,1)S(1)}, bf16[1,192,768]{2,1,0:T(8,128)(2,1)S(1)}, u32[]{:S(2)}, u32[]{:S(2)}) collective-permute-start(bf16[1,192,768]{2,1,0:T(8,128)(2,1)S(1)} %copy-done.40), channel_id=1, source_target_pairs={{0,8},{8,0},{16,24},{24,16},{1,9},{9,1},{17,25},{25,17},{2,10},{10... | collective-permute-start | bytes 884744 | tf_op jit(solution)/shard_map/ppermute | solution.py:718
  157.8 13.4 %collective-permute-start.21 = (bf16[1,192,768]{2,1,0:T(8,128)(2,1)S(1)}, bf16[1,192,768]{2,1,0:T(8,128)(2,1)S(1)}, u32[]{:S(2)}, u32[]{:S(2)}) collective-permute-start(bf16[1,192,768]{2,1,0:T(8,128)(2,1)S(1)} %copy-done.39), channel_id=1, source_target_pairs={{0,16},{8,24},{16,0},{24,8},{1,17},{9,25},{17,1},{25,9},{2,18},{10... | collective-permute-start | bytes 884744 | tf_op jit(solution)/shard_map/ppermute | solution.py:718
  172.3 20.0 %collective-permute-start.25 = (bf16[2,112,768]{2,1,0:T(8,128)(2,1)S(1)}, bf16[2,112,768]{2,1,0:T(8,128)(2,1)S(1)}, u32[]{:S(2)}, u32[]{:S(2)}) collective-permute-start(bf16[2,112,768]{2,1,0:T(8,128)(2,1)S(1)} %pad_maximum_fusion.8), channel_id=1, source_target_pairs={{0,4},{1,5},{2,6},{3,7},{4,0},{5,1},{6,2},{7,3},{8,12},{9,13},{10,... | collective-permute-start | bytes 1032200 | tf_op jit(solution)/shard_map/ppermute | solution.py:718
  173.3 15.4 %collective-permute-start.26 = (bf16[2,2,96,768]{3,2,1,0:T(8,128)(2,1)S(1)}, bf16[2,2,96,768]{3,2,1,0:T(8,128)(2,1)S(1)}, u32[]{:S(2)}, u32[]{:S(2)}) collective-permute-start(bf16[2,2,96,768]{3,2,1,0:T(8,128)(2,1)S(1)} %get-tuple-element.279), channel_id=1, source_target_pairs={{0,8},{8,0},{16,24},{24,16},{1,9},{9,1},{17,25},{25,17},{2,10},{10... | collective-permute-start | bytes 1769480 | tf_op jit(solution)/shard_map/ppermute | solution.py:718
  174.8 15.1 %collective-permute-start.27 = (bf16[2,2,96,768]{3,2,1,0:T(8,128)(2,1)S(1)}, bf16[2,2,96,768]{3,2,1,0:T(8,128)(2,1)S(1)}, u32[]{:S(2)}, u32[]{:S(2)}) collective-permute-start(bf16[2,2,96,768]{3,2,1,0:T(8,128)(2,1)S(1)} %get-tuple-element.280), channel_id=1, source_target_pairs={{0,16},{8,24},{16,0},{24,8},{1,17},{9,25},{17,1},{25,9},{2,18},{10... | collective-permute-start | bytes 1769480 | tf_op jit(solution)/shard_map/ppermute | solution.py:718
  178.6 26.8 %collective-permute-start.24 = (bf16[2,256,768]{2,1,0:T(8,128)(2,1)S(1)}, bf16[2,256,768]{2,1,0:T(8,128)(2,1)S(1)}, u32[]{:S(2)}, u32[]{:S(2)}) collective-permute-start(bf16[2,256,768]{2,1,0:T(8,128)(2,1)S(1)} %slice_bitcast_fusion.1), channel_id=1, source_target_pairs={{0,2},{1,3},{2,0},{3,1},{4,6},{5,7},{6,4},{7,5},{8,10},{9,11},{10,... | collective-permute-start | bytes 2359304 | tf_op jit(solution)/shard_map/ppermute | solution.py:718
  190.1 27.0 %collective-permute-start.33 = (bf16[2,2,2,96,768]{4,3,2,1,0:T(8,128)(2,1)S(1)}, bf16[2,2,2,96,768]{4,3,2,1,0:T(8,128)(2,1)S(1)}, u32[]{:S(2)}, u32[]{:S(2)}) collective-permute-start(bf16[2,2,2,96,768]{4,3,2,1,0:T(8,128)(2,1)S(1)} %pad_maximum_fusion.1.refs_0_), channel_id=1, source_target_pairs={{0,16},{8,24},{16,0},{24,8},{1,17},{9,25},{17,1},{25,9},{2,18},{10... | collective-permute-start | bytes 3538952 | tf_op jit(solution)/shard_map/ppermute | solution.py:718
  191.7 28.9 %collective-permute-start.34 = (bf16[2,2,2,96,768]{4,3,2,1,0:T(8,128)(2,1)S(1)}, bf16[2,2,2,96,768]{4,3,2,1,0:T(8,128)(2,1)S(1)}, u32[]{:S(2)}, u32[]{:S(2)}) collective-permute-start(bf16[2,2,2,96,768]{4,3,2,1,0:T(8,128)(2,1)S(1)} %pad_maximum_fusion.2.refs_1_), channel_id=1, source_target_pairs={{0,8},{8,0},{16,24},{24,16},{1,9},{9,1},{17,25},{25,17},{2,10},{10... | collective-permute-start | bytes 3538952 | tf_op jit(solution)/shard_map/ppermute | solution.py:718
  192.3 28.4 %collective-permute-start.35 = (bf16[2,2,2,96,768]{4,3,2,1,0:T(8,128)(2,1)S(1)}, bf16[2,2,2,96,768]{4,3,2,1,0:T(8,128)(2,1)S(1)}, u32[]{:S(2)}, u32[]{:S(2)}) collective-permute-start(bf16[2,2,2,96,768]{4,3,2,1,0:T(8,128)(2,1)S(1)} %pad_maximum_fusion.1.refs_0_), channel_id=1, source_target_pairs={{0,1},{1,0},{2,3},{3,2},{4,5},{5,4},{6,7},{7,6},{8,9},{9,8},{10,11... | collective-permute-start | bytes 3538952 | tf_op jit(solution)/shard_map/ppermute | solution.py:718
  192.3 28.4 %collective-permute-start.36 = (bf16[2,2,2,96,768]{4,3,2,1,0:T(8,128)(2,1)S(1)}, bf16[2,2,2,96,768]{4,3,2,1,0:T(8,128)(2,1)S(1)}, u32[]{:S(2)}, u32[]{:S(2)}) collective-permute-start(bf16[2,2,2,96,768]{4,3,2,1,0:T(8,128)(2,1)S(1)} %pad_maximum_fusion.2.refs_1_), channel_id=1, source_target_pairs={{0,1},{1,0},{2,3},{3,2},{4,5},{5,4},{6,7},{7,6},{8,9},{9,8},{10,11... | collective-permute-start | bytes 3538952 | tf_op jit(solution)/shard_map/ppermute | solution.py:718
  220.7 22.7 %collective-permute-start.41 = (bf16[2,2,2,96,768]{4,3,2,1,0:T(8,128)(2,1)S(1)}, bf16[2,2,2,96,768]{4,3,2,1,0:T(8,128)(2,1)S(1)}, u32[]{:S(2)}, u32[]{:S(2)}) collective-permute-start(bf16[2,2,2,96,768]{4,3,2,1,0:T(8,128)(2,1)S(1)} %collective-permute-done.33.refs_2_), channel_id=1, source_target_pairs={{0,1},{1,0},{2,3},{3,2},{4,5},{5,4},{6,7},{7,6},{8,9},{9,8},{10,11... | collective-permute-start | bytes 3538952 | tf_op jit(solution)/shard_map/ppermute | solution.py:718
  220.7 22.7 %collective-permute-start.42 = (bf16[2,2,2,96,768]{4,3,2,1,0:T(8,128)(2,1)S(1)}, bf16[2,2,2,96,768]{4,3,2,1,0:T(8,128)(2,1)S(1)}, u32[]{:S(2)}, u32[]{:S(2)}) collective-permute-start(bf16[2,2,2,96,768]{4,3,2,1,0:T(8,128)(2,1)S(1)} %collective-permute-done.34.refs_3_), channel_id=1, source_target_pairs={{0,1},{1,0},{2,3},{3,2},{4,5},{5,4},{6,7},{7,6},{8,9},{9,8},{10,11... | collective-permute-start | bytes 3538952 | tf_op jit(solution)/shard_map/ppermute | solution.py:718
  226.8 15.2 %collective-permute-start.37 = (bf16[2,2,112,768]{3,2,1,0:T(8,128)(2,1)S(1)}, bf16[2,2,112,768]{3,2,1,0:T(8,128)(2,1)S(1)}, u32[]{:S(2)}, u32[]{:S(2)}) collective-permute-start(bf16[2,2,112,768]{3,2,1,0:T(8,128)(2,1)S(1)} %pad_maximum_fusion.3.refs_0_), channel_id=1, source_target_pairs={{0,16},{8,24},{16,0},{24,8},{1,17},{9,25},{17,1},{25,9},{2,18},{10... | collective-permute-start | bytes 2064392 | tf_op jit(solution)/shard_map/ppermute | solution.py:718
  227.8 35.5 %collective-permute-start.28 = (bf16[2,256,768]{2,1,0:T(8,128)(2,1)}, bf16[2,256,768]{2,1,0:T(8,128)(2,1)}, u32[]{:S(2)}, u32[]{:S(2)}) collective-permute-start(bf16[2,256,768]{2,1,0:T(8,128)(2,1)} %fusion.12), channel_id=1, source_target_pairs={{0,4},{1,5},{2,6},{3,7},{4,0},{5,1},{6,2},{7,3},{8,12},{9,13},{10,... | collective-permute-start | bytes 2359304 | tf_op jit(solution)/shard_map/ppermute | solution.py:718
  229.7 33.5 %collective-permute-start.29 = (bf16[2,256,768]{2,1,0:T(8,128)(2,1)}, bf16[2,256,768]{2,1,0:T(8,128)(2,1)}, u32[]{:S(2)}, u32[]{:S(2)}) collective-permute-start(bf16[2,256,768]{2,1,0:T(8,128)(2,1)} %slice_bitcast_fusion), channel_id=1, source_target_pairs={{0,2},{1,3},{2,0},{3,1},{4,6},{5,7},{6,4},{7,5},{8,10},{9,11},{10,... | collective-permute-start | bytes 2359304 | tf_op jit(solution)/shard_map/ppermute | solution.py:718
  242.0 15.1 %collective-permute-start.38 = (bf16[2,2,112,768]{3,2,1,0:T(8,128)(2,1)}, bf16[2,2,112,768]{3,2,1,0:T(8,128)(2,1)}, u32[]{:S(2)}, u32[]{:S(2)}) collective-permute-start(bf16[2,2,112,768]{3,2,1,0:T(8,128)(2,1)} %pad_maximum_fusion.4.refs_1_), channel_id=1, source_target_pairs={{0,8},{8,0},{16,24},{24,16},{1,9},{9,1},{17,25},{25,17},{2,10},{10... | collective-permute-start | bytes 2064392 | tf_op jit(solution)/shard_map/ppermute | solution.py:718
  243.4 13.7 %collective-permute-start.39 = (bf16[2,2,112,768]{3,2,1,0:T(8,128)(2,1)S(1)}, bf16[2,2,112,768]{3,2,1,0:T(8,128)(2,1)}, u32[]{:S(2)}, u32[]{:S(2)}) collective-permute-start(bf16[2,2,112,768]{3,2,1,0:T(8,128)(2,1)S(1)} %pad_maximum_fusion.3.refs_0_), channel_id=1, source_target_pairs={{0,1},{1,0},{2,3},{3,2},{4,5},{5,4},{6,7},{7,6},{8,9},{9,8},{10,11... | collective-permute-start | bytes 2064392 | tf_op jit(solution)/shard_map/ppermute | solution.py:718
  243.5 13.6 %collective-permute-start.40 = (bf16[2,2,112,768]{3,2,1,0:T(8,128)(2,1)}, bf16[2,2,112,768]{3,2,1,0:T(8,128)(2,1)}, u32[]{:S(2)}, u32[]{:S(2)}) collective-permute-start(bf16[2,2,112,768]{3,2,1,0:T(8,128)(2,1)} %pad_maximum_fusion.4.refs_1_), channel_id=1, source_target_pairs={{0,1},{1,0},{2,3},{3,2},{4,5},{5,4},{6,7},{7,6},{8,9},{9,8},{10,11... | collective-permute-start | bytes 2064392 | tf_op jit(solution)/shard_map/ppermute | solution.py:718
  (54 other events, 499.5 us)

commit v5 on v4

--- a/solution.py
+++ b/solution.py
@@ -19,7 +19,7 @@
 COST = 0.02
 ATTEND_PAIRS = 9
 BACK_PAIRS = 3
-TAIL = "QMNNMQNQMQMmQnQ"
+TAIL = "QMNNMQNQMMmQNQnQ"
 
 NN = (((1,), (0,)), ((), ()))
 NT = (((1,), (1,)), ((), ()))
@@ -738,6 +738,7 @@
 
     def send(self, exchanges):
         if not isinstance(exchanges[0], tuple):
+            self.token = exchanges[-1:]
             return exchanges
         sent = self.hold([array for array, _, _ in exchanges])
         self.token = sent
@@ -789,14 +790,18 @@
     yield from spread_pieces(add(own, got).astype(BF16))
 
 
-def spread_pieces(total):
+def spread_pieces(total, twins_last=False):
     (near,) = yield [(total, "blk", 2)]
     pair_a, pair_b = jnp.stack([total[0], near[0]]), jnp.stack([total[1], near[1]])
     got_a, got_b = yield [(pair_a, "dp", 1), (pair_b, "dp", 2)]
     two = [jnp.stack([pair_a, got_a]), jnp.stack([pair_b, got_b])]
-    *far, twin_a, twin_b = yield [(two[0], "dp", 2), (two[1], "dp", 1)] + [(o, "blk", 1) for o in two]
-    far_twins = yield [(o, "blk", 1) for o in far]
-    yield two + far + [twin_a, twin_b] + far_twins
+    far = yield [(two[0], "dp", 2), (two[1], "dp", 1)] + [(o, "blk", 1) for o in two if not twins_last]
+    if twins_last:
+        twins = yield [(o, "blk", 1) for o in two + far]
+        yield two + far + twins
+    else:
+        far_twins = yield [(o, "blk", 1) for o in far[:2]]
+        yield two + far + far_twins
 
 
 def placed(k, outer, meta, rows):
@@ -1009,7 +1014,7 @@
             yield from sum_halves(own[0], sums.astype(BF16), n_blk)
 
         order.advance(mlp)
-        chains["M"] = order.start(spread_pieces(mlp.held[0]))
+        chains["M"] = order.start(spread_pieces(mlp.held[0], True))
         chains["Q"] = order.start(of_rest())
     ng_part, sums = order.done(join(meta, order.hold(grads), x_all, ngm, w_cut))
 

time: 280 us -> 274 us (0.979)
  waiting for transfers between devices: 90.9 us -> 87.4 us
    ppermute x45, waiting for transfers between devices: 90.9 us -> 87.4 us  [swap(): return lax.ppermute(x, axis, [(i, i ^ mask) for i in range(size)])]
  transfers between devices with their start and end apart: 45 -> 45, of which waited for: 20 -> 20; matrix products, arithmetic and copies ran while one was open for 6% -> 6% of each run, Pallas kernels for 32% -> 33%
where the time goes in v5:
time: 274 us
  Pallas kernels  124 us (45%)
  waiting for transfers between devices  87.4 us (32%)
  starting transfers between devices  36.7 us (13%)
  local copies, waits for them, and re-layouts  14.3 us (5%)
  other arithmetic  10.4 us (4%)
    pallas_call x10, Pallas kernels, call(): pl.pallas_call(kernel, out_shape=out_shapes, grid_spec=pltpu.PrefetchScal...  124 us
    ppermute x45, waiting for transfers between devices, swap(): return lax.ppermute(x, axis, [(i, i ^ mask) for i in range(size)])  87.4 us
    ppermute x45, starting transfers between devices, swap(): return lax.ppermute(x, axis, [(i, i ^ mask) for i in range(size)])  36.7 us
  transfers between devices with their start and end apart: 45, of which 20 were waited for; matrix products, arithmetic and copies ran while one was open for 6% of the time, Pallas kernels for 33%

profile of v5, /device:TPU:0, one launch (start us, length us, event | category | flops | bytes accessed | tf_op | source)
XLA Modules:
  0.0 273.7 jit_solution(8312511095443491501)
XLA Ops:
  2.2 3.1 %collective-permute-start.1 = (bf16[256,768]{1,0:T(8,128)(2,1)S(1)}, bf16[256,768]{1,0:T(8,128)(2,1)S(1)}, u32[]{:S(2)}, u32[]{:S(2)}) collective-permute-start(bf16[256,768]{1,0:T(8,128)(2,1)S(1)} %get-tuple-element.182.refs_0_), channel_id=1, source_target_pairs={{0,2},{1,3},{2,0},{3,1},{4,6},{5,7},{6,4},{7,5},{8,10},{9,11},{10,... | collective-permute-start | bytes 1179656 | tf_op jit(solution)/shard_map/ppermute | solution.py:718
  5.2 2.6 collective-permute-start
  8.7 4.0 %cut.1.refs_6_.refs_5_ = bf16[576,768]{1,0:T(8,128)(2,1)} custom-call(s32[9]{0:T(128)} %concatenate.12.meta_ref, bf16[768,2304]{1,0:T(8,128)(2,1)} %refs_2_.1, bf16[768,2304]{1,0:T(8,128)(2,1)} %refs_2_.1, bf16[768,2304]{1,0:T(8,128)(2,1)} %refs_2_.1), custom_call_target="tpu_custom_call" | custom-call | bytes 53084 | tf_op jit(solution)/shard_map/cut/pallas_call | solution.py:59
  12.7 9.0 %collective-permute-done.1.refs_1_ = bf16[256,768]{1,0:T(8,128)(2,1)S(1)} collective-permute-done((bf16[256,768]{1,0:T(8,128)(2,1)S(1)}, bf16[256,768]{1,0:T(8,128)(2,1)S(1)}, u32[]{:S(2)}, u32[]{:S(2)}) %collective-permute-start.1) | collective-permute-done | bytes 393248 | tf_op jit(solution)/shard_map/ppermute | solution.py:718
  21.8 4.3 %collective-permute-done.refs_0_ = bf16[256,768]{1,0:T(8,128)(2,1)S(1)} collective-permute-done((bf16[256,768]{1,0:T(8,128)(2,1)S(1)}, bf16[256,768]{1,0:T(8,128)(2,1)S(1)}, u32[]{:S(2)}, u32[]{:S(2)}) %collective-permute-start) | collective-permute-done | bytes 393248 | tf_op jit(solution)/shard_map/ppermute | solution.py:718
  26.2 3.0 %collective-permute-start.7 = (bf16[256,768]{1,0:T(8,128)(2,1)S(1)}, bf16[256,768]{1,0:T(8,128)(2,1)S(1)}, u32[]{:S(2)}, u32[]{:S(2)}) collective-permute-start(bf16[256,768]{1,0:T(8,128)(2,1)S(1)} %get-tuple-element.180), channel_id=1, source_target_pairs={{0,4},{1,5},{2,6},{3,7},{4,0},{5,1},{6,2},{7,3},{8,12},{9,13},{10,... | collective-permute-start | bytes 1179656 | tf_op jit(solution)/shard_map/ppermute | solution.py:718
  31.1 6.1 %project.2 = (bf16[8,256,768]{2,1,0:T(8,128)(2,1)}, bf16[8,256,768]{2,1,0:T(8,128)(2,1)}, bf16[8,192,256]{2,1,0:T(8,128)(2,1)}, bf16[8,192,256]{2,1,0:T(8,128)(2...) custom-call(s32[9]{0:T(128)} %concatenate.12.meta_ref, ...), custom_call_target="tpu_custom_call" | custom-call | flops 18119392 | bytes 157286 | tf_op jit(solution)/shard_map/project/pallas_call | solution.py:59
  37.2 6.8 %collective-permute-done.3.refs_1_ = bf16[256,768]{1,0:T(8,128)(2,1)S(1)} collective-permute-done((bf16[256,768]{1,0:T(8,128)(2,1)S(1)}, bf16[256,768]{1,0:T(8,128)(2,1)S(1)}, u32[]{:S(2)}, u32[]{:S(2)}) %collective-permute-start.3) | collective-permute-done | bytes 393248 | tf_op jit(solution)/shard_map/ppermute | solution.py:718
  44.6 2.9 %collective-permute-done.7.refs_4_ = bf16[256,768]{1,0:T(8,128)(2,1)S(1)} collective-permute-done((bf16[256,768]{1,0:T(8,128)(2,1)S(1)}, bf16[256,768]{1,0:T(8,128)(2,1)S(1)}, u32[]{:S(2)}, u32[]{:S(2)}) %collective-permute-start.7) | collective-permute-done | bytes 393248 | tf_op jit(solution)/shard_map/ppermute | solution.py:718
  48.3 6.1 %project.3 = (bf16[8,256,768]{2,1,0:T(8,128)(2,1)}, bf16[8,256,768]{2,1,0:T(8,128)(2,1)}, bf16[8,192,256]{2,1,0:T(8,128)(2,1)}, bf16[8,192,256]{2,1,0:T(8,128)(2...) custom-call(s32[9]{0:T(128)} %concatenate.12.meta_ref, ...), custom_call_target="tpu_custom_call", output_to_operand_aliasing={{0}: (8, {}), {1}: (9, {}), {2}: (10, {}), {3}: (11, {}), {... | custom-call | flops 18119392 | bytes 157286 | tf_op jit(solution)/shard_map/project/pallas_call | solution.py:59
  54.4 1.8 collective-permute-done.8.refs_1_
  56.2 8.1 %collective-permute-done.11.refs_5_ = bf16[256,768]{1,0:T(8,128)(2,1)S(1)} collective-permute-done((bf16[256,768]{1,0:T(8,128)(2,1)S(1)}, bf16[256,768]{1,0:T(8,128)(2,1)S(1)}, u32[]{:S(2)}, u32[]{:S(2)}) %collective-permute-start.11) | collective-permute-done | bytes 393248 | tf_op jit(solution)/shard_map/ppermute | solution.py:718
  64.4 1.7 collective-permute-done.13.refs_7_
  66.9 24.6 %feed.1 = (bf16[8,256,768]{2,1,0:T(8,128)(2,1)}, bf16[8,256,768]{2,1,0:T(8,128)(2,1)}, bf16[8,256,768]{2,1,0:T(8,128)(2,1)}, bf16[2,2,96,768]{3,2,1,0:T(8,128)(2...) custom-call(s32[9]{0:T(128)} %concatenate.12.meta_ref, ...), custom_call_target="tpu_custom_call" | custom-call | flops 289910304 | bytes 346030 | tf_op jit(solution)/shard_map/feed/pallas_call | solution.py:59
  94.5 14.4 %attend.1 = (bf16[8,192,256]{2,1,0:T(8,128)(2,1)}, f32[8,8,256]{2,1,0:T(8,128)}) custom-call(s32[9]{0:T(128)} %concatenate.12.meta_ref, bf16[8,192,256]{2,1,0:T(8,128)(2,1)} %get-tuple-element.249.refs_0_, bf16[8,3,256,64]{3,2,1,0:T(8,128)(2,1)} %get-tuple-element.231.refs_1_.refs_4_, bf16[8,192,256]{2,1,0:T(8,128)(2,1)} %get-tuple-element.232.refs_2_), custom_call_target="tpu_custom_call" | custom-call | flops 72155448 | bytes 125829 | tf_op jit(solution)/shard_map/attend/pallas_call | solution.py:59
  111.3 8.0 %mix.1 = (bf16[8,256,768]{2,1,0:T(8,128)(2,1)}, bf16[8,192,256]{2,1,0:T(8,128)(2,1)}, f32[8,8,256]{2,1,0:T(8,128)}, f32[192,768]{1,0:T(8,128)}) custom-call(s32[9]{0:T(128)} %concatenate.12.meta_ref, bf16[8,192,256]{2,1,0:T(8,128)(2,1)} %get-tuple-element.241.refs_0_, bf16[8,256,768]{2,1,0:T(8,128)(2,1)} %get-tuple-element.242.refs_1_, ...), custom_call_target="tpu_custom_call" | custom-call | flops 36238784 | bytes 314572 | tf_op jit(solution)/shard_map/mix/pallas_call | solution.py:59
  119.9 2.0 slice_bitcast_fusion.7
  122.0 31.2 %attend_back.1 = (bf16[1,192,768]{2,1,0:T(8,128)(2,1)}, bf16[1,192,768]{2,1,0:T(8,128)(2,1)}, bf16[1,192,768]{2,1,0:T(8,128)(2,1)}, bf16[1,192,768]{2,1,0:T(8,12...) custom-call(s32[9]{0:T(128)} %concatenate.12.meta_ref, ...), custom_call_target="tpu_custom_call" | custom-call | flops 180388624 | bytes 125829 | tf_op jit(solution)/shard_map/attend_back/pallas_call | solution.py:59
  153.4 2.4 collective-permute-start.19
  159.2 8.8 %join.1 = (bf16[8,256,768]{2,1,0:T(8,128)(2,1)}, f32[16,768]{1,0:T(8,128)}) custom-call(s32[9]{0:T(128)} %concatenate.12.meta_ref, bf16[8,192,256]{2,1,0:T(8,128)(2,1)} %get-tuple-element.268.refs_0_, bf16[8,192,256]{2,1,0:T(8,128)(2,1)} %get-tuple-element.269.refs_1_, bf16[8,192,256]{2,1,0:T(8,128)(2,1)} %get-tuple-element.270.refs_2_, ...), custom_call_target="tpu_custom_call" | custom-call | flops 36238784 | bytes 314572 | tf_op jit(solution)/shard_map/join/pallas_call | solution.py:59
  168.0 2.1 slice_bitcast_fusion.6
  175.7 1.6 collective-permute-done.23
  178.7 9.3 %collective-permute-done.26 = bf16[2,2,96,768]{3,2,1,0:T(8,128)(2,1)S(1)} collective-permute-done((bf16[2,2,96,768]{3,2,1,0:T(8,128)(2,1)S(1)}, bf16[2,2,96,768]{3,2,1,0:T(8,128)(2,1)S(1)}, u32[]{:S(2)}, u32[]{:S(2)}) %collective-permute-start.26) | collective-permute-done | bytes 589856 | tf_op jit(solution)/shard_map/ppermute | solution.py:718
  195.6 10.1 %collective-permute-done.24 = bf16[2,256,768]{2,1,0:T(8,128)(2,1)S(1)} collective-permute-done((bf16[2,256,768]{2,1,0:T(8,128)(2,1)S(1)}, bf16[2,256,768]{2,1,0:T(8,128)(2,1)S(1)}, u32[]{:S(2)}, u32[]{:S(2)}) %collective-permute-start.24) | collective-permute-done | bytes 786464 | tf_op jit(solution)/shard_map/ppermute | solution.py:718
  206.7 5.5 %collective-permute-done.30 = bf16[2,112,768]{2,1,0:T(8,128)(2,1)S(1)} collective-permute-done((bf16[2,112,768]{2,1,0:T(8,128)(2,1)S(1)}, bf16[2,112,768]{2,1,0:T(8,128)(2,1)S(1)}, u32[]{:S(2)}, u32[]{:S(2)}) %collective-permute-start.30) | collective-permute-done | bytes 344096 | tf_op jit(solution)/shard_map/ppermute | solution.py:718
  214.1 3.5 %collective-permute-done.33.refs_2_ = bf16[2,2,2,96,768]{4,3,2,1,0:T(8,128)(2,1)} collective-permute-done((bf16[2,2,2,96,768]{4,3,2,1,0:T(8,128)(2,1)S(1)}, bf16[2,2,2,96,768]{4,3,2,1,0:T(8,128)(2,1)}, u32[]{:S(2)}, u32[]{:S(2)}) %collective-permute-start.33) | collective-permute-done | bytes 1179680 | tf_op jit(solution)/shard_map/ppermute | solution.py:718
  220.3 2.0 collective-permute-start.28
  227.3 11.3 %fill.1 = (f32[768,3072]{1,0:T(8,128)}, f32[3072,768]{1,0:T(8,128)}) custom-call(s32[9]{0:T(128)} %concatenate.12.meta_ref, bf16[2,2,2,96,768]{4,3,2,1,0:T(8,128)(2,1)} %copy-done.1, bf16[2,2,2,96,768]{4,3,2,1,0:T(8,128)(2,1)} %pad_maximum_fusion.2.refs_1_, bf16[2,2,2,96,768]{4,3,2,1,0:T(8,128)(2,1)} %collective-permute-done.33.refs_2_, ...), custom_call_target="tpu_custom_call" | custom-call | bytes 566231 | tf_op jit(solution)/shard_map/fill/pallas_call | solution.py:59
  242.1 15.8 %collective-permute-done.28 = bf16[2,256,768]{2,1,0:T(8,128)(2,1)S(1)} collective-permute-done((bf16[2,256,768]{2,1,0:T(8,128)(2,1)}, bf16[2,256,768]{2,1,0:T(8,128)(2,1)S(1)}, u32[]{:S(2)}, u32[]{:S(2)}) %collective-permute-start.28) | collective-permute-done | bytes 786464 | tf_op jit(solution)/shard_map/ppermute | solution.py:718
  257.9 1.6 collective-permute-done.29
  261.1 2.1 fusion.9
  264.6 9.1 %tail.1 = (f32[768,2304]{1,0:T(8,128)}, f32[768,768]{1,0:T(8,128)}, f32[768]{0:T(1024)}, f32[768]{0:T(1024)}) custom-call(s32[9]{0:T(128)} %concatenate.12.meta_ref, bf16[2,2,112,768]{3,2,1,0:T(8,128)(2,1)} %copy-done.3, bf16[2,2,112,768]{3,2,1,0:T(8,128)(2,1)} %copy-done.4, bf16[2,2,112,768]{3,2,1,0:T(8,128)(2,1)} %copy-done.9, ...), custom_call_target="tpu_custom_call" | custom-call | bytes 283115 | tf_op jit(solution)/shard_map/tail/pallas_call | solution.py:59
  (200 shorter events, 47.5 us)
Async XLA Ops:
  2.2 19.6 %collective-permute-start.1 = (bf16[256,768]{1,0:T(8,128)(2,1)S(1)}, bf16[256,768]{1,0:T(8,128)(2,1)S(1)}, u32[]{:S(2)}, u32[]{:S(2)}) collective-permute-start(bf16[256,768]{1,0:T(8,128)(2,1)S(1)} %get-tuple-element.182.refs_0_), channel_id=1, source_target_pairs={{0,2},{1,3},{2,0},{3,1},{4,6},{5,7},{6,4},{7,5},{8,10},{9,11},{10,... | collective-permute-start | bytes 1179656 | tf_op jit(solution)/shard_map/ppermute | solution.py:718
  5.2 16.5 %collective-permute-start.2 = (bf16[256,768]{1,0:T(8,128)(2,1)S(1)}, bf16[256,768]{1,0:T(8,128)(2,1)S(1)}, u32[]{:S(2)}, u32[]{:S(2)}) collective-permute-start(bf16[256,768]{1,0:T(8,128)(2,1)S(1)} %get-tuple-element.182.refs_0_), channel_id=1, source_target_pairs={{0,1},{1,0},{2,3},{3,2},{4,5},{5,4},{6,7},{7,6},{8,9},{9,8},{10,11... | collective-permute-start | bytes 1179656 | tf_op jit(solution)/shard_map/ppermute | solution.py:718
  5.2 20.9 %collective-permute-start = (bf16[256,768]{1,0:T(8,128)(2,1)S(1)}, bf16[256,768]{1,0:T(8,128)(2,1)S(1)}, u32[]{:S(2)}, u32[]{:S(2)}) collective-permute-start(bf16[256,768]{1,0:T(8,128)(2,1)S(1)} %get-tuple-element.378), channel_id=1, source_target_pairs={{0,4},{1,5},{2,6},{3,7},{4,0},{5,1},{6,2},{7,3},{8,12},{9,13},{10,... | collective-permute-start | bytes 1179656 | tf_op jit(solution)/shard_map/ppermute | solution.py:718
  26.1 17.9 %collective-permute-start.3 = (bf16[256,768]{1,0:T(8,128)(2,1)S(1)}, bf16[256,768]{1,0:T(8,128)(2,1)S(1)}, u32[]{:S(2)}, u32[]{:S(2)}) collective-permute-start(bf16[256,768]{1,0:T(8,128)(2,1)S(1)} %collective-permute-done.refs_0_), channel_id=1, source_target_pairs={{0,2},{1,3},{2,0},{3,1},{4,6},{5,7},{6,4},{7,5},{8,10},{9,11},{10,... | collective-permute-start | bytes 1179656 | tf_op jit(solution)/shard_map/ppermute | solution.py:718
  26.1 17.9 %collective-permute-start.4 = (bf16[256,768]{1,0:T(8,128)(2,1)S(1)}, bf16[256,768]{1,0:T(8,128)(2,1)S(1)}, u32[]{:S(2)}, u32[]{:S(2)}) collective-permute-start(bf16[256,768]{1,0:T(8,128)(2,1)S(1)} %collective-permute-done.refs_0_), channel_id=1, source_target_pairs={{0,1},{1,0},{2,3},{3,2},{4,5},{5,4},{6,7},{7,6},{8,9},{9,8},{10,11... | collective-permute-start | bytes 1179656 | tf_op jit(solution)/shard_map/ppermute | solution.py:718
  26.2 21.3 %collective-permute-start.7 = (bf16[256,768]{1,0:T(8,128)(2,1)S(1)}, bf16[256,768]{1,0:T(8,128)(2,1)S(1)}, u32[]{:S(2)}, u32[]{:S(2)}) collective-permute-start(bf16[256,768]{1,0:T(8,128)(2,1)S(1)} %get-tuple-element.180), channel_id=1, source_target_pairs={{0,4},{1,5},{2,6},{3,7},{4,0},{5,1},{6,2},{7,3},{8,12},{9,13},{10,... | collective-permute-start | bytes 1179656 | tf_op jit(solution)/shard_map/ppermute | solution.py:718
  44.1 12.1 %collective-permute-start.8 = (bf16[256,768]{1,0:T(8,128)(2,1)S(1)}, bf16[256,768]{1,0:T(8,128)(2,1)S(1)}, u32[]{:S(2)}, u32[]{:S(2)}) collective-permute-start(bf16[256,768]{1,0:T(8,128)(2,1)S(1)} %get-tuple-element.216.refs_0_), channel_id=1, source_target_pairs={{0,2},{1,3},{2,0},{3,1},{4,6},{5,7},{6,4},{7,5},{8,10},{9,11},{10,... | collective-permute-start | bytes 1179656 | tf_op jit(solution)/shard_map/ppermute | solution.py:718
  44.2 12.0 %collective-permute-start.9 = (bf16[256,768]{1,0:T(8,128)(2,1)S(1)}, bf16[256,768]{1,0:T(8,128)(2,1)S(1)}, u32[]{:S(2)}, u32[]{:S(2)}) collective-permute-start(bf16[256,768]{1,0:T(8,128)(2,1)S(1)} %get-tuple-element.216.refs_0_), channel_id=1, source_target_pairs={{0,1},{1,0},{2,3},{3,2},{4,5},{5,4},{6,7},{7,6},{8,9},{9,8},{10,11... | collective-permute-start | bytes 1179656 | tf_op jit(solution)/shard_map/ppermute | solution.py:718
  47.5 16.8 %collective-permute-start.11 = (bf16[256,768]{1,0:T(8,128)(2,1)S(1)}, bf16[256,768]{1,0:T(8,128)(2,1)S(1)}, u32[]{:S(2)}, u32[]{:S(2)}) collective-permute-start(bf16[256,768]{1,0:T(8,128)(2,1)S(1)} %collective-permute-done.7.refs_4_), channel_id=1, source_target_pairs={{0,2},{1,3},{2,0},{3,1},{4,6},{5,7},{6,4},{7,5},{8,10},{9,11},{10,... | collective-permute-start | bytes 1179656 | tf_op jit(solution)/shard_map/ppermute | solution.py:718
  47.5 16.8 %collective-permute-start.12 = (bf16[256,768]{1,0:T(8,128)(2,1)S(1)}, bf16[256,768]{1,0:T(8,128)(2,1)S(1)}, u32[]{:S(2)}, u32[]{:S(2)}) collective-permute-start(bf16[256,768]{1,0:T(8,128)(2,1)S(1)} %collective-permute-done.7.refs_4_), channel_id=1, source_target_pairs={{0,1},{1,0},{2,3},{3,2},{4,5},{5,4},{6,7},{7,6},{8,9},{9,8},{10,11... | collective-permute-start | bytes 1179656 | tf_op jit(solution)/shard_map/ppermute | solution.py:718
  91.5 17.5 %collective-permute-start.14 = (bf16[2,2,96,768]{3,2,1,0:T(8,128)(2,1)}, bf16[2,2,96,768]{3,2,1,0:T(8,128)(2,1)S(1)}, u32[]{:S(2)}, u32[]{:S(2)}) collective-permute-start(bf16[2,2,96,768]{3,2,1,0:T(8,128)(2,1)} %get-tuple-element.228), channel_id=1, source_target_pairs={{0,8},{8,0},{16,24},{24,16},{1,9},{9,1},{17,25},{25,17},{2,10},{10... | collective-permute-start | bytes 1769480 | tf_op jit(solution)/shard_map/ppermute | solution.py:718
  93.0 15.9 %collective-permute-start.15 = (bf16[2,2,96,768]{3,2,1,0:T(8,128)(2,1)}, bf16[2,2,96,768]{3,2,1,0:T(8,128)(2,1)S(1)}, u32[]{:S(2)}, u32[]{:S(2)}) collective-permute-start(bf16[2,2,96,768]{3,2,1,0:T(8,128)(2,1)} %get-tuple-element.229), channel_id=1, source_target_pairs={{0,16},{8,24},{16,0},{24,8},{1,17},{9,25},{17,1},{25,9},{2,18},{10... | collective-permute-start | bytes 1769480 | tf_op jit(solution)/shard_map/ppermute | solution.py:718
  110.1 9.2 %collective-permute-start.16 = (bf16[2,96,768]{2,1,0:T(8,128)(2,1)S(1)}, bf16[2,96,768]{2,1,0:T(8,128)(2,1)S(1)}, u32[]{:S(2)}, u32[]{:S(2)}) collective-permute-start(bf16[2,96,768]{2,1,0:T(8,128)(2,1)S(1)} %slice_bitcast_fusion.11), channel_id=1, source_target_pairs={{0,16},{8,24},{16,0},{24,8},{1,17},{9,25},{17,1},{25,9},{2,18},{10... | collective-permute-start | bytes 884744 | tf_op jit(solution)/shard_map/ppermute | solution.py:718
  119.6 33.6 %collective-permute-start.18 = (bf16[2,2,96,768]{3,2,1,0:T(8,128)(2,1)S(1)}, bf16[2,2,96,768]{3,2,1,0:T(8,128)(2,1)S(1)}, u32[]{:S(2)}, u32[]{:S(2)}) collective-permute-start(bf16[2,2,96,768]{3,2,1,0:T(8,128)(2,1)S(1)} %pad_maximum_fusion.5), channel_id=1, source_target_pairs={{0,4},{1,5},{2,6},{3,7},{4,0},{5,1},{6,2},{7,3},{8,12},{9,13},{10,... | collective-permute-start | bytes 1769480 | tf_op jit(solution)/shard_map/ppermute | solution.py:718
  153.4 18.0 %collective-permute-start.19 = (bf16[2,2,96,768]{3,2,1,0:T(8,128)(2,1)S(1)}, bf16[2,2,96,768]{3,2,1,0:T(8,128)(2,1)S(1)}, u32[]{:S(2)}, u32[]{:S(2)}) collective-permute-start(bf16[2,2,96,768]{3,2,1,0:T(8,128)(2,1)S(1)} %add_convert_fusion), channel_id=1, source_target_pairs={{0,2},{1,3},{2,0},{3,1},{4,6},{5,7},{6,4},{7,5},{8,10},{9,11},{10,... | collective-permute-start | bytes 1769480 | tf_op jit(solution)/shard_map/ppermute | solution.py:718
  155.7 14.9 %collective-permute-start.20 = (bf16[1,192,768]{2,1,0:T(8,128)(2,1)S(1)}, bf16[1,192,768]{2,1,0:T(8,128)(2,1)S(1)}, u32[]{:S(2)}, u32[]{:S(2)}) collective-permute-start(bf16[1,192,768]{2,1,0:T(8,128)(2,1)S(1)} %copy-done.38), channel_id=1, source_target_pairs={{0,8},{8,0},{16,24},{24,16},{1,9},{9,1},{17,25},{25,17},{2,10},{10... | collective-permute-start | bytes 884744 | tf_op jit(solution)/shard_map/ppermute | solution.py:718
  157.2 13.4 %collective-permute-start.21 = (bf16[1,192,768]{2,1,0:T(8,128)(2,1)S(1)}, bf16[1,192,768]{2,1,0:T(8,128)(2,1)S(1)}, u32[]{:S(2)}, u32[]{:S(2)}) collective-permute-start(bf16[1,192,768]{2,1,0:T(8,128)(2,1)S(1)} %copy-done.37), channel_id=1, source_target_pairs={{0,16},{8,24},{16,0},{24,8},{1,17},{9,25},{17,1},{25,9},{2,18},{10... | collective-permute-start | bytes 884744 | tf_op jit(solution)/shard_map/ppermute | solution.py:718
  158.8 11.9 %collective-permute-start.22 = (bf16[1,192,768]{2,1,0:T(8,128)(2,1)S(1)}, bf16[1,192,768]{2,1,0:T(8,128)(2,1)S(1)}, u32[]{:S(2)}, u32[]{:S(2)}) collective-permute-start(bf16[1,192,768]{2,1,0:T(8,128)(2,1)S(1)} %copy-done.36), channel_id=1, source_target_pairs={{0,24},{8,16},{16,8},{24,0},{1,25},{9,17},{17,9},{25,1},{2,26},{10... | collective-permute-start | bytes 884744 | tf_op jit(solution)/shard_map/ppermute | solution.py:718
  171.7 21.0 %collective-permute-start.25 = (bf16[2,112,768]{2,1,0:T(8,128)(2,1)S(1)}, bf16[2,112,768]{2,1,0:T(8,128)(2,1)S(1)}, u32[]{:S(2)}, u32[]{:S(2)}) collective-permute-start(bf16[2,112,768]{2,1,0:T(8,128)(2,1)S(1)} %pad_maximum_fusion.8), channel_id=1, source_target_pairs={{0,4},{1,5},{2,6},{3,7},{4,0},{5,1},{6,2},{7,3},{8,12},{9,13},{10,... | collective-permute-start | bytes 1032200 | tf_op jit(solution)/shard_map/ppermute | solution.py:718
  172.7 15.4 %collective-permute-start.26 = (bf16[2,2,96,768]{3,2,1,0:T(8,128)(2,1)S(1)}, bf16[2,2,96,768]{3,2,1,0:T(8,128)(2,1)S(1)}, u32[]{:S(2)}, u32[]{:S(2)}) collective-permute-start(bf16[2,2,96,768]{3,2,1,0:T(8,128)(2,1)S(1)} %get-tuple-element.279), channel_id=1, source_target_pairs={{0,8},{8,0},{16,24},{24,16},{1,9},{9,1},{17,25},{25,17},{2,10},{10... | collective-permute-start | bytes 1769480 | tf_op jit(solution)/shard_map/ppermute | solution.py:718
  174.2 15.1 %collective-permute-start.27 = (bf16[2,2,96,768]{3,2,1,0:T(8,128)(2,1)S(1)}, bf16[2,2,96,768]{3,2,1,0:T(8,128)(2,1)S(1)}, u32[]{:S(2)}, u32[]{:S(2)}) collective-permute-start(bf16[2,2,96,768]{3,2,1,0:T(8,128)(2,1)S(1)} %get-tuple-element.280), channel_id=1, source_target_pairs={{0,16},{8,24},{16,0},{24,8},{1,17},{9,25},{17,1},{25,9},{2,18},{10... | collective-permute-start | bytes 1769480 | tf_op jit(solution)/shard_map/ppermute | solution.py:718
  178.0 27.6 %collective-permute-start.24 = (bf16[2,256,768]{2,1,0:T(8,128)(2,1)S(1)}, bf16[2,256,768]{2,1,0:T(8,128)(2,1)S(1)}, u32[]{:S(2)}, u32[]{:S(2)}) collective-permute-start(bf16[2,256,768]{2,1,0:T(8,128)(2,1)S(1)} %slice_bitcast_fusion.1), channel_id=1, source_target_pairs={{0,2},{1,3},{2,0},{3,1},{4,6},{5,7},{6,4},{7,5},{8,10},{9,11},{10,... | collective-permute-start | bytes 2359304 | tf_op jit(solution)/shard_map/ppermute | solution.py:718
  190.6 27.0 %collective-permute-start.33 = (bf16[2,2,2,96,768]{4,3,2,1,0:T(8,128)(2,1)S(1)}, bf16[2,2,2,96,768]{4,3,2,1,0:T(8,128)(2,1)}, u32[]{:S(2)}, u32[]{:S(2)}) collective-permute-start(bf16[2,2,2,96,768]{4,3,2,1,0:T(8,128)(2,1)S(1)} %pad_maximum_fusion.1.refs_0_), channel_id=1, source_target_pairs={{0,16},{8,24},{16,0},{24,8},{1,17},{9,25},{17,1},{25,9},{2,18},{10... | collective-permute-start | bytes 3538952 | tf_op jit(solution)/shard_map/ppermute | solution.py:718
  192.1 26.9 %collective-permute-start.34 = (bf16[2,2,2,96,768]{4,3,2,1,0:T(8,128)(2,1)}, bf16[2,2,2,96,768]{4,3,2,1,0:T(8,128)(2,1)}, u32[]{:S(2)}, u32[]{:S(2)}) collective-permute-start(bf16[2,2,2,96,768]{4,3,2,1,0:T(8,128)(2,1)} %pad_maximum_fusion.2.refs_1_), channel_id=1, source_target_pairs={{0,8},{8,0},{16,24},{24,16},{1,9},{9,1},{17,25},{25,17},{2,10},{10... | collective-permute-start | bytes 3538952 | tf_op jit(solution)/shard_map/ppermute | solution.py:718
  192.8 19.4 %collective-permute-start.30 = (bf16[2,112,768]{2,1,0:T(8,128)(2,1)S(1)}, bf16[2,112,768]{2,1,0:T(8,128)(2,1)S(1)}, u32[]{:S(2)}, u32[]{:S(2)}) collective-permute-start(bf16[2,112,768]{2,1,0:T(8,128)(2,1)S(1)} %add_convert_fusion.3), channel_id=1, source_target_pairs={{0,2},{1,3},{2,0},{3,1},{4,6},{5,7},{6,4},{7,5},{8,10},{9,11},{10,... | collective-permute-start | bytes 1032200 | tf_op jit(solution)/shard_map/ppermute | solution.py:718
  220.3 37.6 %collective-permute-start.28 = (bf16[2,256,768]{2,1,0:T(8,128)(2,1)}, bf16[2,256,768]{2,1,0:T(8,128)(2,1)S(1)}, u32[]{:S(2)}, u32[]{:S(2)}) collective-permute-start(bf16[2,256,768]{2,1,0:T(8,128)(2,1)} %fusion.12), channel_id=1, source_target_pairs={{0,4},{1,5},{2,6},{3,7},{4,0},{5,1},{6,2},{7,3},{8,12},{9,13},{10,... | collective-permute-start | bytes 2359304 | tf_op jit(solution)/shard_map/ppermute | solution.py:718
  223.7 35.8 %collective-permute-start.29 = (bf16[2,256,768]{2,1,0:T(8,128)(2,1)}, bf16[2,256,768]{2,1,0:T(8,128)(2,1)S(1)}, u32[]{:S(2)}, u32[]{:S(2)}) collective-permute-start(bf16[2,256,768]{2,1,0:T(8,128)(2,1)} %slice_bitcast_fusion), channel_id=1, source_target_pairs={{0,2},{1,3},{2,0},{3,1},{4,6},{5,7},{6,4},{7,5},{8,10},{9,11},{10,... | collective-permute-start | bytes 2359304 | tf_op jit(solution)/shard_map/ppermute | solution.py:718
  225.1 13.6 %collective-permute-start.31 = (bf16[2,112,768]{2,1,0:T(8,128)(2,1)}, bf16[2,112,768]{2,1,0:T(8,128)(2,1)S(1)}, u32[]{:S(2)}, u32[]{:S(2)}) collective-permute-start(bf16[2,112,768]{2,1,0:T(8,128)(2,1)} %get-tuple-element.294), channel_id=1, source_target_pairs={{0,8},{8,0},{16,24},{24,16},{1,9},{9,1},{17,25},{25,17},{2,10},{10... | collective-permute-start | bytes 1032200 | tf_op jit(solution)/shard_map/ppermute | solution.py:718
  225.7 13.0 %collective-permute-start.32 = (bf16[2,112,768]{2,1,0:T(8,128)(2,1)}, bf16[2,112,768]{2,1,0:T(8,128)(2,1)S(1)}, u32[]{:S(2)}, u32[]{:S(2)}) collective-permute-start(bf16[2,112,768]{2,1,0:T(8,128)(2,1)} %get-tuple-element.295), channel_id=1, source_target_pairs={{0,16},{8,24},{16,0},{24,8},{1,17},{9,25},{17,1},{25,9},{2,18},{10... | collective-permute-start | bytes 1032200 | tf_op jit(solution)/shard_map/ppermute | solution.py:718
  239.7 20.8 %collective-permute-start.39 = (bf16[2,2,112,768]{3,2,1,0:T(8,128)(2,1)S(1)}, bf16[2,2,112,768]{3,2,1,0:T(8,128)(2,1)S(1)}, u32[]{:S(2)}, u32[]{:S(2)}) collective-permute-start(bf16[2,2,112,768]{3,2,1,0:T(8,128)(2,1)S(1)} %pad_maximum_fusion.3.refs_0_), channel_id=1, source_target_pairs={{0,16},{8,24},{16,0},{24,8},{1,17},{9,25},{17,1},{25,9},{2,18},{10... | collective-permute-start | bytes 2064392 | tf_op jit(solution)/shard_map/ppermute | solution.py:718
  240.6 19.8 %collective-permute-start.40 = (bf16[2,2,112,768]{3,2,1,0:T(8,128)(2,1)S(1)}, bf16[2,2,112,768]{3,2,1,0:T(8,128)(2,1)S(1)}, u32[]{:S(2)}, u32[]{:S(2)}) collective-permute-start(bf16[2,2,112,768]{3,2,1,0:T(8,128)(2,1)S(1)} %pad_maximum_fusion.4.refs_1_), channel_id=1, source_target_pairs={{0,8},{8,0},{16,24},{24,16},{1,9},{9,1},{17,25},{25,17},{2,10},{10... | collective-permute-start | bytes 2064392 | tf_op jit(solution)/shard_map/ppermute | solution.py:718
  242.1 18.4 %collective-permute-start.41 = (bf16[2,2,112,768]{3,2,1,0:T(8,128)(2,1)S(1)}, bf16[2,2,112,768]{3,2,1,0:T(8,128)(2,1)S(1)}, u32[]{:S(2)}, u32[]{:S(2)}) collective-permute-start(bf16[2,2,112,768]{3,2,1,0:T(8,128)(2,1)S(1)} %pad_maximum_fusion.3.refs_0_), channel_id=1, source_target_pairs={{0,1},{1,0},{2,3},{3,2},{4,5},{5,4},{6,7},{7,6},{8,9},{9,8},{10,11... | collective-permute-start | bytes 2064392 | tf_op jit(solution)/shard_map/ppermute | solution.py:718
  (52 other events, 392.5 us)

commit v6 on v5

--- a/solution.py
+++ b/solution.py
@@ -853,52 +853,54 @@
     srcs, (gq_ref, go_ref, gain_ref, bias_ref, hold_ref, part_ref) = refs[:8], refs[8:]
     rows = srcs[0].shape[2] - 16
     i = pl.program_id(0)
-
-    @pl.when(i == 0)
+    apart = (jnp.bitwise_xor(meta[Y_POS], lax.rem(i, 2)), jnp.bitwise_xor(meta[X_POS], i // 2))
+    for k, src in enumerate(srcs):
+        b, far, core = k % 2, (k // 2) % 2, k // 4
+
+        @pl.when(apart[b] == far)
+        def _():
+            for rt1 in range(2):
+                shard = jnp.bitwise_xor(meta[QUARTER], rt1 * 2 + core)
+                at = pl.multiple_of(shard * wide + b * rows, 16)
+                hold_ref[pl.ds(at, rows), :] = src[0, rt1, 16:].astype(F32)
+                if b == 0:
+                    part_ref[shard * 4 + i] = src[0, rt1, 0:16].astype(F32)
+
+    @pl.when(i < 3)
     def _():
-        for k, src in enumerate(srcs):
-            for outer in range(2):
-                row = placed(k % 4, outer, meta, rows)
-                for rt1 in range(2):
-                    shard = jnp.bitwise_xor(meta[QUARTER], rt1 * 2 + k // 4)
-                    at = pl.multiple_of(shard * 4 * wide + row, 16)
-                    hold_ref[pl.ds(at, rows), :] = src[outer, rt1, 16:].astype(F32)
-                    if k % 2 == 0:
-                        part_ref[shard * 4 + row // (2 * rows)] = src[outer, rt1, 0:16].astype(F32)
+        gq_ref[...] = hold_ref[...].T
+
+    @pl.when(i == 3)
+    def _():
+        go_ref[...] = hold_ref[...]
         total = part_ref[0]
         for n in range(1, 4 * TENSOR):
             total = total + part_ref[n]
         gain_ref[...] = total[0]
         bias_ref[...] = total[1]
 
-    def block(part):
-        return jnp.concatenate([hold_ref[(4 * s + part) * wide : (4 * s + part + 1) * wide, :] for s in range(TENSOR)], axis=0)
-
-    for third in range(3):
-
-        @pl.when(i == third)
-        def _():
-            gq_ref[...] = block(third).T
-
-    @pl.when(i == 3)
-    def _():
-        go_ref[...] = block(3)
-
 
 def tail(meta, arrays, width, wide):
     outs = [sds((width, 3 * TENSOR * wide), F32), sds((TENSOR * wide, width), F32), sds((width,), F32), sds((width,), F32)]
+    def source(k):
+        def at(i, s):
+            outer = jnp.bitwise_xor(s[Y_POS], lax.rem(i, 2)) if k % 2 else jnp.bitwise_xor(s[X_POS], i // 2)
+            return outer, 0, 0, 0
+
+        return pl.BlockSpec((1,) + arrays[k].shape[1:], at)
+
     return call(
         partial(tail_kernel, wide),
         "tail",
         meta,
         (4,),
         list(arrays),
-        [once(a.shape) for a in arrays],
+        [source(k) for k in range(8)],
         outs,
         [pl.BlockSpec((width, TENSOR * wide), lambda i, s: (0, jnp.minimum(i, 2)))] + [whole(o.shape) for o in outs[1:]],
         0,
         6 * 4 * width * width,
-        scratch=[pltpu.VMEM((TENSOR * 4 * wide, width), F32), pltpu.VMEM((4 * TENSOR, 16, width), F32)],
+        scratch=[pltpu.VMEM((TENSOR * wide, width), F32), pltpu.VMEM((4 * TENSOR, 16, width), F32)],
     )
 
 

time: 274 us -> 276 us (level)
  no operation moved by 1% of the time
where the time goes in v6:
time: 276 us; the launch traced here: 275 us
  Pallas kernels  125 us (45%)
  waiting for transfers between devices  87.4 us (32%)
  starting transfers between devices  36.7 us (13%)
  local copies, waits for them, and re-layouts  14.3 us (5%)
  other arithmetic  10.4 us (4%)
    pallas_call x10, Pallas kernels, call(): pl.pallas_call(kernel, out_shape=out_shapes, grid_spec=pltpu.PrefetchScal...  125 us
    ppermute x45, waiting for transfers between devices, swap(): return lax.ppermute(x, axis, [(i, i ^ mask) for i in range(size)])  87.4 us
    ppermute x45, starting transfers between devices, swap(): return lax.ppermute(x, axis, [(i, i ^ mask) for i in range(size)])  36.7 us
  transfers between devices with their start and end apart: 45, of which 20 were waited for; matrix products, arithmetic and copies ran while one was open for 6% of the time, Pallas kernels for 33%

profile of v6, /device:TPU:0, one launch (start us, length us, event | category | flops | bytes accessed | tf_op | source)
XLA Modules:
  0.0 275.1 jit_solution(4141411063563151879)
XLA Ops:
  2.2 3.1 %collective-permute-start.1 = (bf16[256,768]{1,0:T(8,128)(2,1)S(1)}, bf16[256,768]{1,0:T(8,128)(2,1)S(1)}, u32[]{:S(2)}, u32[]{:S(2)}) collective-permute-start(bf16[256,768]{1,0:T(8,128)(2,1)S(1)} %get-tuple-element.182.refs_0_), channel_id=1, source_target_pairs={{0,2},{1,3},{2,0},{3,1},{4,6},{5,7},{6,4},{7,5},{8,10},{9,11},{10,... | collective-permute-start | bytes 1179656 | tf_op jit(solution)/shard_map/ppermute | solution.py:718
  5.2 2.6 collective-permute-start
  8.7 4.0 %cut.1.refs_6_.refs_5_ = bf16[576,768]{1,0:T(8,128)(2,1)} custom-call(s32[9]{0:T(128)} %concatenate.12.meta_ref, bf16[768,2304]{1,0:T(8,128)(2,1)} %refs_2_.1, bf16[768,2304]{1,0:T(8,128)(2,1)} %refs_2_.1, bf16[768,2304]{1,0:T(8,128)(2,1)} %refs_2_.1), custom_call_target="tpu_custom_call" | custom-call | bytes 53084 | tf_op jit(solution)/shard_map/cut/pallas_call | solution.py:59
  12.7 9.0 %collective-permute-done.1.refs_1_ = bf16[256,768]{1,0:T(8,128)(2,1)S(1)} collective-permute-done((bf16[256,768]{1,0:T(8,128)(2,1)S(1)}, bf16[256,768]{1,0:T(8,128)(2,1)S(1)}, u32[]{:S(2)}, u32[]{:S(2)}) %collective-permute-start.1) | collective-permute-done | bytes 393248 | tf_op jit(solution)/shard_map/ppermute | solution.py:718
  21.8 4.3 %collective-permute-done.refs_0_ = bf16[256,768]{1,0:T(8,128)(2,1)S(1)} collective-permute-done((bf16[256,768]{1,0:T(8,128)(2,1)S(1)}, bf16[256,768]{1,0:T(8,128)(2,1)S(1)}, u32[]{:S(2)}, u32[]{:S(2)}) %collective-permute-start) | collective-permute-done | bytes 393248 | tf_op jit(solution)/shard_map/ppermute | solution.py:718
  26.2 3.0 %collective-permute-start.7 = (bf16[256,768]{1,0:T(8,128)(2,1)S(1)}, bf16[256,768]{1,0:T(8,128)(2,1)S(1)}, u32[]{:S(2)}, u32[]{:S(2)}) collective-permute-start(bf16[256,768]{1,0:T(8,128)(2,1)S(1)} %get-tuple-element.180), channel_id=1, source_target_pairs={{0,4},{1,5},{2,6},{3,7},{4,0},{5,1},{6,2},{7,3},{8,12},{9,13},{10,... | collective-permute-start | bytes 1179656 | tf_op jit(solution)/shard_map/ppermute | solution.py:718
  31.1 6.1 %project.2 = (bf16[8,256,768]{2,1,0:T(8,128)(2,1)}, bf16[8,256,768]{2,1,0:T(8,128)(2,1)}, bf16[8,192,256]{2,1,0:T(8,128)(2,1)}, bf16[8,192,256]{2,1,0:T(8,128)(2...) custom-call(s32[9]{0:T(128)} %concatenate.12.meta_ref, ...), custom_call_target="tpu_custom_call" | custom-call | flops 18119392 | bytes 157286 | tf_op jit(solution)/shard_map/project/pallas_call | solution.py:59
  37.2 6.8 %collective-permute-done.3.refs_1_ = bf16[256,768]{1,0:T(8,128)(2,1)S(1)} collective-permute-done((bf16[256,768]{1,0:T(8,128)(2,1)S(1)}, bf16[256,768]{1,0:T(8,128)(2,1)S(1)}, u32[]{:S(2)}, u32[]{:S(2)}) %collective-permute-start.3) | collective-permute-done | bytes 393248 | tf_op jit(solution)/shard_map/ppermute | solution.py:718
  44.6 2.9 %collective-permute-done.7.refs_4_ = bf16[256,768]{1,0:T(8,128)(2,1)S(1)} collective-permute-done((bf16[256,768]{1,0:T(8,128)(2,1)S(1)}, bf16[256,768]{1,0:T(8,128)(2,1)S(1)}, u32[]{:S(2)}, u32[]{:S(2)}) %collective-permute-start.7) | collective-permute-done | bytes 393248 | tf_op jit(solution)/shard_map/ppermute | solution.py:718
  48.3 6.1 %project.3 = (bf16[8,256,768]{2,1,0:T(8,128)(2,1)}, bf16[8,256,768]{2,1,0:T(8,128)(2,1)}, bf16[8,192,256]{2,1,0:T(8,128)(2,1)}, bf16[8,192,256]{2,1,0:T(8,128)(2...) custom-call(s32[9]{0:T(128)} %concatenate.12.meta_ref, ...), custom_call_target="tpu_custom_call", output_to_operand_aliasing={{0}: (8, {}), {1}: (9, {}), {2}: (10, {}), {3}: (11, {}), {... | custom-call | flops 18119392 | bytes 157286 | tf_op jit(solution)/shard_map/project/pallas_call | solution.py:59
  54.4 1.8 collective-permute-done.8.refs_1_
  56.2 8.1 %collective-permute-done.11.refs_5_ = bf16[256,768]{1,0:T(8,128)(2,1)S(1)} collective-permute-done((bf16[256,768]{1,0:T(8,128)(2,1)S(1)}, bf16[256,768]{1,0:T(8,128)(2,1)S(1)}, u32[]{:S(2)}, u32[]{:S(2)}) %collective-permute-start.11) | collective-permute-done | bytes 393248 | tf_op jit(solution)/shard_map/ppermute | solution.py:718
  64.4 1.7 collective-permute-done.13.refs_7_
  66.9 24.6 %feed.1 = (bf16[8,256,768]{2,1,0:T(8,128)(2,1)}, bf16[8,256,768]{2,1,0:T(8,128)(2,1)}, bf16[8,256,768]{2,1,0:T(8,128)(2,1)}, bf16[2,2,96,768]{3,2,1,0:T(8,128)(2...) custom-call(s32[9]{0:T(128)} %concatenate.12.meta_ref, ...), custom_call_target="tpu_custom_call" | custom-call | flops 289910304 | bytes 346030 | tf_op jit(solution)/shard_map/feed/pallas_call | solution.py:59
  94.5 14.4 %attend.1 = (bf16[8,192,256]{2,1,0:T(8,128)(2,1)}, f32[8,8,256]{2,1,0:T(8,128)}) custom-call(s32[9]{0:T(128)} %concatenate.12.meta_ref, bf16[8,192,256]{2,1,0:T(8,128)(2,1)} %get-tuple-element.249.refs_0_, bf16[8,3,256,64]{3,2,1,0:T(8,128)(2,1)} %get-tuple-element.231.refs_1_.refs_4_, bf16[8,192,256]{2,1,0:T(8,128)(2,1)} %get-tuple-element.232.refs_2_), custom_call_target="tpu_custom_call" | custom-call | flops 72155448 | bytes 125829 | tf_op jit(solution)/shard_map/attend/pallas_call | solution.py:59
  111.3 8.0 %mix.1 = (bf16[8,256,768]{2,1,0:T(8,128)(2,1)}, bf16[8,192,256]{2,1,0:T(8,128)(2,1)}, f32[8,8,256]{2,1,0:T(8,128)}, f32[192,768]{1,0:T(8,128)}) custom-call(s32[9]{0:T(128)} %concatenate.12.meta_ref, bf16[8,192,256]{2,1,0:T(8,128)(2,1)} %get-tuple-element.241.refs_0_, bf16[8,256,768]{2,1,0:T(8,128)(2,1)} %get-tuple-element.242.refs_1_, ...), custom_call_target="tpu_custom_call" | custom-call | flops 36238784 | bytes 314572 | tf_op jit(solution)/shard_map/mix/pallas_call | solution.py:59
  119.9 2.0 slice_bitcast_fusion.7
  122.0 31.2 %attend_back.1 = (bf16[1,192,768]{2,1,0:T(8,128)(2,1)}, bf16[1,192,768]{2,1,0:T(8,128)(2,1)}, bf16[1,192,768]{2,1,0:T(8,128)(2,1)}, bf16[1,192,768]{2,1,0:T(8,12...) custom-call(s32[9]{0:T(128)} %concatenate.12.meta_ref, ...), custom_call_target="tpu_custom_call" | custom-call | flops 180388624 | bytes 125829 | tf_op jit(solution)/shard_map/attend_back/pallas_call | solution.py:59
  153.4 2.4 collective-permute-start.19
  159.2 8.8 %join.1 = (bf16[8,256,768]{2,1,0:T(8,128)(2,1)}, f32[16,768]{1,0:T(8,128)}) custom-call(s32[9]{0:T(128)} %concatenate.12.meta_ref, bf16[8,192,256]{2,1,0:T(8,128)(2,1)} %get-tuple-element.268.refs_0_, bf16[8,192,256]{2,1,0:T(8,128)(2,1)} %get-tuple-element.269.refs_1_, bf16[8,192,256]{2,1,0:T(8,128)(2,1)} %get-tuple-element.270.refs_2_, ...), custom_call_target="tpu_custom_call" | custom-call | flops 36238784 | bytes 314572 | tf_op jit(solution)/shard_map/join/pallas_call | solution.py:59
  168.0 2.1 slice_bitcast_fusion.6
  175.7 1.6 collective-permute-done.23
  178.7 9.3 %collective-permute-done.26 = bf16[2,2,96,768]{3,2,1,0:T(8,128)(2,1)S(1)} collective-permute-done((bf16[2,2,96,768]{3,2,1,0:T(8,128)(2,1)S(1)}, bf16[2,2,96,768]{3,2,1,0:T(8,128)(2,1)S(1)}, u32[]{:S(2)}, u32[]{:S(2)}) %collective-permute-start.26) | collective-permute-done | bytes 589856 | tf_op jit(solution)/shard_map/ppermute | solution.py:718
  195.6 10.1 %collective-permute-done.24 = bf16[2,256,768]{2,1,0:T(8,128)(2,1)S(1)} collective-permute-done((bf16[2,256,768]{2,1,0:T(8,128)(2,1)S(1)}, bf16[2,256,768]{2,1,0:T(8,128)(2,1)S(1)}, u32[]{:S(2)}, u32[]{:S(2)}) %collective-permute-start.24) | collective-permute-done | bytes 786464 | tf_op jit(solution)/shard_map/ppermute | solution.py:718
  206.7 5.5 %collective-permute-done.30 = bf16[2,112,768]{2,1,0:T(8,128)(2,1)S(1)} collective-permute-done((bf16[2,112,768]{2,1,0:T(8,128)(2,1)S(1)}, bf16[2,112,768]{2,1,0:T(8,128)(2,1)S(1)}, u32[]{:S(2)}, u32[]{:S(2)}) %collective-permute-start.30) | collective-permute-done | bytes 344096 | tf_op jit(solution)/shard_map/ppermute | solution.py:718
  214.1 3.5 %collective-permute-done.33.refs_2_ = bf16[2,2,2,96,768]{4,3,2,1,0:T(8,128)(2,1)} collective-permute-done((bf16[2,2,2,96,768]{4,3,2,1,0:T(8,128)(2,1)S(1)}, bf16[2,2,2,96,768]{4,3,2,1,0:T(8,128)(2,1)}, u32[]{:S(2)}, u32[]{:S(2)}) %collective-permute-start.33) | collective-permute-done | bytes 1179680 | tf_op jit(solution)/shard_map/ppermute | solution.py:718
  220.3 2.0 collective-permute-start.28
  227.3 11.3 %fill.1 = (f32[768,3072]{1,0:T(8,128)}, f32[3072,768]{1,0:T(8,128)}) custom-call(s32[9]{0:T(128)} %concatenate.12.meta_ref, bf16[2,2,2,96,768]{4,3,2,1,0:T(8,128)(2,1)} %copy-done.1, bf16[2,2,2,96,768]{4,3,2,1,0:T(8,128)(2,1)} %pad_maximum_fusion.2.refs_1_, bf16[2,2,2,96,768]{4,3,2,1,0:T(8,128)(2,1)} %collective-permute-done.33.refs_2_, ...), custom_call_target="tpu_custom_call" | custom-call | bytes 566231 | tf_op jit(solution)/shard_map/fill/pallas_call | solution.py:59
  242.1 15.8 %collective-permute-done.28 = bf16[2,256,768]{2,1,0:T(8,128)(2,1)S(1)} collective-permute-done((bf16[2,256,768]{2,1,0:T(8,128)(2,1)}, bf16[2,256,768]{2,1,0:T(8,128)(2,1)S(1)}, u32[]{:S(2)}, u32[]{:S(2)}) %collective-permute-start.28) | collective-permute-done | bytes 786464 | tf_op jit(solution)/shard_map/ppermute | solution.py:718
  257.9 1.6 collective-permute-done.29
  261.1 2.1 fusion.9
  264.6 10.3 %tail.1 = (f32[768,2304]{1,0:T(8,128)}, f32[768,768]{1,0:T(8,128)}, f32[768]{0:T(1024)}, f32[768]{0:T(1024)}) custom-call(s32[9]{0:T(128)} %concatenate.12.meta_ref, bf16[2,2,112,768]{3,2,1,0:T(8,128)(2,1)} %copy-done.3, bf16[2,2,112,768]{3,2,1,0:T(8,128)(2,1)} %copy-done.4, bf16[2,2,112,768]{3,2,1,0:T(8,128)(2,1)} %copy-done.9, ...), custom_call_target="tpu_custom_call" | custom-call | bytes 283115 | tf_op jit(solution)/shard_map/tail/pallas_call | solution.py:59
  (200 shorter events, 47.5 us)
Async XLA Ops:
  2.2 19.6 %collective-permute-start.1 = (bf16[256,768]{1,0:T(8,128)(2,1)S(1)}, bf16[256,768]{1,0:T(8,128)(2,1)S(1)}, u32[]{:S(2)}, u32[]{:S(2)}) collective-permute-start(bf16[256,768]{1,0:T(8,128)(2,1)S(1)} %get-tuple-element.182.refs_0_), channel_id=1, source_target_pairs={{0,2},{1,3},{2,0},{3,1},{4,6},{5,7},{6,4},{7,5},{8,10},{9,11},{10,... | collective-permute-start | bytes 1179656 | tf_op jit(solution)/shard_map/ppermute | solution.py:718
  5.2 16.5 %collective-permute-start.2 = (bf16[256,768]{1,0:T(8,128)(2,1)S(1)}, bf16[256,768]{1,0:T(8,128)(2,1)S(1)}, u32[]{:S(2)}, u32[]{:S(2)}) collective-permute-start(bf16[256,768]{1,0:T(8,128)(2,1)S(1)} %get-tuple-element.182.refs_0_), channel_id=1, source_target_pairs={{0,1},{1,0},{2,3},{3,2},{4,5},{5,4},{6,7},{7,6},{8,9},{9,8},{10,11... | collective-permute-start | bytes 1179656 | tf_op jit(solution)/shard_map/ppermute | solution.py:718
  5.2 20.9 %collective-permute-start = (bf16[256,768]{1,0:T(8,128)(2,1)S(1)}, bf16[256,768]{1,0:T(8,128)(2,1)S(1)}, u32[]{:S(2)}, u32[]{:S(2)}) collective-permute-start(bf16[256,768]{1,0:T(8,128)(2,1)S(1)} %get-tuple-element.378), channel_id=1, source_target_pairs={{0,4},{1,5},{2,6},{3,7},{4,0},{5,1},{6,2},{7,3},{8,12},{9,13},{10,... | collective-permute-start | bytes 1179656 | tf_op jit(solution)/shard_map/ppermute | solution.py:718
  26.1 17.9 %collective-permute-start.3 = (bf16[256,768]{1,0:T(8,128)(2,1)S(1)}, bf16[256,768]{1,0:T(8,128)(2,1)S(1)}, u32[]{:S(2)}, u32[]{:S(2)}) collective-permute-start(bf16[256,768]{1,0:T(8,128)(2,1)S(1)} %collective-permute-done.refs_0_), channel_id=1, source_target_pairs={{0,2},{1,3},{2,0},{3,1},{4,6},{5,7},{6,4},{7,5},{8,10},{9,11},{10,... | collective-permute-start | bytes 1179656 | tf_op jit(solution)/shard_map/ppermute | solution.py:718
  26.1 17.9 %collective-permute-start.4 = (bf16[256,768]{1,0:T(8,128)(2,1)S(1)}, bf16[256,768]{1,0:T(8,128)(2,1)S(1)}, u32[]{:S(2)}, u32[]{:S(2)}) collective-permute-start(bf16[256,768]{1,0:T(8,128)(2,1)S(1)} %collective-permute-done.refs_0_), channel_id=1, source_target_pairs={{0,1},{1,0},{2,3},{3,2},{4,5},{5,4},{6,7},{7,6},{8,9},{9,8},{10,11... | collective-permute-start | bytes 1179656 | tf_op jit(solution)/shard_map/ppermute | solution.py:718
  26.2 21.3 %collective-permute-start.7 = (bf16[256,768]{1,0:T(8,128)(2,1)S(1)}, bf16[256,768]{1,0:T(8,128)(2,1)S(1)}, u32[]{:S(2)}, u32[]{:S(2)}) collective-permute-start(bf16[256,768]{1,0:T(8,128)(2,1)S(1)} %get-tuple-element.180), channel_id=1, source_target_pairs={{0,4},{1,5},{2,6},{3,7},{4,0},{5,1},{6,2},{7,3},{8,12},{9,13},{10,... | collective-permute-start | bytes 1179656 | tf_op jit(solution)/shard_map/ppermute | solution.py:718
  44.1 12.1 %collective-permute-start.8 = (bf16[256,768]{1,0:T(8,128)(2,1)S(1)}, bf16[256,768]{1,0:T(8,128)(2,1)S(1)}, u32[]{:S(2)}, u32[]{:S(2)}) collective-permute-start(bf16[256,768]{1,0:T(8,128)(2,1)S(1)} %get-tuple-element.216.refs_0_), channel_id=1, source_target_pairs={{0,2},{1,3},{2,0},{3,1},{4,6},{5,7},{6,4},{7,5},{8,10},{9,11},{10,... | collective-permute-start | bytes 1179656 | tf_op jit(solution)/shard_map/ppermute | solution.py:718
  44.2 12.0 %collective-permute-start.9 = (bf16[256,768]{1,0:T(8,128)(2,1)S(1)}, bf16[256,768]{1,0:T(8,128)(2,1)S(1)}, u32[]{:S(2)}, u32[]{:S(2)}) collective-permute-start(bf16[256,768]{1,0:T(8,128)(2,1)S(1)} %get-tuple-element.216.refs_0_), channel_id=1, source_target_pairs={{0,1},{1,0},{2,3},{3,2},{4,5},{5,4},{6,7},{7,6},{8,9},{9,8},{10,11... | collective-permute-start | bytes 1179656 | tf_op jit(solution)/shard_map/ppermute | solution.py:718
  47.5 16.8 %collective-permute-start.11 = (bf16[256,768]{1,0:T(8,128)(2,1)S(1)}, bf16[256,768]{1,0:T(8,128)(2,1)S(1)}, u32[]{:S(2)}, u32[]{:S(2)}) collective-permute-start(bf16[256,768]{1,0:T(8,128)(2,1)S(1)} %collective-permute-done.7.refs_4_), channel_id=1, source_target_pairs={{0,2},{1,3},{2,0},{3,1},{4,6},{5,7},{6,4},{7,5},{8,10},{9,11},{10,... | collective-permute-start | bytes 1179656 | tf_op jit(solution)/shard_map/ppermute | solution.py:718
  47.5 16.8 %collective-permute-start.12 = (bf16[256,768]{1,0:T(8,128)(2,1)S(1)}, bf16[256,768]{1,0:T(8,128)(2,1)S(1)}, u32[]{:S(2)}, u32[]{:S(2)}) collective-permute-start(bf16[256,768]{1,0:T(8,128)(2,1)S(1)} %collective-permute-done.7.refs_4_), channel_id=1, source_target_pairs={{0,1},{1,0},{2,3},{3,2},{4,5},{5,4},{6,7},{7,6},{8,9},{9,8},{10,11... | collective-permute-start | bytes 1179656 | tf_op jit(solution)/shard_map/ppermute | solution.py:718
  91.5 17.5 %collective-permute-start.14 = (bf16[2,2,96,768]{3,2,1,0:T(8,128)(2,1)}, bf16[2,2,96,768]{3,2,1,0:T(8,128)(2,1)S(1)}, u32[]{:S(2)}, u32[]{:S(2)}) collective-permute-start(bf16[2,2,96,768]{3,2,1,0:T(8,128)(2,1)} %get-tuple-element.228), channel_id=1, source_target_pairs={{0,8},{8,0},{16,24},{24,16},{1,9},{9,1},{17,25},{25,17},{2,10},{10... | collective-permute-start | bytes 1769480 | tf_op jit(solution)/shard_map/ppermute | solution.py:718
  93.0 15.9 %collective-permute-start.15 = (bf16[2,2,96,768]{3,2,1,0:T(8,128)(2,1)}, bf16[2,2,96,768]{3,2,1,0:T(8,128)(2,1)S(1)}, u32[]{:S(2)}, u32[]{:S(2)}) collective-permute-start(bf16[2,2,96,768]{3,2,1,0:T(8,128)(2,1)} %get-tuple-element.229), channel_id=1, source_target_pairs={{0,16},{8,24},{16,0},{24,8},{1,17},{9,25},{17,1},{25,9},{2,18},{10... | collective-permute-start | bytes 1769480 | tf_op jit(solution)/shard_map/ppermute | solution.py:718
  110.1 9.2 %collective-permute-start.16 = (bf16[2,96,768]{2,1,0:T(8,128)(2,1)S(1)}, bf16[2,96,768]{2,1,0:T(8,128)(2,1)S(1)}, u32[]{:S(2)}, u32[]{:S(2)}) collective-permute-start(bf16[2,96,768]{2,1,0:T(8,128)(2,1)S(1)} %slice_bitcast_fusion.11), channel_id=1, source_target_pairs={{0,16},{8,24},{16,0},{24,8},{1,17},{9,25},{17,1},{25,9},{2,18},{10... | collective-permute-start | bytes 884744 | tf_op jit(solution)/shard_map/ppermute | solution.py:718
  119.6 33.6 %collective-permute-start.18 = (bf16[2,2,96,768]{3,2,1,0:T(8,128)(2,1)S(1)}, bf16[2,2,96,768]{3,2,1,0:T(8,128)(2,1)S(1)}, u32[]{:S(2)}, u32[]{:S(2)}) collective-permute-start(bf16[2,2,96,768]{3,2,1,0:T(8,128)(2,1)S(1)} %pad_maximum_fusion.5), channel_id=1, source_target_pairs={{0,4},{1,5},{2,6},{3,7},{4,0},{5,1},{6,2},{7,3},{8,12},{9,13},{10,... | collective-permute-start | bytes 1769480 | tf_op jit(solution)/shard_map/ppermute | solution.py:718
  153.4 18.0 %collective-permute-start.19 = (bf16[2,2,96,768]{3,2,1,0:T(8,128)(2,1)S(1)}, bf16[2,2,96,768]{3,2,1,0:T(8,128)(2,1)S(1)}, u32[]{:S(2)}, u32[]{:S(2)}) collective-permute-start(bf16[2,2,96,768]{3,2,1,0:T(8,128)(2,1)S(1)} %add_convert_fusion), channel_id=1, source_target_pairs={{0,2},{1,3},{2,0},{3,1},{4,6},{5,7},{6,4},{7,5},{8,10},{9,11},{10,... | collective-permute-start | bytes 1769480 | tf_op jit(solution)/shard_map/ppermute | solution.py:718
  155.7 14.9 %collective-permute-start.20 = (bf16[1,192,768]{2,1,0:T(8,128)(2,1)S(1)}, bf16[1,192,768]{2,1,0:T(8,128)(2,1)S(1)}, u32[]{:S(2)}, u32[]{:S(2)}) collective-permute-start(bf16[1,192,768]{2,1,0:T(8,128)(2,1)S(1)} %copy-done.38), channel_id=1, source_target_pairs={{0,8},{8,0},{16,24},{24,16},{1,9},{9,1},{17,25},{25,17},{2,10},{10... | collective-permute-start | bytes 884744 | tf_op jit(solution)/shard_map/ppermute | solution.py:718
  157.2 13.4 %collective-permute-start.21 = (bf16[1,192,768]{2,1,0:T(8,128)(2,1)S(1)}, bf16[1,192,768]{2,1,0:T(8,128)(2,1)S(1)}, u32[]{:S(2)}, u32[]{:S(2)}) collective-permute-start(bf16[1,192,768]{2,1,0:T(8,128)(2,1)S(1)} %copy-done.37), channel_id=1, source_target_pairs={{0,16},{8,24},{16,0},{24,8},{1,17},{9,25},{17,1},{25,9},{2,18},{10... | collective-permute-start | bytes 884744 | tf_op jit(solution)/shard_map/ppermute | solution.py:718
  158.8 11.9 %collective-permute-start.22 = (bf16[1,192,768]{2,1,0:T(8,128)(2,1)S(1)}, bf16[1,192,768]{2,1,0:T(8,128)(2,1)S(1)}, u32[]{:S(2)}, u32[]{:S(2)}) collective-permute-start(bf16[1,192,768]{2,1,0:T(8,128)(2,1)S(1)} %copy-done.36), channel_id=1, source_target_pairs={{0,24},{8,16},{16,8},{24,0},{1,25},{9,17},{17,9},{25,1},{2,26},{10... | collective-permute-start | bytes 884744 | tf_op jit(solution)/shard_map/ppermute | solution.py:718
  171.7 21.0 %collective-permute-start.25 = (bf16[2,112,768]{2,1,0:T(8,128)(2,1)S(1)}, bf16[2,112,768]{2,1,0:T(8,128)(2,1)S(1)}, u32[]{:S(2)}, u32[]{:S(2)}) collective-permute-start(bf16[2,112,768]{2,1,0:T(8,128)(2,1)S(1)} %pad_maximum_fusion.8), channel_id=1, source_target_pairs={{0,4},{1,5},{2,6},{3,7},{4,0},{5,1},{6,2},{7,3},{8,12},{9,13},{10,... | collective-permute-start | bytes 1032200 | tf_op jit(solution)/shard_map/ppermute | solution.py:718
  172.7 15.4 %collective-permute-start.26 = (bf16[2,2,96,768]{3,2,1,0:T(8,128)(2,1)S(1)}, bf16[2,2,96,768]{3,2,1,0:T(8,128)(2,1)S(1)}, u32[]{:S(2)}, u32[]{:S(2)}) collective-permute-start(bf16[2,2,96,768]{3,2,1,0:T(8,128)(2,1)S(1)} %get-tuple-element.279), channel_id=1, source_target_pairs={{0,8},{8,0},{16,24},{24,16},{1,9},{9,1},{17,25},{25,17},{2,10},{10... | collective-permute-start | bytes 1769480 | tf_op jit(solution)/shard_map/ppermute | solution.py:718
  174.2 15.1 %collective-permute-start.27 = (bf16[2,2,96,768]{3,2,1,0:T(8,128)(2,1)S(1)}, bf16[2,2,96,768]{3,2,1,0:T(8,128)(2,1)S(1)}, u32[]{:S(2)}, u32[]{:S(2)}) collective-permute-start(bf16[2,2,96,768]{3,2,1,0:T(8,128)(2,1)S(1)} %get-tuple-element.280), channel_id=1, source_target_pairs={{0,16},{8,24},{16,0},{24,8},{1,17},{9,25},{17,1},{25,9},{2,18},{10... | collective-permute-start | bytes 1769480 | tf_op jit(solution)/shard_map/ppermute | solution.py:718
  178.0 27.6 %collective-permute-start.24 = (bf16[2,256,768]{2,1,0:T(8,128)(2,1)S(1)}, bf16[2,256,768]{2,1,0:T(8,128)(2,1)S(1)}, u32[]{:S(2)}, u32[]{:S(2)}) collective-permute-start(bf16[2,256,768]{2,1,0:T(8,128)(2,1)S(1)} %slice_bitcast_fusion.1), channel_id=1, source_target_pairs={{0,2},{1,3},{2,0},{3,1},{4,6},{5,7},{6,4},{7,5},{8,10},{9,11},{10,... | collective-permute-start | bytes 2359304 | tf_op jit(solution)/shard_map/ppermute | solution.py:718
  190.6 27.0 %collective-permute-start.33 = (bf16[2,2,2,96,768]{4,3,2,1,0:T(8,128)(2,1)S(1)}, bf16[2,2,2,96,768]{4,3,2,1,0:T(8,128)(2,1)}, u32[]{:S(2)}, u32[]{:S(2)}) collective-permute-start(bf16[2,2,2,96,768]{4,3,2,1,0:T(8,128)(2,1)S(1)} %pad_maximum_fusion.1.refs_0_), channel_id=1, source_target_pairs={{0,16},{8,24},{16,0},{24,8},{1,17},{9,25},{17,1},{25,9},{2,18},{10... | collective-permute-start | bytes 3538952 | tf_op jit(solution)/shard_map/ppermute | solution.py:718
  192.1 26.9 %collective-permute-start.34 = (bf16[2,2,2,96,768]{4,3,2,1,0:T(8,128)(2,1)}, bf16[2,2,2,96,768]{4,3,2,1,0:T(8,128)(2,1)}, u32[]{:S(2)}, u32[]{:S(2)}) collective-permute-start(bf16[2,2,2,96,768]{4,3,2,1,0:T(8,128)(2,1)} %pad_maximum_fusion.2.refs_1_), channel_id=1, source_target_pairs={{0,8},{8,0},{16,24},{24,16},{1,9},{9,1},{17,25},{25,17},{2,10},{10... | collective-permute-start | bytes 3538952 | tf_op jit(solution)/shard_map/ppermute | solution.py:718
  192.8 19.4 %collective-permute-start.30 = (bf16[2,112,768]{2,1,0:T(8,128)(2,1)S(1)}, bf16[2,112,768]{2,1,0:T(8,128)(2,1)S(1)}, u32[]{:S(2)}, u32[]{:S(2)}) collective-permute-start(bf16[2,112,768]{2,1,0:T(8,128)(2,1)S(1)} %add_convert_fusion.3), channel_id=1, source_target_pairs={{0,2},{1,3},{2,0},{3,1},{4,6},{5,7},{6,4},{7,5},{8,10},{9,11},{10,... | collective-permute-start | bytes 1032200 | tf_op jit(solution)/shard_map/ppermute | solution.py:718
  220.3 37.6 %collective-permute-start.28 = (bf16[2,256,768]{2,1,0:T(8,128)(2,1)}, bf16[2,256,768]{2,1,0:T(8,128)(2,1)S(1)}, u32[]{:S(2)}, u32[]{:S(2)}) collective-permute-start(bf16[2,256,768]{2,1,0:T(8,128)(2,1)} %fusion.12), channel_id=1, source_target_pairs={{0,4},{1,5},{2,6},{3,7},{4,0},{5,1},{6,2},{7,3},{8,12},{9,13},{10,... | collective-permute-start | bytes 2359304 | tf_op jit(solution)/shard_map/ppermute | solution.py:718
  223.7 35.8 %collective-permute-start.29 = (bf16[2,256,768]{2,1,0:T(8,128)(2,1)}, bf16[2,256,768]{2,1,0:T(8,128)(2,1)S(1)}, u32[]{:S(2)}, u32[]{:S(2)}) collective-permute-start(bf16[2,256,768]{2,1,0:T(8,128)(2,1)} %slice_bitcast_fusion), channel_id=1, source_target_pairs={{0,2},{1,3},{2,0},{3,1},{4,6},{5,7},{6,4},{7,5},{8,10},{9,11},{10,... | collective-permute-start | bytes 2359304 | tf_op jit(solution)/shard_map/ppermute | solution.py:718
  225.1 13.6 %collective-permute-start.31 = (bf16[2,112,768]{2,1,0:T(8,128)(2,1)}, bf16[2,112,768]{2,1,0:T(8,128)(2,1)S(1)}, u32[]{:S(2)}, u32[]{:S(2)}) collective-permute-start(bf16[2,112,768]{2,1,0:T(8,128)(2,1)} %get-tuple-element.294), channel_id=1, source_target_pairs={{0,8},{8,0},{16,24},{24,16},{1,9},{9,1},{17,25},{25,17},{2,10},{10... | collective-permute-start | bytes 1032200 | tf_op jit(solution)/shard_map/ppermute | solution.py:718
  225.7 13.0 %collective-permute-start.32 = (bf16[2,112,768]{2,1,0:T(8,128)(2,1)}, bf16[2,112,768]{2,1,0:T(8,128)(2,1)S(1)}, u32[]{:S(2)}, u32[]{:S(2)}) collective-permute-start(bf16[2,112,768]{2,1,0:T(8,128)(2,1)} %get-tuple-element.295), channel_id=1, source_target_pairs={{0,16},{8,24},{16,0},{24,8},{1,17},{9,25},{17,1},{25,9},{2,18},{10... | collective-permute-start | bytes 1032200 | tf_op jit(solution)/shard_map/ppermute | solution.py:718
  239.7 20.8 %collective-permute-start.39 = (bf16[2,2,112,768]{3,2,1,0:T(8,128)(2,1)S(1)}, bf16[2,2,112,768]{3,2,1,0:T(8,128)(2,1)S(1)}, u32[]{:S(2)}, u32[]{:S(2)}) collective-permute-start(bf16[2,2,112,768]{3,2,1,0:T(8,128)(2,1)S(1)} %pad_maximum_fusion.3.refs_0_), channel_id=1, source_target_pairs={{0,16},{8,24},{16,0},{24,8},{1,17},{9,25},{17,1},{25,9},{2,18},{10... | collective-permute-start | bytes 2064392 | tf_op jit(solution)/shard_map/ppermute | solution.py:718
  240.6 19.8 %collective-permute-start.40 = (bf16[2,2,112,768]{3,2,1,0:T(8,128)(2,1)S(1)}, bf16[2,2,112,768]{3,2,1,0:T(8,128)(2,1)S(1)}, u32[]{:S(2)}, u32[]{:S(2)}) collective-permute-start(bf16[2,2,112,768]{3,2,1,0:T(8,128)(2,1)S(1)} %pad_maximum_fusion.4.refs_1_), channel_id=1, source_target_pairs={{0,8},{8,0},{16,24},{24,16},{1,9},{9,1},{17,25},{25,17},{2,10},{10... | collective-permute-start | bytes 2064392 | tf_op jit(solution)/shard_map/ppermute | solution.py:718
  242.1 18.4 %collective-permute-start.41 = (bf16[2,2,112,768]{3,2,1,0:T(8,128)(2,1)S(1)}, bf16[2,2,112,768]{3,2,1,0:T(8,128)(2,1)S(1)}, u32[]{:S(2)}, u32[]{:S(2)}) collective-permute-start(bf16[2,2,112,768]{3,2,1,0:T(8,128)(2,1)S(1)} %pad_maximum_fusion.3.refs_0_), channel_id=1, source_target_pairs={{0,1},{1,0},{2,3},{3,2},{4,5},{5,4},{6,7},{7,6},{8,9},{9,8},{10,11... | collective-permute-start | bytes 2064392 | tf_op jit(solution)/shard_map/ppermute | solution.py:718
  (52 other events, 392.5 us)
